TPU v7x, 32 devices: a whole 2x2x4 slice. The times are simulated.
32 devices in a mesh: patch: 8 (over z, y), band: 4 (over x, core).
Axes of the slice: x: 2, y: 2, z: 4, core: 2. Of those that a mesh axis runs over, the one named last changes fastest.
Arguments:
- blocks: bfloat16 [4, 256, 256, 256], P('band', 'patch'), may hold values from -6 to 6
- dest_patch: int32 [4, 256], P('band', 'patch'), may hold values from 0 to 7, as said below
- dest_slot: int32 [4, 256], P('band', 'patch'), may hold values from 0 to 3
- weights: bfloat16 [4, 256], P('band', 'patch'), may hold values from 0.25 to 4
- psf_taps: bfloat16 [4, 256, 2, 41], P('band', 'patch'), may hold values from -1 to 1
- det_taps: float32 [4, 25], P('band'), may hold values from -1.25 to 1.25
- noise_var: float32 [4], P('band'), may hold values from 0.5 to 2
Outputs:
- coadd_image: float32 [4, 512, 4096], P('band', None, 'patch')
- chi_square: float32 [512, 4096], P('band', 'patch')
Inputs may be any that keep to these rules, and one draw needn't show every extreme that they name: `dest_patch`: within each band, among the 32 blocks of one index of patch (aligned runs of 32 blocks), at most 4 go to any one patch; in every band some patch receives exactly 4 blocks from every index of patch.
All inputs are finite; a program needn't handle non-finite values.
Results may differ from a plain program's by a relative error of at most 0.0048.
Values may be sent and summed in bfloat16 or wider, within the bound.
No kernel may reach another device: no remote copies, remote signals or barrier semaphores. Data moves between devices by JAX's collectives and lax.ppermute only.
A program may use at most 192 MiB of HBM per device.

v0:
```python
import math

import jax
import jax.numpy as jnp
from jax import lax
from jax.sharding import PartitionSpec as P

TH = 2
TW = 2
DR = 12
CAP = 4
SLOTS = 4


def padded_2(shard, sides, width):
    for axis, dim in sides:
        size, length = (lax.axis_size(axis), shard.shape[dim])
        up = [(i, (i + 1) % size) for i in range(size)]
        down = [(j, i) for i, j in up]
        last = lax.slice_in_dim(shard, length - width, length, axis=dim)
        initial = lax.slice_in_dim(shard, 0, width, axis=dim)
        before = lax.ppermute(last, axis, up)
        after = lax.ppermute(initial, axis, down)
        shard = jnp.concatenate([before, shard, after], axis=dim)
    return shard


def offset_grid(rows, cols, start):
    row_index = lax.broadcasted_iota(jnp.int32, (rows, cols), 0)
    col_index = lax.broadcasted_iota(jnp.int32, (rows, cols), 1)
    return col_index - row_index + start


def tap_onehot(tap_count, number, start):
    offsets = offset_grid(number, number, start)
    return (offsets[None, :, :] == jnp.arange(tap_count, dtype=jnp.int32)[:, None, None]).astype(
        jnp.bfloat16
    )


def banded_float(kernel, rows, cols, start):
    offsets = offset_grid(rows, cols, start)
    table = jnp.zeros((rows, cols), jnp.float32)
    for tap_index in range(kernel.shape[0]):
        table = table + jnp.where(
            offsets == tap_index, kernel[tap_index], jnp.zeros((), jnp.float32)
        )
    return table


def match_blocks(raw_blocks, block_taps):
    number = raw_blocks.shape[0]
    block_edge = raw_blocks.shape[-1]
    tap_count = block_taps.shape[-1]
    groups = math.gcd(number, 8)
    per_group = number // groups
    onehot = tap_onehot(tap_count, block_edge, tap_count // 2)

    def match_group(grouped):
        group_blocks, group_taps = grouped
        matrices = jnp.einsum(
            "nct,tij->ncij", group_taps, onehot, preferred_element_type=jnp.float32
        ).astype(jnp.bfloat16)
        half_pass = jnp.einsum(
            "nij,njk->nik", matrices[:, 0], group_blocks, preferred_element_type=jnp.float32
        ).astype(jnp.bfloat16)
        return jnp.einsum(
            "nij,nkj->nik", half_pass, matrices[:, 1], preferred_element_type=jnp.float32
        ).astype(jnp.bfloat16)

    matched = lax.map(
        match_group,
        (
            raw_blocks.reshape(groups, per_group, block_edge, block_edge),
            block_taps.reshape(groups, per_group, 2, tap_count),
        ),
    )
    return matched.reshape(number, block_edge, block_edge)


def local(blocks, dest_patch, dest_slot, weights, psf_taps, det_taps, noise_var):
    npatch = lax.axis_size("patch")
    local_blocks = blocks[0]
    block_edge = local_blocks.shape[-1]
    tap_count = psf_taps.shape[-1]
    target = dest_patch[0]
    dest_hits = (target[:, None] == jnp.arange(npatch, dtype=jnp.int32)[None, :]).astype(jnp.int32)
    earlier = jnp.cumsum(dest_hits, axis=0) - dest_hits
    slot_rank = jnp.sum(earlier * dest_hits, axis=1)
    position = target * CAP + slot_rank
    total_slots = npatch * CAP
    weight_buffer = (
        jnp.zeros((total_slots,), jnp.bfloat16).at[position].set(weights[0]).reshape(npatch, CAP)
    )
    tile_buffer = (
        jnp.zeros((total_slots,), jnp.int32).at[position].set(dest_slot[0]).reshape(npatch, CAP)
    )
    block_buffer = (
        jnp.zeros((total_slots, block_edge, block_edge), jnp.bfloat16)
        .at[position]
        .set(local_blocks)
    )
    block_buffer = block_buffer.reshape(npatch, CAP, block_edge, block_edge)
    taps_buffer = jnp.zeros((total_slots, 2, tap_count), jnp.bfloat16).at[position].set(psf_taps[0])
    taps_buffer = taps_buffer.reshape(npatch, CAP, 2, tap_count)
    raw_blocks = lax.all_to_all(block_buffer, "patch", split_axis=0, concat_axis=0, tiled=True)
    block_taps = lax.all_to_all(taps_buffer, "patch", split_axis=0, concat_axis=0, tiled=True)
    arrived_weights = lax.all_to_all(
        weight_buffer, "patch", split_axis=0, concat_axis=0, tiled=True
    )
    arrived_tiles = lax.all_to_all(tile_buffer, "patch", split_axis=0, concat_axis=0, tiled=True)
    sources = raw_blocks.shape[0]
    items = raw_blocks.shape[1]
    matched_here = match_blocks(
        raw_blocks.reshape(sources * items, block_edge, block_edge),
        block_taps.reshape(sources * items, 2, tap_count),
    )
    received = matched_here.reshape(sources, items, block_edge, block_edge)
    arrived_blocks = received.reshape(total_slots, block_edge, block_edge)
    tile_picks = (
        arrived_tiles.reshape(1, total_slots) == jnp.arange(SLOTS, dtype=jnp.int32)[:, None]
    )
    selected = jnp.where(
        tile_picks, arrived_weights.reshape(1, total_slots), jnp.zeros((), jnp.bfloat16)
    )
    weighted = lax.dot_general(
        selected, arrived_blocks, (((1,), (0,)), ((), ())), preferred_element_type=jnp.float32
    )
    weight_sum = jnp.sum(selected.astype(jnp.float32), axis=1)
    tile_values = weighted / jnp.maximum(weight_sum, 1.0)[:, None, None]
    tile_rows = []
    for row_index in range(TH):
        tile_rows.append(
            jnp.concatenate(
                [tile_values[row_index * TW + col_index] for col_index in range(TW)], axis=1
            )
        )
    patch_image = jnp.concatenate(tile_rows, axis=0)
    kernel = det_taps[0]
    padded = padded_2(patch_image, (("patch", 1),), DR)
    columns = patch_image.shape[1]
    pixel_rows = patch_image.shape[0]
    col_table = banded_float(kernel, columns, columns + 2 * DR, 0)
    col_pass = lax.dot_general(
        padded, col_table, (((1,), (1,)), ((), ())), precision=lax.Precision.HIGHEST
    )
    row_table = banded_float(kernel, pixel_rows, pixel_rows, DR)
    row_pass = jnp.dot(row_table, col_pass, precision=lax.Precision.HIGHEST)
    band_term = row_pass * row_pass / noise_var[0]
    chi_part = lax.psum_scatter(band_term, "band", scatter_dimension=0, tiled=True)
    return (patch_image[None], chi_part)


def solution(mesh):
    in_specs = (
        P("band", "patch", None, None),
        P("band", "patch"),
        P("band", "patch"),
        P("band", "patch"),
        P("band", "patch", None, None),
        P("band", None),
        P("band"),
    )
    out_specs = (P("band", None, "patch"), P("band", "patch"))
    return jax.shard_map(local, mesh=mesh, in_specs=in_specs, out_specs=out_specs, check_vma=False)
```

profile of v0, /device:TPU:0, one launch (start us, length us, event | category | flops | bytes accessed | tf_op | source)
XLA Modules:
  0.0 270.5 jit_solution(4475779878685457182)
XLA Ops:
  7.2 0.7 fusion.339
  7.9 0.8 select_reduce_fusion
  8.8 0.7 fusion.344
  9.5 0.9 scatter_custom_fusion.1
  10.3 0.7 all_to_all.24
  11.0 7.3 %all-to-all-start.1 = ((bf16[8,1,4]{2,1,0:T(2,128)(2,1)}), bf16[8,1,4]{2,1,0:T(2,128)(2,1)S(1)}, u32[]{:S(2)}, u32[]{:S(2)}) async-start(bf16[8,1,4]{2,1,0:T(2,128)(2,1)} %all_to_all.24), calls=%async_computation.1 | async-start | bytes 8192 | tf_op jit(solution)/shard_map/all_to_all | solution.py:108
  18.3 0.8 scatter_custom_fusion
  19.1 0.7 all_to_all.18
  19.8 2.8 %scatter_fusion = bf16[32,2,41]{2,1,0:T(2,128)(2,1)S(1)} fusion(bf16[32,2,41]{2,1,0:T(2,128)(2,1)S(1)} %broadcast_in_dim.255, s32[32]{0:T(128)S(1)} %fusion.344, bf16[32,2,41]{2,1,0:T(2,128)(2,1)} %bitcast.100), kind=kCustom, calls=%fused_computation.2 | custom fusion | bytes 15872 | tf_op jit(solution)/shard_map/scatter | solution.py:104
  22.7 2.0 all-to-all-done.1
  24.7 4.0 %all-to-all-start = ((s32[8,1,4]{2,1,0:T(1,128)}), s32[8,1,4]{2,1,0:T(1,128)S(1)}, u32[]{:S(2)}, u32[]{:S(2)}) async-start(s32[8,1,4]{2,1,0:T(1,128)} %bitcast.5), calls=%async_computation | async-start | bytes 8192 | tf_op jit(solution)/shard_map/all_to_all | solution.py:111
  28.7 0.7 reshape.165
  29.4 5.7 %all-to-all-done = s32[8,1,4]{2,1,0:T(1,128)S(1)} async-done(((s32[8,1,4]{2,1,0:T(1,128)}), s32[8,1,4]{2,1,0:T(1,128)S(1)}, u32[]{:S(2)}, u32[]{:S(2)}) %all-to-all-start) | async-done | bytes 160 | tf_op jit(solution)/shard_map/all_to_all | solution.py:111
  35.1 3.3 %all-to-all-start.2 = ((bf16[8,2,164]{2,1,0:T(2,128)(2,1)}), bf16[8,2,164]{2,1,0:T(2,128)(2,1)S(1)}, u32[]{:S(2)}, u32[]{:S(2)}) async-start(bf16[8,2,164]{2,1,0:T(2,128)(2,1)} %reshape.165), calls=%async_computation.2 | async-start | bytes 16384 | tf_op jit(solution)/shard_map/all_to_all | solution.py:107
  38.4 2.5 broadcast_in_dim.256
  40.9 11.4 %scatter_fusion.1 = bf16[32,256,256]{2,1,0:T(8,128)(2,1)} fusion(bf16[32,256,256]{2,1,0:T(8,128)(2,1)} %broadcast_in_dim.256, s32[32]{0:T(128)S(1)} %fusion.344, bf16[32,256,256]{2,1,0:T(8,128)(2,1)} %bitcast.96), kind=kCustom, calls=%fused_computation.3 | custom fusion | bytes 12583040 | tf_op jit(solution)/shard_map/scatter | solution.py:101
  52.2 6.0 %all-to-all-start.3 = ((bf16[8,4,256,256]{3,2,1,0:T(8,128)(2,1)}), bf16[8,4,256,256]{3,2,1,0:T(8,128)(2,1)}, u32[]{:S(2)}, u32[]{:S(2)}) async-start(bf16[8,4,256,256]{3,2,1,0:T(8,128)(2,1)} %bitcast.95), calls=%async_computation.3 | async-start | bytes 8388608 | tf_op jit(solution)/shard_map/all_to_all | solution.py:106
  58.3 0.7 fusion.407
  59.2 0.5 broadcast.68
  59.7 0.7 reduce.4
  60.7 88.7 %all-to-all-done.3 = bf16[8,4,256,256]{3,2,1,0:T(8,128)(2,1)} async-done(((bf16[8,4,256,256]{3,2,1,0:T(8,128)(2,1)}), bf16[8,4,256,256]{3,2,1,0:T(8,128)(2,1)}, u32[]{:S(2)}, u32[]{:S(2)}) %all-to-all-start.3) | async-done | bytes 4194336 | tf_op jit(solution)/shard_map/all_to_all | solution.py:106
  149.4 29.0 %while.11 = (s32[]{:T(128)}, bf16[8,4,256,256]{3,2,1,0:T(8,128)(2,1)}, bf16[8,4,2,41]{3,1,2,0:T(4,128)(2,1)S(1)}, bf16[8,4,256,256]{3,2,1,0:T(8,128)(2,1)}, s32[256,256]{1,0:T(8,128)S(1)}, /*index=5*/s32[]{:T(128)}) while((s32[]{:T(128)}, bf16[8,4,256,256]{3,2,1,0:T(8,128)(2,1)}, bf16[8,4,2,41]{3,1,2,0:T(4,128)(2,1)S(1)}, ...), condition=%wide.region_7.8_spmd.clone, body=%wide.region_6.7_spmd.clone.sunk | while | flops 317849600 | bytes 5508169 | solution.py:71
  149.4 1.0 fusion.422
  150.7 2.3 fusion.423
  153.0 1.0 fusion.422
  154.3 2.3 fusion.423
  156.6 1.0 fusion.422
  157.9 2.3 fusion.423
  160.2 1.0 fusion.422
  161.6 2.3 fusion.423
  163.9 1.0 fusion.422
  165.2 2.3 fusion.423
  167.5 1.0 fusion.422
  168.8 2.3 fusion.423
  171.1 1.0 fusion.422
  172.5 2.3 fusion.423
  174.7 1.0 fusion.422
  176.1 2.3 fusion.423
  178.4 4.6 %fusion.24 = f32[4,256,256]{2,0,1:T(4,128)S(1)} fusion(bf16[32,256,256]{2,1,0:T(8,128)(2,1)} %bitcast.97, s32[32]{0:T(128)S(1)} %eq.344, bf16[32]{0:T(256)(128)(2,1)S(1)} %broadcast_in_dim.251), kind=kOutput, calls=%fused_computation.25 | convolution fusion | flops 16777472 | bytes 5243072 | tf_op jit(solution)/shard_map/dot_general | solution.py:126
  183.3 1.1 maximum_maximum_fusion
  184.6 1.5 collective-permute-start
  186.1 3.3 %collective-permute-start.1 = (f32[512,12]{1,0:T(8,128)S(1)}, f32[512,12]{1,0:T(8,128)S(1)}, u32[]{:S(2)}, u32[]{:S(2)}) collective-permute-start(f32[512,12]{1,0:T(8,128)S(1)} %get-tuple-element.66), channel_id=1, source_target_pairs={{4,0},{8,4},{12,8},{16,12},{20,16},{24,20},{28,24},{0,28},{5,1},{9... | collective-permute-start | bytes 73736 | tf_op jit(solution)/shard_map/ppermute | solution.py:23
  189.3 0.7 fusion.408
  190.7 5.8 %collective-permute-done = f32[512,12]{1,0:T(8,128)S(1)} collective-permute-done((f32[512,12]{1,0:T(8,128)S(1)}, f32[512,12]{1,0:T(8,128)S(1)}, u32[]{:S(2)}, u32[]{:S(2)}) %collective-permute-start) | collective-permute-done | bytes 24608 | tf_op jit(solution)/shard_map/ppermute | solution.py:22
  196.5 2.2 collective-permute-done.1
  198.7 19.0 %fusion.27 = f32[512,512]{1,0:T(8,128)S(1)} fusion(f32[512,12]{1,0:T(8,128)S(1)} %collective-permute-done.1, f32[256,256]{1,0:T(8,128)S(1)} %get-tuple-element.70, f32[256,256]{1,0:T(8,128)S(1)} %get-tuple-element.71, f32[256,256]{1,0:T(8,128)S(1)} %get-tuple-element.72, f32[256,256]{1,0:T(8,128)S(1)} %get-tuple-element.69, ...), kind=kOutput, calls=%fused_computation.29 | convolution fusion | flops 1708064768 | bytes 2146404 | tf_op jit(solution)/shard_map/dot_general | solution.py:144
  217.7 21.9 %fusion.26 = f32[512,512]{1,0:T(8,128)} fusion(f32[512,512]{1,0:T(8,128)S(1)} %fusion.27, f32[]{:T(128)} %bitcast.94, f32[]{:T(128)} %bitcast.42, f32[]{:T(128)} %bitcast.41, f32[]{:T(128)} %bitcast.40, f32[]{:T(128)} %bitcast.39, f32[]{:T(128)} %bitcast.38, f32[]{:T(128)} %bitcast.37, f32[]{:T(128)} %bitcast.36, f32[]{:T(128)} %bitcast.35, f32[]{:T(128)} %bitcast.34, ...), kind=kOutput, calls=%fused_computation.28 | convolution fusion | flops 1631059968 | bytes 2097256 | tf_op jit(solution)/shard_map/dot_general | solution.py:148
  239.6 24.1 %reduce-scatter.2.cloned.1.call-done = f32[128,512]{1,0:T(8,128)} async-done(((f32[512,512]{1,0:T(8,128)}), f32[128,512]{1,0:T(8,128)}) %reduce-scatter.2.cloned.1.call-update) | async-done | bytes 262160 | tf_op jit(solution)/shard_map/reduce_scatter | solution.py:150
  (27 shorter events, 3.9 us)
Async XLA Ops:
  11.0 13.7 %all-to-all-start.1 = ((bf16[8,1,4]{2,1,0:T(2,128)(2,1)}), bf16[8,1,4]{2,1,0:T(2,128)(2,1)S(1)}, u32[]{:S(2)}, u32[]{:S(2)}) async-start(bf16[8,1,4]{2,1,0:T(2,128)(2,1)} %all_to_all.24), calls=%async_computation.1 | async-start | bytes 8192 | tf_op jit(solution)/shard_map/all_to_all | solution.py:108
  24.7 10.4 %all-to-all-start = ((s32[8,1,4]{2,1,0:T(1,128)}), s32[8,1,4]{2,1,0:T(1,128)S(1)}, u32[]{:S(2)}, u32[]{:S(2)}) async-start(s32[8,1,4]{2,1,0:T(1,128)} %bitcast.5), calls=%async_computation | async-start | bytes 8192 | tf_op jit(solution)/shard_map/all_to_all | solution.py:111
  35.1 17.2 %all-to-all-start.2 = ((bf16[8,2,164]{2,1,0:T(2,128)(2,1)}), bf16[8,2,164]{2,1,0:T(2,128)(2,1)S(1)}, u32[]{:S(2)}, u32[]{:S(2)}) async-start(bf16[8,2,164]{2,1,0:T(2,128)(2,1)} %reshape.165), calls=%async_computation.2 | async-start | bytes 16384 | tf_op jit(solution)/shard_map/all_to_all | solution.py:107
  52.2 6.1 %copy-start = (f32[1,25]{1,0:T(1,128)S(1)}, f32[1,25]{1,0:T(1,128)}, u32[]{:S(2)}) copy-start(f32[1,25]{1,0:T(1,128)} %param.14) | copy-start | bytes 304
  52.2 97.1 %all-to-all-start.3 = ((bf16[8,4,256,256]{3,2,1,0:T(8,128)(2,1)}), bf16[8,4,256,256]{3,2,1,0:T(8,128)(2,1)}, u32[]{:S(2)}, u32[]{:S(2)}) async-start(bf16[8,4,256,256]{3,2,1,0:T(8,128)(2,1)} %bitcast.95), calls=%async_computation.3 | async-start | bytes 8388608 | tf_op jit(solution)/shard_map/all_to_all | solution.py:106
  58.3 205.4 %reduce-scatter.2.cloned.1.call-start = ((), (), s32[]{:S(2)}) async-start(), calls=%async_computation.5 | async-start | bytes 1310720 | tf_op jit(solution)/shard_map/reduce_scatter | solution.py:150
  184.6 11.9 %collective-permute-start = (f32[512,12]{1,0:T(8,128)S(1)}, f32[512,12]{1,0:T(8,128)S(1)}, u32[]{:S(2)}, u32[]{:S(2)}) collective-permute-start(f32[512,12]{1,0:T(8,128)S(1)} %get-tuple-element.65), channel_id=1, source_target_pairs={{0,4},{4,8},{8,12},{12,16},{16,20},{20,24},{24,28},{28,0},{1,5},{5... | collective-permute-start | bytes 73736 | tf_op jit(solution)/shard_map/ppermute | solution.py:22
  186.1 12.6 %collective-permute-start.1 = (f32[512,12]{1,0:T(8,128)S(1)}, f32[512,12]{1,0:T(8,128)S(1)}, u32[]{:S(2)}, u32[]{:S(2)}) collective-permute-start(f32[512,12]{1,0:T(8,128)S(1)} %get-tuple-element.66), channel_id=1, source_target_pairs={{4,0},{8,4},{12,8},{16,12},{20,16},{24,20},{28,24},{0,28},{5,1},{9... | collective-permute-start | bytes 73736 | tf_op jit(solution)/shard_map/ppermute | solution.py:23
Sparse Core Ops, SparseCore 0:
  239.7 23.9 reduce-scatter.1
where the time goes:
time: 272 us; the launch traced here: 271 us
  waiting for transfers between devices  129 us (47%)
  matrix products  71.5 us (26%)
  local copies, waits for them, and re-layouts  25.7 us (9%)
  starting transfers between devices  25.4 us (9%)
  between operations  14.8 us (5%)
  other arithmetic  4.5 us (2%)
    all_to_all x1, waiting for transfers between devices, local(): lax.all_to_all(block_buffer, 'patch', split_axis=0, concat_axis=0, tiled=...  88.7 us
    reduce_scatter x1, waiting for transfers between devices, local(): lax.psum_scatter(band_term, 'band', scatter_dimension=0, tiled=True)  24.1 us
    dot_general x1, matrix products, local(): row_pass = jnp.dot(row_table, col_pass, precision=lax.Precision.HIGHEST)  21.9 us
    dot_general x1, matrix products, local(): lax.dot_general(padded, col_table, (((1,), (1,)), ((), ())), precision=la...  19 us
    dot_general x8, matrix products, match_group(): jnp.einsum('nij,nkj->nik', half_pass, matrices[:, 1], preferred_element_t...  18.4 us
    scatter x1, local copies, waits for them, and re-layouts, local(): block_buffer = jnp.zeros((total_slots, block_edge, block_edge), jnp.bfloa...  11.4 us
    dot_general x8, matrix products, match_group(): jnp.einsum('nct,tij->ncij', group_taps, onehot, preferred_element_type=jn...  7.63 us
    all_to_all x1, starting transfers between devices, local(): lax.all_to_all(weight_buffer, 'patch', split_axis=0, concat_axis=0, tiled...  7.28 us
  transfers between devices with their start and end apart: 7, of which 6 were waited for; matrix products, arithmetic and copies ran while one was open for 8% of the time, Pallas kernels for 0%

commit v1 on v0

v1 whole, which is shorter than its diff:
```python
import jax
import jax.numpy as jnp
import numpy as np
from jax import lax
from jax.experimental import pallas as pl
from jax.experimental.pallas import tpu as pltpu
from jax.sharding import PartitionSpec as P

TH = 2
TW = 2
DR = 12
CAP = 4
SLOTS = 4
PAD = 16
DIGITS = 16
UNIT = 512


def dest_table(outer):
    table = np.zeros((outer, outer), np.int32)
    for z in range(outer):
        def due(d):
            if d > z:
                return (outer - 1 + z - d, 0)
            if d < z:
                return (outer - 1 - z + d, 1)
            return (outer, 0)

        table[z] = sorted(range(outer), key=due)
    return table


def toeplitz(row):
    half = row.shape[1] // 2
    wide = jnp.broadcast_to(row, (half, 2 * half))
    skew = pltpu.roll(wide, 0, 1, stride=1, stride_axis=0)
    diag = skew[:, :half]
    off = skew[:, half:]
    i = lax.broadcasted_iota(jnp.int32, (half, half), 0)
    j = lax.broadcasted_iota(jnp.int32, (half, half), 1)
    upper = jnp.where(j < i, off, 0.0)
    lower = jnp.where(j > i, off, 0.0)
    top = jnp.concatenate([diag, upper], axis=1)
    bottom = jnp.concatenate([lower, diag], axis=1)
    return jnp.concatenate([top, bottom], axis=0).astype(jnp.bfloat16)


def match_kernel(npatch, lists, order, blocks, taps, *rest):
    outs = rest[:npatch]
    acc, pay, edges, digits, count, index, sems = rest[npatch:]
    number, edge = blocks.shape[0], blocks.shape[-1]
    ntaps = taps.shape[-1]
    side = TH * edge

    def clear(p, carry):
        count[p] = 0
        for r in range(CAP):
            index[p * CAP + r] = -1
        return carry

    lax.fori_loop(0, npatch, clear, 0)

    def place(n, carry):
        p = lists[0, n]
        r = count[p]
        count[p] = r + 1
        index[p * CAP + r] = n
        return carry

    lax.fori_loop(0, number, place, 0)

    lane = lax.broadcasted_iota(jnp.int32, (8, 128), 1)

    def patch(k, carry):
        p = order[k]
        acc[...] = jnp.zeros(acc.shape, acc.dtype)
        row = jnp.zeros((8, 128), jnp.float32)
        for r in range(CAP):
            found = index[p * CAP + r]
            n = jnp.maximum(found, 0)
            s = lists[1, n]
            units = jnp.where(found >= 0, lists[2, n], 0)
            w = units.astype(jnp.float32) * (1.0 / UNIT)
            tap = taps[n].astype(jnp.float32)
            tap = jnp.concatenate([tap, jnp.zeros((2, edge - ntaps), jnp.float32)], axis=1)
            tap = pltpu.roll(tap, edge - ntaps // 2, 1)
            col = toeplitz(tap[0:1])
            half = jnp.dot(col, blocks[n], preferred_element_type=jnp.float32).astype(jnp.bfloat16)
            rowm = toeplitz(tap[1:2])
            matched = lax.dot_general(
                rowm, half, (((1,), (1,)), ((), ())), preferred_element_type=jnp.float32
            ).astype(jnp.bfloat16)
            acc[s] = acc[s] + w * matched.astype(jnp.float32)
            bit = lax.shift_right_logical(jnp.full((8, 128), units), lane % DIGITS) & 1
            row = row + jnp.where(lane // DIGITS == s, bit, 0).astype(jnp.float32)
        digits[p] = row
        for s in range(SLOTS):
            top = (s % TW) * edge
            left = (s // TW) * edge
            pay[k, PAD + top : PAD + top + edge, left : left + edge] = acc[s].astype(jnp.bfloat16)
        edges[p, 0] = pay[k, PAD : 2 * PAD, :]
        edges[p, 1] = pay[k, side : side + PAD, :]
        return carry

    lax.fori_loop(0, npatch, patch, 0)

    first = lax.broadcasted_iota(jnp.int32, (PAD, side), 0) == 0
    for k in range(npatch):
        p = order[k]
        before = lax.rem(p + npatch - 1, npatch)
        after = lax.rem(p + 1, npatch)
        row = jnp.concatenate(
            [digits[p], digits[before], digits[after], jnp.zeros((8, side - 3 * 128), jnp.float32)],
            axis=1,
        )
        row = jnp.concatenate([row, row], axis=0)
        pay[k, :PAD, :] = jnp.where(first, row, edges[before, 1].astype(jnp.float32)).astype(jnp.bfloat16)
        pay[k, PAD + side :, :] = edges[after, 0]
        pltpu.make_async_copy(pay.at[k], outs[k], sems.at[k]).start()
    for k in range(npatch):
        pltpu.make_async_copy(pay.at[k], outs[k], sems.at[k]).wait()


def match_blocks(lists, order, blocks, taps):
    npatch = order.shape[0]
    edge = blocks.shape[-1]
    side = TH * edge
    rows = side + 2 * PAD
    smem = pl.BlockSpec(memory_space=pltpu.SMEM)
    vmem = pl.BlockSpec(memory_space=pltpu.VMEM)
    return pl.pallas_call(
        lambda *refs: match_kernel(npatch, *refs),
        out_shape=[jax.ShapeDtypeStruct((rows, side), jnp.bfloat16)] * npatch,
        in_specs=[smem] * 2 + [vmem] * 2,
        out_specs=[pl.BlockSpec(memory_space=pl.ANY)] * npatch,
        scratch_shapes=[
            pltpu.VMEM((SLOTS, edge, edge), jnp.float32),
            pltpu.VMEM((npatch, rows, side), jnp.bfloat16),
            pltpu.VMEM((npatch, 2, PAD, side), jnp.bfloat16),
            pltpu.VMEM((npatch, 8, 128), jnp.float32),
            pltpu.SMEM((npatch,), jnp.int32),
            pltpu.SMEM((npatch * CAP,), jnp.int32),
            pltpu.SemaphoreType.DMA((npatch,)),
        ],
        compiler_params=pltpu.CompilerParams(vmem_limit_bytes=48 * 1024 * 1024),
        name="match",
    )(lists, order, blocks, taps)


def split(value):
    high = value.astype(jnp.bfloat16)
    return high, (value - high.astype(jnp.float32)).astype(jnp.bfloat16)


def dot3(ah, al, bh, bl, dims):
    def one(a, b):
        return lax.dot_general(a, b, (dims, ((), ())), preferred_element_type=jnp.float32)

    return one(ah, bh) + (one(ah, bl) + one(al, bh))


def tail_kernel(own, other, up, down, noise, colh, coll, rowh, rowl, image, chi):
    f32 = jnp.float32
    side = image.shape[0]
    edge = side // TH
    total = own[...].astype(f32) + other[...].astype(f32) + (up[...].astype(f32) + down[...].astype(f32))
    row = total[0:1, :]
    lane = lax.broadcasted_iota(jnp.int32, (1, side), 1)
    value = row * lax.shift_left(jnp.ones((1, side), jnp.int32), lane % DIGITS).astype(f32) * (1.0 / UNIT)

    def scale(group, s):
        here = (lane >= group * 128 + s * DIGITS) & (lane < group * 128 + (s + 1) * DIGITS)
        weight_sum = jnp.sum(jnp.where(here, value, 0.0), axis=1, keepdims=True)
        return jnp.broadcast_to(1.0 / jnp.maximum(weight_sum, 1.0), (1, edge))

    def factors(group, column):
        return jnp.concatenate([scale(group, r * TW + column) for r in range(TH)], axis=1)

    parts = [total[:PAD] * factors(1, TW - 1)]
    for column in range(TW):
        parts.append(total[PAD + column * edge : PAD + (column + 1) * edge] * factors(0, column))
    parts.append(total[PAD + side :] * factors(2, 0))
    padded = jnp.concatenate(parts, axis=0)
    image[...] = padded[PAD : PAD + side].T
    ph, plo = split(padded)
    col_pass = dot3(colh[...], coll[...], ph, plo, ((1,), (0,)))
    ch, cl = split(col_pass)
    row_pass = dot3(rowh[...], rowl[...], ch, cl, ((1,), (1,)))
    chi[...] = row_pass * row_pass * (1.0 / noise[0])


def tables_kernel(det, colh, coll, rowh, rowl):
    for high, low, start in ((colh, coll, DR - PAD), (rowh, rowl, DR)):
        offsets = (
            lax.broadcasted_iota(jnp.int32, high.shape, 1)
            - lax.broadcasted_iota(jnp.int32, high.shape, 0)
            + start
        )
        table = jnp.zeros(high.shape, jnp.float32)
        for tap in range(det.shape[1]):
            table = jnp.where(offsets == tap, det[0, tap], table)
        high[...], low[...] = split(table)


def filter_tables(det, rows, side):
    return pl.pallas_call(
        tables_kernel,
        out_shape=[jax.ShapeDtypeStruct(s, jnp.bfloat16) for s in [(side, rows)] * 2 + [(side, side)] * 2],
        in_specs=[pl.BlockSpec(memory_space=pltpu.SMEM)],
        out_specs=[pl.BlockSpec(memory_space=pltpu.VMEM)] * 4,
        compiler_params=pltpu.CompilerParams(vmem_limit_bytes=40 * 1024 * 1024),
        cost_estimate=pl.CostEstimate(flops=20_000_000, bytes_accessed=2_000_000, transcendentals=0),
        name="tables",
    )(det)


def finish(own, other, up, down, noise, det):
    rows, side = own.shape
    colh, coll, rowh, rowl = filter_tables(det, rows, side)
    smem = pl.BlockSpec(memory_space=pltpu.SMEM)
    vmem = pl.BlockSpec(memory_space=pltpu.VMEM)
    return pl.pallas_call(
        tail_kernel,
        out_shape=[jax.ShapeDtypeStruct((side, side), jnp.float32)] * 2,
        in_specs=[vmem] * 4 + [smem] + [vmem] * 4,
        out_specs=[vmem] * 2,
        compiler_params=pltpu.CompilerParams(vmem_limit_bytes=40 * 1024 * 1024),
        name="finish",
    )(own, other, up, down, noise, colh, coll, rowh, rowl)


def local(blocks, dest_patch, dest_slot, weights, psf_taps, det_taps, noise_var):
    f32, bf16 = jnp.float32, jnp.bfloat16
    npatch = lax.axis_size("patch")
    outer = npatch // 2
    me = lax.axis_index("patch")
    z = me // 2
    table = dest_table(outer)
    where_is = np.argsort(table, axis=1)
    order = np.zeros((npatch, npatch), np.int32)
    for i in range(npatch):
        for s in range(outer):
            order[i, 2 * s] = table[i // 2, s] * 2 + 1 - i % 2
            order[i, 2 * s + 1] = table[i // 2, s] * 2 + i % 2
    order = lax.dynamic_index_in_dim(jnp.asarray(order), me, 0, keepdims=False)
    units = (weights.astype(f32) * UNIT).astype(jnp.int32)
    lists = jnp.concatenate([dest_patch, dest_slot, units], axis=0)
    payloads = match_blocks(lists, order, blocks[0], psf_taps[0])
    swap = [(i, i ^ 1) for i in range(npatch)]
    kept = []
    for s in range(outer):
        other = lax.ppermute(payloads[2 * s], "patch", swap)
        kept.append((payloads[2 * s + 1], other))

    def combined(s):
        return kept[s][0].astype(f32) + kept[s][1].astype(f32)

    def chosen(places):
        values = sorted(set(places.values()))
        result = combined(values[-1])
        for v in values[:-1]:
            mine = functools_any([z == q for q, s in places.items() if s == v])
            result = jnp.where(mine, combined(v), result)
        return result

    up = down = None
    for t in range(outer - 1):
        up_places = {q: int(where_is[q][outer - 1 - t + q]) for q in range(t + 1)}
        down_places = {outer - 1 - q: int(where_is[outer - 1 - q][t - q]) for q in range(t + 1)}
        send_up = chosen(up_places)
        send_down = chosen(down_places)
        if up is not None:
            send_up = send_up + up.astype(f32)
            send_down = send_down + down.astype(f32)
        up_pairs = [(2 * q + y, 2 * q + 2 + y) for q in range(t + 1) for y in range(2)]
        down_pairs = [(npatch - 1 - a, npatch - 1 - b) for a, b in up_pairs]
        up = lax.ppermute(send_up.astype(bf16), "patch", up_pairs)
        down = lax.ppermute(send_down.astype(bf16), "patch", down_pairs)
    image, term = finish(kept[-1][0], kept[-1][1], up, down, noise_var, det_taps)
    band = lax.axis_index("band")
    rows = term.shape[0] // 4
    chunks = term.reshape(2, 2, rows, term.shape[1])
    core, far = band % 2, band // 2
    mine = lax.dynamic_index_in_dim(chunks, core, 1, keepdims=False)
    theirs = lax.dynamic_index_in_dim(chunks, 1 - core, 1, keepdims=False)
    pair = mine + lax.ppermute(theirs, "band", [(i, i ^ 1) for i in range(4)])
    mine = lax.dynamic_index_in_dim(pair, far, 0, keepdims=False)
    theirs = lax.dynamic_index_in_dim(pair, 1 - far, 0, keepdims=False)
    chi = mine + lax.ppermute(theirs, "band", [(i, i ^ 2) for i in range(4)])
    return image[None], chi


def functools_any(flags):
    result = flags[0]
    for flag in flags[1:]:
        result = result | flag
    return result


def solution(mesh):
    in_specs = (
        P("band", "patch", None, None),
        P("band", "patch"),
        P("band", "patch"),
        P("band", "patch"),
        P("band", "patch", None, None),
        P("band", None),
        P("band"),
    )
    out_specs = (P("band", None, "patch"), P("band", "patch"))
    return jax.shard_map(local, mesh=mesh, in_specs=in_specs, out_specs=out_specs, check_vma=False)
```

time: 272 us -> 102 us (0.38)
  waiting for transfers between devices: 129 us -> 42.2 us
  matrix products: 71.5 us -> 0 us
  local copies, waits for them, and re-layouts: 25.7 us -> 1.48 us
  Pallas kernels: 0 us -> 16.4 us
  between operations: 14.8 us -> 1.42 us
  starting transfers between devices: 25.4 us -> 31.1 us
  other arithmetic: 4.5 us -> 9.24 us
    all_to_all x4 -> x0, waiting for transfers between devices: 96.4 us -> none  [the longest x1 88.7 us: local(): lax.all_to_all(block_buffer, 'patch', split_axis=0, concat_axis=0, tiled=...]
    dot_general x19 -> x0, matrix products: 71.5 us -> none  [the longest x1 21.9 us: local(): row_pass = jnp.dot(row_table, col_pass, precision=lax.Precision.HIGHEST)]
    ppermute x2 -> x12, waiting for transfers between devices: 8.01 us -> 42.2 us  [the longest x4 16.6 us: local(): other = lax.ppermute(payloads[2 * s], 'patch', swap)]
    ppermute x2 -> x12, starting transfers between devices: 4.78 us -> 31.1 us  [the longest x3 19.1 us: local(): up = lax.ppermute(send_up.astype(bf16), 'patch', up_pairs)]
    reduce_scatter x1 -> x0, waiting for transfers between devices: 24.1 us -> none  [local(): lax.psum_scatter(band_term, 'band', scatter_dimension=0, tiled=True)]
    all_to_all x4 -> x0, starting transfers between devices: 20.6 us -> none  [the longest x1 7.28 us: local(): lax.all_to_all(weight_buffer, 'patch', split_axis=0, concat_axis=0, tiled...]
    pallas_call x0 -> x3, Pallas kernels: none -> 16.4 us  [the longest x1 11.1 us: match_blocks(): pl.pallas_call(lambda *refs: match_kernel(npatch, *refs), out_shape=[jax....]
    scatter x4 -> x0, local copies, waits for them, and re-layouts: 15.9 us -> none  [the longest x1 11.4 us: local(): block_buffer = jnp.zeros((total_slots, block_edge, block_edge), jnp.bfloa...]
  transfers between devices with their start and end apart: 7 -> 12, of which waited for: 6 -> 8; matrix products, arithmetic and copies ran while one was open for 8% -> 7% of each run, Pallas kernels for 0% -> 2%
where the time goes in v1:
time: 102 us
  waiting for transfers between devices  42.2 us (41%)
  starting transfers between devices  31.1 us (30%)
  Pallas kernels  16.4 us (16%)
  other arithmetic  9.24 us (9%)
  local copies, waits for them, and re-layouts  1.48 us (1%)
  between operations  1.42 us (1%)
    ppermute x3, starting transfers between devices, local(): up = lax.ppermute(send_up.astype(bf16), 'patch', up_pairs)  19.1 us
    ppermute x4, waiting for transfers between devices, local(): other = lax.ppermute(payloads[2 * s], 'patch', swap)  16.6 us
    ppermute x3, waiting for transfers between devices, local(): up = lax.ppermute(send_up.astype(bf16), 'patch', up_pairs)  12.8 us
    pallas_call x1, Pallas kernels, match_blocks(): pl.pallas_call(lambda *refs: match_kernel(npatch, *refs), out_shape=[jax....  11.1 us
    ppermute x1, waiting for transfers between devices, local(): chi = mine + lax.ppermute(theirs, 'band', [(i, i ^ 2) for i in range(4)])  6.86 us
    ppermute x4, starting transfers between devices, local(): other = lax.ppermute(payloads[2 * s], 'patch', swap)  6.15 us
    convert_element_type x2, other arithmetic, local(): down = lax.ppermute(send_down.astype(bf16), 'patch', down_pairs)  6.07 us
    ppermute x3, starting transfers between devices, local(): down = lax.ppermute(send_down.astype(bf16), 'patch', down_pairs)  4.23 us
  transfers between devices with their start and end apart: 12, of which 8 were waited for; matrix products, arithmetic and copies ran while one was open for 7% of the time, Pallas kernels for 2%

profile of v1, /device:TPU:0, one launch (start us, length us, event | category | flops | bytes accessed | tf_op | source)
XLA Modules:
  0.0 101.8 jit_solution(11550436472685051081)
XLA Ops:
  0.6 0.7 multiply_convert_fusion
  1.3 0.7 fusion.1.refs_1_
  2.0 0.7 pad_add_fusion.refs_0_
  2.7 0.0 copy-start
  2.7 0.7 copy-done
  3.4 11.1 %match.1 = (bf16[544,512]{1,0:T(8,128)(2,1)S(1)}, bf16[544,512]{1,0:T(8,128)(2,1)S(1)}, bf16[544,512]{1,0:T(8,128)(2,1)S(1)}, bf16[544,512]{1,0:T(8,128)(2,1)S(1...) custom-call(s32[3,32]{1,0:T(4,128)S(1)} %pad_add_fusion.refs_0_, ...), custom_call_target="tpu_custom_call" | custom-call | tf_op jit(solution)/shard_map/match/pallas_call | solution.py:131
  14.5 3.0 %collective-permute-start.3 = (bf16[544,512]{1,0:T(8,128)(2,1)S(1)}, bf16[544,512]{1,0:T(8,128)(2,1)S(1)}, u32[]{:S(2)}, u32[]{:S(2)}) collective-permute-start(bf16[544,512]{1,0:T(8,128)(2,1)S(1)} %get-tuple-element.23), channel_id=1, source_target_pairs={{0,4},{4,0},{8,12},{12,8},{16,20},{20,16},{24,28},{28,24},{1,5},{5... | collective-permute-start | bytes 1671176 | tf_op jit(solution)/shard_map/ppermute | solution.py:252
  17.6 0.1 collective-permute-start.1
  17.6 13.4 %collective-permute-done.3 = bf16[544,512]{1,0:T(8,128)(2,1)S(1)} collective-permute-done((bf16[544,512]{1,0:T(8,128)(2,1)S(1)}, bf16[544,512]{1,0:T(8,128)(2,1)S(1)}, u32[]{:S(2)}, u32[]{:S(2)}) %collective-permute-start.3) | collective-permute-done | bytes 557088 | tf_op jit(solution)/shard_map/ppermute | solution.py:252
  31.0 0.0 copy-start.2
  31.0 1.0 fusion
  32.0 4.8 %collective-permute-start.4 = (bf16[544,512]{1,0:T(8,128)(2,1)}, bf16[544,512]{1,0:T(8,128)(2,1)}, u32[]{:S(2)}, u32[]{:S(2)}) collective-permute-start(bf16[544,512]{1,0:T(8,128)(2,1)} %fusion), channel_id=1, source_target_pairs={{0,8},{4,12},{1,9},{5,13},{2,10},{6,14},{3,11},{7,15}} | collective-permute-start | bytes 1671176 | tf_op jit(solution)/shard_map/ppermute | solution.py:277
  36.9 1.5 %collective-permute-start.7 = (bf16[544,512]{1,0:T(8,128)(2,1)}, bf16[544,512]{1,0:T(8,128)(2,1)}, u32[]{:S(2)}, u32[]{:S(2)}) collective-permute-start(bf16[544,512]{1,0:T(8,128)(2,1)} %fusion), channel_id=1, source_target_pairs={{28,20},{24,16},{29,21},{25,17},{30,22},{26,18},{31,23},{27,19}} | collective-permute-start | bytes 1671176 | tf_op jit(solution)/shard_map/ppermute | solution.py:278
  38.3 0.0 copy-done.2
  38.3 1.5 %collective-permute-start.2 = (bf16[544,512]{1,0:T(8,128)(2,1)S(1)}, bf16[544,512]{1,0:T(8,128)(2,1)}, u32[]{:S(2)}, u32[]{:S(2)}) collective-permute-start(bf16[544,512]{1,0:T(8,128)(2,1)S(1)} %get-tuple-element.21), channel_id=1, source_target_pairs={{0,4},{4,0},{8,12},{12,8},{16,20},{20,16},{24,28},{28,24},{1,5},{5... | collective-permute-start | bytes 1671176 | tf_op jit(solution)/shard_map/ppermute | solution.py:252
  39.8 3.2 %collective-permute-done.1 = bf16[544,512]{1,0:T(8,128)(2,1)} collective-permute-done((bf16[544,512]{1,0:T(8,128)(2,1)S(1)}, bf16[544,512]{1,0:T(8,128)(2,1)}, u32[]{:S(2)}, u32[]{:S(2)}) %collective-permute-start.1) | collective-permute-done | bytes 557088 | tf_op jit(solution)/shard_map/ppermute | solution.py:252
  43.1 3.1 %collective-permute-done.4 = bf16[544,512]{1,0:T(8,128)(2,1)} collective-permute-done((bf16[544,512]{1,0:T(8,128)(2,1)}, bf16[544,512]{1,0:T(8,128)(2,1)}, u32[]{:S(2)}, u32[]{:S(2)}) %collective-permute-start.4) | collective-permute-done | bytes 557088 | tf_op jit(solution)/shard_map/ppermute | solution.py:277
  46.2 0.0 collective-permute-done.7
  46.2 3.0 %add_convert_fusion.1 = (bf16[544,512]{1,0:T(8,128)(2,1)}, bf16[544,512]{1,0:T(8,128)(2,1)}) fusion(bf16[544,512]{1,0:T(8,128)(2,1)} %collective-permute-done.7, bf16[544,512]{1,0:T(8,128)(2,1)} %collective-permute-done.1, bf16[544,512]{1,0:T(8,128)(2,1)S(1)} %get-tuple-element.18, bf16[544,512]{1,0:T(8,128)(2,1)} %copy-done.2, ...), kind=kLoop, calls=%fused_computation.1 | loop fusion | flops 3899392 | bytes 4456450 | tf_op jit(solution)/shard_map/convert_element_type | solution.py:278
  49.3 5.2 %collective-permute-start.5 = (bf16[544,512]{1,0:T(8,128)(2,1)}, bf16[544,512]{1,0:T(8,128)(2,1)}, u32[]{:S(2)}, u32[]{:S(2)}) collective-permute-start(bf16[544,512]{1,0:T(8,128)(2,1)} %get-tuple-element.31), channel_id=1, source_target_pairs={{0,8},{4,12},{8,16},{12,20},{1,9},{5,13},{9,17},{13,21},{2,10},{6,... | collective-permute-start | bytes 1671176 | tf_op jit(solution)/shard_map/ppermute | solution.py:277
  54.4 1.5 %collective-permute-start.8 = (bf16[544,512]{1,0:T(8,128)(2,1)}, bf16[544,512]{1,0:T(8,128)(2,1)}, u32[]{:S(2)}, u32[]{:S(2)}) collective-permute-start(bf16[544,512]{1,0:T(8,128)(2,1)} %get-tuple-element.30), channel_id=1, source_target_pairs={{28,20},{24,16},{20,12},{16,8},{29,21},{25,17},{21,13},{17,9},{30,... | collective-permute-start | bytes 1671176 | tf_op jit(solution)/shard_map/ppermute | solution.py:278
  55.9 1.5 %collective-permute-start = (bf16[544,512]{1,0:T(8,128)(2,1)}, bf16[544,512]{1,0:T(8,128)(2,1)S(1)}, u32[]{:S(2)}, u32[]{:S(2)}) collective-permute-start(bf16[544,512]{1,0:T(8,128)(2,1)} %get-tuple-element.17), channel_id=1, source_target_pairs={{0,4},{4,0},{8,12},{12,8},{16,20},{20,16},{24,28},{28,24},{1,5},{5... | collective-permute-start | bytes 1671176 | tf_op jit(solution)/shard_map/ppermute | solution.py:252
  57.4 0.0 collective-permute-done.2
  57.4 5.4 %collective-permute-done.5 = bf16[544,512]{1,0:T(8,128)(2,1)} collective-permute-done((bf16[544,512]{1,0:T(8,128)(2,1)}, bf16[544,512]{1,0:T(8,128)(2,1)}, u32[]{:S(2)}, u32[]{:S(2)}) %collective-permute-start.5) | collective-permute-done | bytes 557088 | tf_op jit(solution)/shard_map/ppermute | solution.py:277
  62.9 0.0 collective-permute-done.8
  62.9 0.0 copy-start.1
  62.9 3.0 %add_convert_fusion = (bf16[544,512]{1,0:T(8,128)(2,1)}, bf16[544,512]{1,0:T(8,128)(2,1)}) fusion(bf16[544,512]{1,0:T(8,128)(2,1)} %collective-permute-done.8, bf16[544,512]{1,0:T(8,128)(2,1)} %collective-permute-done.2, bf16[544,512]{1,0:T(8,128)(2,1)S(1)} %get-tuple-element.20, bf16[544,512]{1,0:T(8,128)(2,1)} %collective-permute-done.5, ...), kind=kLoop, calls=%fused_computation | loop fusion | flops 3620864 | bytes 4456449 | tf_op jit(solution)/shard_map/convert_element_type | solution.py:278
  65.9 9.1 %collective-permute-start.6 = (bf16[544,512]{1,0:T(8,128)(2,1)}, bf16[544,512]{1,0:T(8,128)(2,1)S(1)}, u32[]{:S(2)}, u32[]{:S(2)}) collective-permute-start(bf16[544,512]{1,0:T(8,128)(2,1)} %get-tuple-element.33), channel_id=1, source_target_pairs={{0,8},{4,12},{8,16},{12,20},{16,24},{20,28},{1,9},{5,13},{9,17},{1... | collective-permute-start | bytes 1671176 | tf_op jit(solution)/shard_map/ppermute | solution.py:277
  75.0 1.3 %collective-permute-start.9 = (bf16[544,512]{1,0:T(8,128)(2,1)}, bf16[544,512]{1,0:T(8,128)(2,1)S(1)}, u32[]{:S(2)}, u32[]{:S(2)}) collective-permute-start(bf16[544,512]{1,0:T(8,128)(2,1)} %get-tuple-element.32), channel_id=1, source_target_pairs={{28,20},{24,16},{20,12},{16,8},{12,4},{8,0},{29,21},{25,17},{21,13... | collective-permute-start | bytes 1671176 | tf_op jit(solution)/shard_map/ppermute | solution.py:278
  77.0 0.0 copy-done.1
  77.0 1.8 %tables.1 = (bf16[512,544]{1,0:T(8,128)(2,1)S(1)}, bf16[512,544]{1,0:T(8,128)(2,1)S(1)}, bf16[512,512]{1,0:T(8,128)(2,1)S(1)}, bf16[512,512]{1,0:T(8,128)(2,1)S(1)}) custom-call(f32[1,25]{1,0:T(1,128)S(1)} %copy-done.1), custom_call_target="tpu_custom_call" | custom-call | flops 20000000 | bytes 2000000 | tf_op jit(solution)/shard_map/tables/pallas_call | solution.py:206
  78.8 0.0 collective-permute-done.other
  78.8 4.2 %collective-permute-done.6.up = bf16[544,512]{1,0:T(8,128)(2,1)S(1)} collective-permute-done((bf16[544,512]{1,0:T(8,128)(2,1)}, bf16[544,512]{1,0:T(8,128)(2,1)S(1)}, u32[]{:S(2)}, u32[]{:S(2)}) %collective-permute-start.6) | collective-permute-done | bytes 557088 | tf_op jit(solution)/shard_map/ppermute | solution.py:277
  83.0 4.0 %collective-permute-done.9.down = bf16[544,512]{1,0:T(8,128)(2,1)S(1)} collective-permute-done((bf16[544,512]{1,0:T(8,128)(2,1)}, bf16[544,512]{1,0:T(8,128)(2,1)S(1)}, u32[]{:S(2)}, u32[]{:S(2)}) %collective-permute-start.9) | collective-permute-done | bytes 557088 | tf_op jit(solution)/shard_map/ppermute | solution.py:278
  87.1 3.5 %finish.1 = (f32[512,512]{1,0:T(8,128)}, f32[512,512]{1,0:T(8,128)S(1)}) custom-call(bf16[544,512]{1,0:T(8,128)(2,1)S(1)} %get-tuple-element.16.own, bf16[544,512]{1,0:T(8,128)(2,1)S(1)} %collective-permute-done.other, bf16[544,512]{1,0:T(8,128)(2,1)S(1)} %collective-permute-done.6.up, bf16[544,512]{1,0:T(8,128)(2,1)S(1)} %collective-permute-done.9.down, ...), custom_call_target="tpu_custom_call" | custom-call | tf_op jit(solution)/shard_map/finish/pallas_call | solution.py:222
  90.6 0.1 collective-permute-start.10
  90.7 1.9 %collective-permute-done.10 = f32[2,128,512]{2,1,0:T(8,128)S(1)} collective-permute-done((f32[2,128,512]{2,1,0:T(8,128)S(1)}, f32[2,128,512]{2,1,0:T(8,128)S(1)}, u32[]{:S(2)}, u32[]{:S(2)}) %collective-permute-start.10) | collective-permute-done | bytes 524320 | tf_op jit(solution)/shard_map/ppermute | solution.py:286
  92.5 0.1 bitcast_add_fusion
  92.7 1.6 %collective-permute-start.11 = (f32[128,512]{1,0:T(8,128)S(1)}, f32[128,512]{1,0:T(8,128)S(1)}, u32[]{:S(2)}, u32[]{:S(2)}) collective-permute-start(f32[128,512]{1,0:T(8,128)S(1)} %dynamic-slice_bitcast_fusion.1), channel_id=1, source_target_pairs={{0,2},{1,3},{2,0},{3,1},{4,6},{5,7},{6,4},{7,5},{8,10},{9,11},{10,... | collective-permute-start | bytes 786440 | tf_op jit(solution)/shard_map/ppermute | solution.py:289
  94.2 6.9 %collective-permute-done.11 = f32[128,512]{1,0:T(8,128)S(1)} collective-permute-done((f32[128,512]{1,0:T(8,128)S(1)}, f32[128,512]{1,0:T(8,128)S(1)}, u32[]{:S(2)}, u32[]{:S(2)}) %collective-permute-start.11) | collective-permute-done | bytes 262176 | tf_op jit(solution)/shard_map/ppermute | solution.py:289
  101.1 0.7 bitcast_add_fusion.1
  (2 shorter events, 0.1 us)
Async XLA Ops:
  2.7 0.7 copy-start
  14.5 16.5 %collective-permute-start.3 = (bf16[544,512]{1,0:T(8,128)(2,1)S(1)}, bf16[544,512]{1,0:T(8,128)(2,1)S(1)}, u32[]{:S(2)}, u32[]{:S(2)}) collective-permute-start(bf16[544,512]{1,0:T(8,128)(2,1)S(1)} %get-tuple-element.23), channel_id=1, source_target_pairs={{0,4},{4,0},{8,12},{12,8},{16,20},{20,16},{24,28},{28,24},{1,5},{5... | collective-permute-start | bytes 1671176 | tf_op jit(solution)/shard_map/ppermute | solution.py:252
  17.6 25.5 %collective-permute-start.1 = (bf16[544,512]{1,0:T(8,128)(2,1)S(1)}, bf16[544,512]{1,0:T(8,128)(2,1)}, u32[]{:S(2)}, u32[]{:S(2)}) collective-permute-start(bf16[544,512]{1,0:T(8,128)(2,1)S(1)} %get-tuple-element.19), channel_id=1, source_target_pairs={{0,4},{4,0},{8,12},{12,8},{16,20},{20,16},{24,28},{28,24},{1,5},{5... | collective-permute-start | bytes 1671176 | tf_op jit(solution)/shard_map/ppermute | solution.py:252
  31.0 7.3 %copy-start.2 = (bf16[544,512]{1,0:T(8,128)(2,1)}, bf16[544,512]{1,0:T(8,128)(2,1)S(1)}, u32[]{:S(2)}) copy-start(bf16[544,512]{1,0:T(8,128)(2,1)S(1)} %collective-permute-done.3) | copy-start | bytes 1671172
  32.0 14.2 %collective-permute-start.4 = (bf16[544,512]{1,0:T(8,128)(2,1)}, bf16[544,512]{1,0:T(8,128)(2,1)}, u32[]{:S(2)}, u32[]{:S(2)}) collective-permute-start(bf16[544,512]{1,0:T(8,128)(2,1)} %fusion), channel_id=1, source_target_pairs={{0,8},{4,12},{1,9},{5,13},{2,10},{6,14},{3,11},{7,15}} | collective-permute-start | bytes 1671176 | tf_op jit(solution)/shard_map/ppermute | solution.py:277
  36.9 9.3 %collective-permute-start.7 = (bf16[544,512]{1,0:T(8,128)(2,1)}, bf16[544,512]{1,0:T(8,128)(2,1)}, u32[]{:S(2)}, u32[]{:S(2)}) collective-permute-start(bf16[544,512]{1,0:T(8,128)(2,1)} %fusion), channel_id=1, source_target_pairs={{28,20},{24,16},{29,21},{25,17},{30,22},{26,18},{31,23},{27,19}} | collective-permute-start | bytes 1671176 | tf_op jit(solution)/shard_map/ppermute | solution.py:278
  38.3 19.1 %collective-permute-start.2 = (bf16[544,512]{1,0:T(8,128)(2,1)S(1)}, bf16[544,512]{1,0:T(8,128)(2,1)}, u32[]{:S(2)}, u32[]{:S(2)}) collective-permute-start(bf16[544,512]{1,0:T(8,128)(2,1)S(1)} %get-tuple-element.21), channel_id=1, source_target_pairs={{0,4},{4,0},{8,12},{12,8},{16,20},{20,16},{24,28},{28,24},{1,5},{5... | collective-permute-start | bytes 1671176 | tf_op jit(solution)/shard_map/ppermute | solution.py:252
  49.3 13.6 %collective-permute-start.5 = (bf16[544,512]{1,0:T(8,128)(2,1)}, bf16[544,512]{1,0:T(8,128)(2,1)}, u32[]{:S(2)}, u32[]{:S(2)}) collective-permute-start(bf16[544,512]{1,0:T(8,128)(2,1)} %get-tuple-element.31), channel_id=1, source_target_pairs={{0,8},{4,12},{8,16},{12,20},{1,9},{5,13},{9,17},{13,21},{2,10},{6,... | collective-permute-start | bytes 1671176 | tf_op jit(solution)/shard_map/ppermute | solution.py:277
  54.4 8.4 %collective-permute-start.8 = (bf16[544,512]{1,0:T(8,128)(2,1)}, bf16[544,512]{1,0:T(8,128)(2,1)}, u32[]{:S(2)}, u32[]{:S(2)}) collective-permute-start(bf16[544,512]{1,0:T(8,128)(2,1)} %get-tuple-element.30), channel_id=1, source_target_pairs={{28,20},{24,16},{20,12},{16,8},{29,21},{25,17},{21,13},{17,9},{30,... | collective-permute-start | bytes 1671176 | tf_op jit(solution)/shard_map/ppermute | solution.py:278
  55.9 22.9 %collective-permute-start = (bf16[544,512]{1,0:T(8,128)(2,1)}, bf16[544,512]{1,0:T(8,128)(2,1)S(1)}, u32[]{:S(2)}, u32[]{:S(2)}) collective-permute-start(bf16[544,512]{1,0:T(8,128)(2,1)} %get-tuple-element.17), channel_id=1, source_target_pairs={{0,4},{4,0},{8,12},{12,8},{16,20},{20,16},{24,28},{28,24},{1,5},{5... | collective-permute-start | bytes 1671176 | tf_op jit(solution)/shard_map/ppermute | solution.py:252
  62.9 14.1 %copy-start.1 = (f32[1,25]{1,0:T(1,128)S(1)}, f32[1,25]{1,0:T(1,128)}, u32[]{:S(2)}) copy-start(f32[1,25]{1,0:T(1,128)} %det.1) | copy-start | bytes 304
  65.9 17.1 %collective-permute-start.6 = (bf16[544,512]{1,0:T(8,128)(2,1)}, bf16[544,512]{1,0:T(8,128)(2,1)S(1)}, u32[]{:S(2)}, u32[]{:S(2)}) collective-permute-start(bf16[544,512]{1,0:T(8,128)(2,1)} %get-tuple-element.33), channel_id=1, source_target_pairs={{0,8},{4,12},{8,16},{12,20},{16,24},{20,28},{1,9},{5,13},{9,17},{1... | collective-permute-start | bytes 1671176 | tf_op jit(solution)/shard_map/ppermute | solution.py:277
  75.0 12.0 %collective-permute-start.9 = (bf16[544,512]{1,0:T(8,128)(2,1)}, bf16[544,512]{1,0:T(8,128)(2,1)S(1)}, u32[]{:S(2)}, u32[]{:S(2)}) collective-permute-start(bf16[544,512]{1,0:T(8,128)(2,1)} %get-tuple-element.32), channel_id=1, source_target_pairs={{28,20},{24,16},{20,12},{16,8},{12,4},{8,0},{29,21},{25,17},{21,13... | collective-permute-start | bytes 1671176 | tf_op jit(solution)/shard_map/ppermute | solution.py:278
  90.6 2.0 %collective-permute-start.10 = (f32[2,128,512]{2,1,0:T(8,128)S(1)}, f32[2,128,512]{2,1,0:T(8,128)S(1)}, u32[]{:S(2)}, u32[]{:S(2)}) collective-permute-start(f32[2,128,512]{2,1,0:T(8,128)S(1)} %dynamic-slice_bitcast_fusion), channel_id=1, source_target_pairs={{0,1},{1,0},{2,3},{3,2},{4,5},{5,4},{6,7},{7,6},{8,9},{9,8},{10,11... | collective-permute-start | bytes 1572872 | tf_op jit(solution)/shard_map/ppermute | solution.py:286
  92.7 8.4 %collective-permute-start.11 = (f32[128,512]{1,0:T(8,128)S(1)}, f32[128,512]{1,0:T(8,128)S(1)}, u32[]{:S(2)}, u32[]{:S(2)}) collective-permute-start(f32[128,512]{1,0:T(8,128)S(1)} %dynamic-slice_bitcast_fusion.1), channel_id=1, source_target_pairs={{0,2},{1,3},{2,0},{3,1},{4,6},{5,7},{6,4},{7,5},{8,10},{9,11},{10,... | collective-permute-start | bytes 786440 | tf_op jit(solution)/shard_map/ppermute | solution.py:289

commit v2 on v1

v2 whole, which is shorter than its diff:
```python
import jax
import jax.numpy as jnp
import numpy as np
from jax import lax
from jax.experimental import pallas as pl
from jax.experimental.pallas import tpu as pltpu
from jax.sharding import PartitionSpec as P

TH = 2
TW = 2
DR = 12
CAP = 4
SLOTS = 4
PAD = 16
DIGITS = 16
UNIT = 512


def dest_table(outer):
    table = np.zeros((outer, outer), np.int32)
    for z in range(outer):
        def due(d):
            if d > z:
                return (outer - 1 + z - d, d == z ^ 1)
            if d < z:
                return (outer - 1 - z + d, d == z ^ 1)
            return (outer, 0)

        table[z] = sorted(range(outer), key=due)
    return table


def toeplitz(row):
    half = row.shape[1] // 2
    wide = jnp.broadcast_to(row, (half, 2 * half))
    skew = pltpu.roll(wide, 0, 1, stride=1, stride_axis=0)
    diag = skew[:, :half]
    off = skew[:, half:]
    i = lax.broadcasted_iota(jnp.int32, (half, half), 0)
    j = lax.broadcasted_iota(jnp.int32, (half, half), 1)
    upper = jnp.where(j < i, off, 0.0)
    lower = jnp.where(j > i, off, 0.0)
    top = jnp.concatenate([diag, upper], axis=1)
    bottom = jnp.concatenate([lower, diag], axis=1)
    return jnp.concatenate([top, bottom], axis=0).astype(jnp.bfloat16)


def make_lists(npatch, dest, count, index):
    def clear(p, carry):
        count[p] = 0
        for r in range(CAP):
            index[p * CAP + r] = -1
        return carry

    lax.fori_loop(0, npatch, clear, 0)

    def place(n, carry):
        p = dest[0, n]
        r = count[p]
        count[p] = r + 1
        index[p * CAP + r] = n
        return carry

    lax.fori_loop(0, dest.shape[1], place, 0)


def match_patch(p, q, k, slot, units, index, block, taps, acc, pay, edges, digits):
    edge = acc.shape[-1]
    ntaps = taps.shape[-1]
    side = TH * edge
    lane = lax.broadcasted_iota(jnp.int32, (8, 128), 1)
    acc[...] = jnp.zeros(acc.shape, acc.dtype)
    row = jnp.zeros((8, 128), jnp.float32)
    for r in range(CAP):
        found = index[p * CAP + r]
        n = jnp.maximum(found, 0)
        s = slot[0, n]
        unit = jnp.where(found >= 0, units[0, n], 0)
        w = unit.astype(jnp.float32) * (1.0 / UNIT)
        tap = taps[n].astype(jnp.float32)
        tap = jnp.concatenate([tap, jnp.zeros((2, edge - ntaps), jnp.float32)], axis=1)
        tap = pltpu.roll(tap, edge - ntaps // 2, 1)
        col = toeplitz(tap[0:1])
        half = jnp.dot(col, block(n, r), preferred_element_type=jnp.float32).astype(jnp.bfloat16)
        rowm = toeplitz(tap[1:2])
        matched = lax.dot_general(
            rowm, half, (((1,), (1,)), ((), ())), preferred_element_type=jnp.float32
        ).astype(jnp.bfloat16)
        acc[s] = acc[s] + w * matched.astype(jnp.float32)
        bit = lax.shift_right_logical(jnp.full((8, 128), unit), lane % DIGITS) & 1
        row = row + jnp.where(lane // DIGITS == s, bit, 0).astype(jnp.float32)
    digits[q] = row
    for s in range(SLOTS):
        top = (s % TW) * edge
        left = (s // TW) * edge
        pay[k, PAD + top : PAD + top + edge, left : left + edge] = acc[s].astype(jnp.bfloat16)
    edges[q, 0] = pay[k, PAD : 2 * PAD, :]
    edges[q, 1] = pay[k, side : side + PAD, :]


def add_halos(k, before, q, after, pay, edges, digits):
    rows, side = pay.shape[1:]
    first = lax.broadcasted_iota(jnp.int32, (PAD, side), 0) == 0
    blank = jnp.zeros((8, side - 3 * 128), jnp.float32)
    row = jnp.concatenate([digits[q], digits[before], digits[after], blank], axis=1)
    row = jnp.concatenate([row, row], axis=0)
    pay[k, :PAD, :] = jnp.where(first, row, edges[before, 1].astype(jnp.float32)).astype(jnp.bfloat16)
    pay[k, rows - PAD :, :] = edges[after, 0]


def first_kernel(
    npatch, dest_in, slot_in, weights_in, blocks_in, taps_in,
    s_a, k_a, s_b, k_b, own, edges, digits, dest, slot, units,
    acc, pay, blocks, taps, weights, wide, count, index, sems, sends,
):
    fetched = [
        pltpu.make_async_copy(dest_in, dest, sems.at[0]),
        pltpu.make_async_copy(weights_in, weights, sems.at[1]),
        pltpu.make_async_copy(slot_in, slot, sems.at[2]),
        pltpu.make_async_copy(taps_in, taps, sems.at[3]),
        pltpu.make_async_copy(blocks_in, blocks, sems.at[4]),
    ]
    for copy in fetched:
        copy.start()
    fetched[1].wait()
    wide[...] = (weights[...].astype(jnp.float32) * UNIT).astype(jnp.int32)
    convert = pltpu.make_async_copy(wide, units, sems.at[5])
    convert.start()
    me = lax.axis_index("patch")
    base = jnp.where(2 * (me // 2) < npatch // 2, npatch - 3, npatch - 1)
    fetched[0].wait()
    make_lists(npatch, dest, count, index)
    convert.wait()
    for copy in fetched[2:]:
        copy.wait()

    rows, side = pay.shape[1:]
    half = rows // 2
    copies = []

    def send(source, out):
        copies.append(pltpu.make_async_copy(source, out, sends.at[len(copies)]))
        copies[-1].start()

    def either_way(first_out, second_out, q, part):
        source = pay.at[q, part * half : (part + 1) * half]
        copy = [pltpu.make_async_copy(source, out, sends.at[len(copies)]) for out in (first_out, second_out)]
        copies.append(copy[0])
        goes = lax.rem(me, 2) == 2 - q
        pl.when(goes)(copy[0].start)
        pl.when(jnp.logical_not(goes))(copy[1].start)

    for q in range(4):
        p = lax.rem(base + q, npatch)
        match_patch(p, q, q, slot, units, index, lambda n, r: blocks[n], taps, acc, pay, edges, digits)
        if q > 1:
            add_halos(q - 1, q - 2, q - 1, q, pay, edges, digits)
            either_way(s_a, k_a, q - 1, 0)
            either_way(s_b, k_b, q - 1, 1)
        if q % 3 == 0:
            send(pay.at[q, PAD : PAD + side], own.at[q // 3])
    for copy in copies:
        copy.wait()


def make_turns(outer):
    last = outer - 1
    turns = [[(0, 0)], [(0, 1)], [(1, 0)]]
    turns += [[(s, 0), (s - 1, 1)] for s in range(2, last)]
    return turns + [[(last - 1, 1)], [(last, 0)], [(last, 1)]]


def rest_kernel(npatch, dest, slot, units, order, blocks_in, taps, own, edges0, digits0, *rest):
    turns = make_turns(npatch // 2)[2:]
    outs = rest[: len(turns) + npatch - 2]
    acc, pay, blocks, edges, digits, count, index, place, sems, sends = rest[len(turns) + npatch - 2 :]
    sent = {part: (turn, i) for turn, parts in enumerate(turns) for i, part in enumerate(parts)}
    rows, side = pay.shape[1:]
    half = rows // 2
    base = (order[0] // 2) * 2 + npatch - 1
    fetch = pltpu.make_async_copy(blocks_in, blocks, sems.at[2])
    fetch.start()

    def put(k, carry):
        place[order[k]] = k - 2
        return carry

    lax.fori_loop(0, npatch, put, 0)
    given = []
    for j in range(2):
        k = place[lax.rem(base + 3 * j, npatch)]
        given.append(pltpu.make_async_copy(own.at[j], pay.at[k, PAD : PAD + side], sems.at[j]))
        given[-1].start()
    make_lists(npatch, dest, count, index)
    for q in range(4):
        edges[q] = edges0[q]
        digits[q] = digits0[q]

    def copies(k):
        result = []
        for j in range(2):
            if k % 2:
                out = outs[len(turns) + k - 1 + j]
            else:
                turn, i = sent[k // 2 + 1, j]
                out = outs[turn].at[i * half : (i + 1) * half]
            result.append(pltpu.make_async_copy(pay.at[k, j * half : (j + 1) * half], out, sends.at[2 * k + j]))
        return result

    def send(q):
        mine = place[lax.rem(base + q, npatch)]
        add_halos(mine, lax.rem(q + npatch - 1, npatch), q, lax.rem(q + 1, npatch), pay, edges, digits)
        for k in range(npatch - 2):

            @pl.when(mine == k)
            def _():
                for copy in copies(k):
                    copy.start()

    given[0].wait()
    given[1].wait()
    fetch.wait()

    def patch(q, carry):
        p = lax.rem(base + q, npatch)
        match_patch(p, q, place[p], slot, units, index, lambda n, r: blocks[n], taps, acc, pay, edges, digits)
        send(q - 1)
        return carry

    lax.fori_loop(4, npatch, patch, 0, unroll=2)
    send(npatch - 1)
    send(0)
    for k in range(npatch - 2):
        for copy in copies(k):
            copy.wait()


def match_blocks(dest, slot, weights, orders, blocks, taps):
    npatch, number = orders.shape[0], blocks.shape[0]
    edge = blocks.shape[-1]
    side = TH * edge
    rows = side + 2 * PAD
    smem = pl.BlockSpec(memory_space=pltpu.SMEM)
    vmem = pl.BlockSpec(memory_space=pltpu.VMEM)
    hbm = pl.BlockSpec(memory_space=pltpu.HBM)
    half = jax.ShapeDtypeStruct((rows // 2, side), jnp.bfloat16)
    acc = pltpu.VMEM((SLOTS, edge, edge), jnp.float32)
    params = pltpu.CompilerParams(vmem_limit_bytes=64 * 1024 * 1024)
    count = pltpu.SMEM((npatch,), jnp.int32)
    index = pltpu.SMEM((npatch * CAP,), jnp.int32)
    s_a, k_a, s_b, k_b, own, edges, digits, dest, slot, units = pl.pallas_call(
        lambda *refs: first_kernel(npatch, *refs),
        out_shape=[half] * 4
        + [
            jax.ShapeDtypeStruct((2, side, side), jnp.bfloat16),
            jax.ShapeDtypeStruct((4, 2, PAD, side), jnp.bfloat16),
            jax.ShapeDtypeStruct((4, 8, 128), jnp.float32),
        ]
        + [jax.ShapeDtypeStruct((1, number), jnp.int32)] * 3,
        in_specs=[hbm] * 5,
        out_specs=[hbm] * 5 + [vmem] * 2 + [smem] * 3,
        scratch_shapes=[
            acc,
            pltpu.VMEM((4, rows, side), jnp.bfloat16),
            pltpu.VMEM(blocks.shape, jnp.bfloat16),
            pltpu.VMEM(taps.shape, jnp.bfloat16),
            pltpu.VMEM((1, number), jnp.bfloat16),
            pltpu.VMEM((1, number), jnp.int32),
            count,
            index,
            pltpu.SemaphoreType.DMA((6,)),
            pltpu.SemaphoreType.DMA((6,)),
        ],
        compiler_params=params,
        name="match_first",
    )(dest, slot, weights, blocks, taps)
    me, _ = lax.optimization_barrier((lax.axis_index("patch"), s_a))
    order = lax.dynamic_index_in_dim(jnp.asarray(orders), me, 0, keepdims=False)
    turns = make_turns(npatch // 2)
    outs = pl.pallas_call(
        lambda *refs: rest_kernel(npatch, *refs),
        out_shape=[jax.ShapeDtypeStruct((rows // 2 * len(turn), side), jnp.bfloat16) for turn in turns[2:]]
        + [half] * (npatch - 2),
        in_specs=[smem] * 4 + [hbm, vmem, hbm, vmem, vmem],
        out_specs=[hbm] * (len(turns) - 2 + npatch - 2),
        scratch_shapes=[
            acc,
            pltpu.VMEM((npatch - 2, rows, side), jnp.bfloat16),
            pltpu.VMEM(blocks.shape, jnp.bfloat16),
            pltpu.VMEM((npatch, 2, PAD, side), jnp.bfloat16),
            pltpu.VMEM((npatch, 8, 128), jnp.float32),
            count,
            index,
            pltpu.SMEM((npatch,), jnp.int32),
            pltpu.SemaphoreType.DMA((3,)),
            pltpu.SemaphoreType.DMA((2 * (npatch - 2),)),
        ],
        compiler_params=params,
        cost_estimate=pl.CostEstimate(flops=2_000_000_000, bytes_accessed=8_000_000, transcendentals=0),
        name="match_rest",
    )(dest, slot, units, order, blocks, taps, own, edges, digits)
    sends = [s_a, s_b] + list(outs[: len(turns) - 2])
    kept = outs[len(turns) - 2 :]
    return sends, [(k_a, k_b)] + [(kept[2 * k], kept[2 * k + 1]) for k in range(npatch // 2 - 1)]


def split(value):
    high = value.astype(jnp.bfloat16)
    return high, (value - high.astype(jnp.float32)).astype(jnp.bfloat16)


def dot3(ah, al, bh, bl, dims):
    def one(a, b):
        return lax.dot_general(a, b, (dims, ((), ())), preferred_element_type=jnp.float32)

    return one(ah, bh) + (one(ah, bl) + one(al, bh))


def chi_rows(place, rowh, rowl, ch, cl, noise):
    rows = pl.ds(pl.multiple_of(place * 128, 128), 128)
    row_pass = dot3(rowh[rows, :], rowl[rows, :], ch, cl, ((1,), (1,)))
    return row_pass * row_pass * (1.0 / noise[0])


def total(x0, x1, x2, x3):
    f32 = jnp.float32
    return x0[...].astype(f32) + x1[...].astype(f32) + (x2[...].astype(f32) + x3[...].astype(f32))


def tail_left(a0, a1, a2, a3, colh, coll, normed, part, factor):
    f32 = jnp.float32
    half, side = a0.shape
    edge = side // TH
    left = total(a0, a1, a2, a3)
    lane = lax.broadcasted_iota(jnp.int32, (1, side), 1)
    power = lax.shift_left(jnp.ones((1, side), jnp.int32), lane % DIGITS).astype(f32) * (1.0 / UNIT)
    value = left[0:1, :] * power

    def scale(group, s):
        here = (lane >= group * 128 + s * DIGITS) & (lane < group * 128 + (s + 1) * DIGITS)
        weight_sum = jnp.sum(jnp.where(here, value, 0.0), axis=1, keepdims=True)
        return jnp.broadcast_to(1.0 / jnp.maximum(weight_sum, 1.0), (1, edge))

    def factors(group, column):
        return jnp.concatenate([scale(group, r * TW + column) for r in range(TH)], axis=1)

    left = jnp.concatenate([left[:PAD] * factors(1, TW - 1), left[PAD:] * factors(0, 0)], axis=0)
    normed[...] = left[PAD:]
    high, low = split(left)
    part[...] = dot3(colh[:, :half], coll[:, :half], high, low, ((1,), (0,)))
    factor[0] = jnp.broadcast_to(factors(0, 1), (8, side))
    factor[1] = jnp.broadcast_to(factors(2, 0), (8, side))


def tail_right(
    b0, b1, b2, b3, factor, part, noise, band, colh, coll, rowh, rowl, normed, give, stay
):
    half, side = b0.shape
    edge = side // TH
    right = total(b0, b1, b2, b3)
    right = jnp.concatenate([right[:edge] * factor[0, 0:1], right[edge:] * factor[1, 0:1]], axis=0)
    normed[...] = right[:edge]
    high, low = split(right)
    ch, cl = split(part[...] + dot3(colh[:, half:], coll[:, half:], high, low, ((1,), (0,))))
    for j, place in enumerate((band[0], band[0] ^ 2)):
        give[j] = chi_rows(place ^ 1, rowh, rowl, ch, cl, noise)
        stay[j] = chi_rows(place, rowh, rowl, ch, cl, noise)


def tail_image(left, right, image):
    edge = left.shape[0]
    image[:, :edge] = left[...].T
    image[:, edge:] = right[...].T


def tables_kernel(det, colh, coll, rowh, rowl):
    for high, low, start in ((colh, coll, DR - PAD), (rowh, rowl, DR)):
        offsets = (
            lax.broadcasted_iota(jnp.int32, high.shape, 1)
            - lax.broadcasted_iota(jnp.int32, high.shape, 0)
            + start
        )
        table = jnp.zeros(high.shape, jnp.float32)
        for tap in range(det.shape[1]):
            table = jnp.where(offsets == tap, det[0, tap], table)
        high[...], low[...] = split(table)


def filter_tables(det, rows, side):
    return pl.pallas_call(
        tables_kernel,
        out_shape=[jax.ShapeDtypeStruct(s, jnp.bfloat16) for s in [(side, rows)] * 2 + [(side, side)] * 2],
        in_specs=[pl.BlockSpec(memory_space=pltpu.SMEM)],
        out_specs=[pl.BlockSpec(memory_space=pltpu.VMEM)] * 4,
        compiler_params=pltpu.CompilerParams(vmem_limit_bytes=40 * 1024 * 1024),
        cost_estimate=pl.CostEstimate(flops=20_000_000, bytes_accessed=2_000_000, transcendentals=0),
        name="tables",
    )(det)


def finish(left, right, noise, det):
    rows, side = left[0].shape[0] * 2, left[0].shape[1]
    f32, bf16 = jnp.float32, jnp.bfloat16
    colh, coll, rowh, rowl = filter_tables(det, rows, side)
    band = lax.axis_index("band")
    where = band.reshape(1).astype(jnp.int32)
    smem = pl.BlockSpec(memory_space=pltpu.SMEM)
    vmem = pl.BlockSpec(memory_space=pltpu.VMEM)
    params = pltpu.CompilerParams(vmem_limit_bytes=40 * 1024 * 1024)
    quarters = jax.ShapeDtypeStruct((2, side // 4, side), f32)
    whole = jax.ShapeDtypeStruct((side, side), f32)
    tile = jax.ShapeDtypeStruct((side // TW, side), f32)
    normed_left, part, factor = pl.pallas_call(
        tail_left,
        out_shape=[tile, whole, jax.ShapeDtypeStruct((2, 8, side), f32)],
        in_specs=[vmem] * 6,
        out_specs=[vmem] * 3,
        compiler_params=params,
        cost_estimate=pl.CostEstimate(flops=500_000_000, bytes_accessed=4_000_000, transcendentals=0),
        name="tail_left",
    )(*left, colh, coll)
    normed_right, give, stay = pl.pallas_call(
        tail_right,
        out_shape=[tile, quarters, quarters],
        in_specs=[vmem] * 6 + [smem] * 2 + [vmem] * 4,
        out_specs=[vmem] * 3,
        compiler_params=params,
        name="tail_right",
    )(*right, factor, part, noise, where, colh, coll, rowh, rowl)
    pair = stay + lax.ppermute(give, "band", [(i, i ^ 1) for i in range(4)])
    beyond = lax.ppermute(pair[1].astype(bf16), "band", [(i, i ^ 2) for i in range(4)])
    normed_right, _ = lax.optimization_barrier((normed_right, pair))
    image = pl.pallas_call(
        tail_image,
        out_shape=whole,
        in_specs=[vmem] * 2,
        out_specs=vmem,
        compiler_params=params,
        cost_estimate=pl.CostEstimate(flops=0, bytes_accessed=2_000_000, transcendentals=0),
        name="tail_image",
    )(normed_left, normed_right)
    return image, pair[0] + beyond.astype(f32)


def either(flags):
    result = flags[0]
    for flag in flags[1:]:
        result = result | flag
    return result


def local(blocks, dest_patch, dest_slot, weights, psf_taps, det_taps, noise_var):
    f32, bf16 = jnp.float32, jnp.bfloat16
    npatch = lax.axis_size("patch")
    outer = npatch // 2
    me = lax.axis_index("patch")
    z = me // 2
    table = dest_table(outer)
    where_is = np.argsort(table, axis=1)
    order = np.zeros((npatch, npatch), np.int32)
    for i in range(npatch):
        for s in range(outer):
            order[i, 2 * s] = table[i // 2, s] * 2 + 1 - i % 2
            order[i, 2 * s + 1] = table[i // 2, s] * 2 + i % 2
    sends, kept = match_blocks(dest_patch, dest_slot, weights, order, blocks[0], psf_taps[0])
    last = outer - 1
    nband = lax.axis_size("band")
    across = [(i, i ^ 1) for i in range(npatch)]
    even = [(i, i ^ 2) for i in range(npatch)]
    odd = []
    for i in range(npatch):
        q = i // 2
        to = q + 1 if q % 2 else q - 1
        for j in range(nband):
            if 0 <= to < outer:
                odd.append((i * nband + j, (2 * to + i % 2) * nband + j))
            else:
                odd.append((i * nband + j, i * nband + (j ^ 1)))
    came = {}
    got = []
    for i, (parts, send) in enumerate(zip(make_turns(outer), sends, strict=True)):
        if i > 2:
            send, _ = lax.optimization_barrier((send, got[i - 2] if i > 3 else got[0]))
        with jax.named_scope(f"across_turn_{i}_of"):
            got.append(lax.ppermute(send, "patch", across))
        for j, part in enumerate(parts):
            rows = got[-1].shape[0] // len(parts)
            came[part] = lax.slice_in_dim(got[-1], j * rows, (j + 1) * rows)

    def combined(s, c):
        return kept[s][c].astype(f32) + came[s, c].astype(f32)

    def chosen(places, c):
        values = sorted(set(places.values()))
        result = combined(values[-1], c)
        for v in values[:-1]:
            result = jnp.where(either([z == q for q, s in places.items() if s == v]), combined(v, c), result)
        return result

    def step(t, parity, c):
        places = {}
        for q in range(outer):
            rising = q % 2 == parity
            hops = q if rising else last - q
            d = last - t + q if rising else t - hops
            if hops <= t and 0 <= d < outer and d != q:
                places[q] = int(where_is[q][d])
        return chosen(places, c)

    def masked(value, ends):
        return jnp.where(either([z == q for q in ends]), 0.0, value.astype(f32))

    evens, odds = [None, None], [None, None]
    for t in range(last):
        for c in range(2):
            send = step(t, 0, c)
            if t > 1:
                send = send + masked(odds[c], (0, last))
            send_odd = step(t, 1, c) + evens[c].astype(f32) if t else None
            side = "left" if c == 0 else "right"
            with jax.named_scope(f"even_step_{t}_{side}"):
                evens[c] = lax.ppermute(send.astype(bf16), "patch", even)
            if t == 1 and c == 1:
                det_taps, _ = lax.optimization_barrier((det_taps, evens[c]))
            if t:
                with jax.named_scope(f"odd_step_{t}_{side}"):
                    odds[c] = lax.ppermute(send_odd.astype(bf16), ("patch", "band"), odd)
    for c in range(2):
        odds[c] = masked(odds[c], (0, last)).astype(bf16)
    ends = [(kept[last][c], came[last, c], evens[c], odds[c]) for c in range(2)]
    image, chi = finish(*ends, noise_var, det_taps)
    return image[None], chi


def solution(mesh):
    in_specs = (
        P("band", "patch", None, None),
        P("band", "patch"),
        P("band", "patch"),
        P("band", "patch"),
        P("band", "patch", None, None),
        P("band", None),
        P("band"),
    )
    out_specs = (P("band", None, "patch"), P("band", "patch"))
    return jax.shard_map(local, mesh=mesh, in_specs=in_specs, out_specs=out_specs, check_vma=False)
```

time: 102 us -> 76 us (0.75); the launches traced: 102 us -> 74.8 us
  waiting for transfers between devices: 42.2 us -> 19.2 us
  starting transfers between devices: 31.1 us -> 23.5 us
  Pallas kernels: 16.4 us -> 21.4 us
  other arithmetic: 9.24 us -> 7.85 us
    ppermute x12 -> x19, waiting for transfers between devices: 42.2 us -> 19.2 us  [the longest x7 12.3 us: local(): got.append(lax.ppermute(send, 'patch', across))]
    ppermute x12 -> x19, starting transfers between devices: 31.1 us -> 23.5 us  [the longest x6 11 us: local(): evens[c] = lax.ppermute(send.astype(bf16), 'patch', even)]
    pallas_call x2 -> x5, Pallas kernels: 14.6 us -> 19.6 us  [the longest x1 7.54 us: match_blocks(): pl.pallas_call(lambda *refs: rest_kernel(npatch, *refs), out_shape=[jax.S...]
    convert_element_type x4 -> x11, other arithmetic: 7.74 us -> 7.04 us  [the longest x5 4.39 us: local(): evens[c] = lax.ppermute(send.astype(bf16), 'patch', even)]
  transfers between devices with their start and end apart: 12 -> 19, of which waited for: 8 -> 8; matrix products, arithmetic and copies ran while one was open for 7% -> 11% of each run, Pallas kernels for 2% -> 16%
where the time goes in v2:
time: 76 us; the launch traced here: 74.8 us
  starting transfers between devices  23.5 us (31%)
  Pallas kernels  21.4 us (28%)
  waiting for transfers between devices  19.2 us (25%)
  other arithmetic  7.85 us (10%)
  between operations  1.54 us (2%)
  local copies, waits for them, and re-layouts  1.26 us (2%)
    ppermute x7, waiting for transfers between devices, local(): got.append(lax.ppermute(send, 'patch', across))  12.3 us
    ppermute x6, starting transfers between devices, local(): evens[c] = lax.ppermute(send.astype(bf16), 'patch', even)  11 us
    ppermute x7, starting transfers between devices, local(): got.append(lax.ppermute(send, 'patch', across))  10.2 us
    pallas_call x1, Pallas kernels, match_blocks(): pl.pallas_call(lambda *refs: rest_kernel(npatch, *refs), out_shape=[jax.S...  7.54 us
    pallas_call x1, Pallas kernels, match_blocks(): pl.pallas_call(lambda *refs: first_kernel(npatch, *refs), out_shape=[half...  6.42 us
    convert_element_type x5, other arithmetic, local(): evens[c] = lax.ppermute(send.astype(bf16), 'patch', even)  4.39 us
    pallas_call x1, Pallas kernels, finish(): pl.pallas_call(tail_right, out_shape=[tile, quarters, quarters], in_specs...  3.22 us
    ppermute x1, waiting for transfers between devices, finish(): lax.ppermute(pair[1].astype(bf16), 'band', [(i, i ^ 2) for i in range(4)])  2.73 us
  transfers between devices with their start and end apart: 19, of which 8 were waited for; matrix products, arithmetic and copies ran while one was open for 11% of the time, Pallas kernels for 16%

profile of v2, /device:TPU:0, one launch (start us, length us, event | category | flops | bytes accessed | tf_op | source)
XLA Modules:
  0.0 74.8 jit_solution(17836978095757115536)
XLA Ops:
  0.6 6.4 %match_first.1 = (bf16[272,512]{1,0:T(8,128)(2,1)}, bf16[272,512]{1,0:T(8,128)(2,1)}, bf16[272,512]{1,0:T(8,128)(2,1)}, bf16[272,512]{1,0:T(8,128)(2,1)}, bf16[2...) custom-call(s32[1,32]{1,0:T(1,128)} %refs_0_.1, ...), custom_call_target="tpu_custom_call" | custom-call | tf_op jit(solution)/shard_map/match_first/pallas_call | solution.py:251
  7.1 3.0 %collective-permute-start.12 = (bf16[272,512]{1,0:T(8,128)(2,1)}, bf16[272,512]{1,0:T(8,128)(2,1)}, u32[]{:S(2)}, u32[]{:S(2)}) collective-permute-start(bf16[272,512]{1,0:T(8,128)(2,1)} %get-tuple-element.69), channel_id=1, source_target_pairs={{0,4},{4,0},{8,12},{12,8},{16,20},{20,16},{24,28},{28,24},{1,5},{5... | collective-permute-start | bytes 835592 | tf_op jit(solution)/shard_map/across_turn_1_of/ppermute | solution.py:485
  10.1 0.1 collective-permute-start
  10.2 1.2 %dynamic-slice_bitcast_fusion.refs_3_ = s32[8]{0:T(128)} fusion(s32[8,8]{1,0:T(8,128)} %constant.35.clone, s32[]{:T(128)S(6)} %select_n.29), kind=kLoop, calls=%fused_computation.20 | loop fusion | bytes 68 | tf_op jit(solution)/shard_map/jit(dynamic_index_in_dim)/squeeze | solution.py:278
  11.4 7.5 %match_rest.1 = (bf16[272,512]{1,0:T(8,128)(2,1)}, bf16[544,512]{1,0:T(8,128)(2,1)}, bf16[272,512]{1,0:T(8,128)(2,1)}, bf16[272,512]{1,0:T(8,128)(2,1)}, bf16[27...) custom-call(s32[1,32]{1,0:T(1,128)} %get-tuple-element.40.refs_0_, ...), custom_call_target="tpu_custom_call" | custom-call | flops 2000000000 | bytes 8000000 | tf_op jit(solution)/shard_map/match_rest/pallas_call | solution.py:280
  19.0 2.0 %collective-permute-start.6 = (bf16[272,512]{1,0:T(8,128)(2,1)}, bf16[272,512]{1,0:T(8,128)(2,1)S(1)}, u32[]{:S(2)}, u32[]{:S(2)}) collective-permute-start(bf16[272,512]{1,0:T(8,128)(2,1)} %get-tuple-element.56), channel_id=1, source_target_pairs={{0,4},{4,0},{8,12},{12,8},{16,20},{20,16},{24,28},{28,24},{1,5},{5... | collective-permute-start | bytes 835592 | tf_op jit(solution)/shard_map/across_turn_2_of/ppermute | solution.py:485
  21.6 2.2 %collective-permute-done = bf16[272,512]{1,0:T(8,128)(2,1)} collective-permute-done((bf16[272,512]{1,0:T(8,128)(2,1)}, bf16[272,512]{1,0:T(8,128)(2,1)}, u32[]{:S(2)}, u32[]{:S(2)}) %collective-permute-start) | collective-permute-done | bytes 278560 | tf_op jit(solution)/shard_map/across_turn_0_of/ppermute | solution.py:485
  23.9 1.1 %fusion = bf16[272,512]{1,0:T(8,128)(2,1)S(1)} fusion(bf16[272,512]{1,0:T(8,128)(2,1)} %collective-permute-done, bf16[272,512]{1,0:T(8,128)(2,1)} %get-tuple-element.54), kind=kLoop, calls=%fused_computation.12 | loop fusion | flops 557056 | bytes 835584 | tf_op jit(solution)/shard_map/even_step_0_left/convert_element_type | solution.py:522
  25.0 2.2 %collective-permute-start.3 = (bf16[272,512]{1,0:T(8,128)(2,1)S(1)}, bf16[272,512]{1,0:T(8,128)(2,1)S(1)}, u32[]{:S(2)}, u32[]{:S(2)}) collective-permute-start(bf16[272,512]{1,0:T(8,128)(2,1)S(1)} %fusion), channel_id=1, source_target_pairs={{0,8},{4,12},{8,0},{12,4},{16,24},{20,28},{24,16},{28,20},{1,9},{5... | collective-permute-start | bytes 835592 | tf_op jit(solution)/shard_map/even_step_0_left/ppermute | solution.py:522
  27.2 1.5 %collective-permute-start.1 = (bf16[544,512]{1,0:T(8,128)(2,1)}, bf16[544,512]{1,0:T(8,128)(2,1)S(1)}, u32[]{:S(2)}, u32[]{:S(2)}) collective-permute-start(bf16[544,512]{1,0:T(8,128)(2,1)} %get-tuple-element.51), channel_id=1, source_target_pairs={{0,4},{4,0},{8,12},{12,8},{16,20},{20,16},{24,28},{28,24},{1,5},{5... | collective-permute-start | bytes 1671176 | tf_op jit(solution)/shard_map/across_turn_3_of/ppermute | solution.py:485
  28.7 0.0 collective-permute-done.12
  28.7 1.1 %fusion.3 = bf16[272,512]{1,0:T(8,128)(2,1)S(1)} fusion(bf16[272,512]{1,0:T(8,128)(2,1)} %collective-permute-done.12, bf16[272,512]{1,0:T(8,128)(2,1)} %get-tuple-element.68), kind=kLoop, calls=%fused_computation.15 | loop fusion | flops 557056 | bytes 835584 | tf_op jit(solution)/shard_map/even_step_0_right/convert_element_type | solution.py:522
  29.8 0.5 collective-permute-start.13
  30.3 0.0 collective-permute-done.6
  30.3 1.0 %fusion.1 = bf16[272,512]{1,0:T(8,128)(2,1)S(1)} fusion(bf16[272,512]{1,0:T(8,128)(2,1)S(1)} %collective-permute-done.6, bf16[272,512]{1,0:T(8,128)(2,1)} %get-tuple-element.55), kind=kLoop, calls=%fused_computation.13 | loop fusion | flops 557056 | bytes 835584 | tf_op jit(solution)/shard_map/even_step_1_left/convert_element_type | solution.py:522
  31.4 0.0 copy-start.2
  31.4 1.6 %collective-permute-start.7 = (bf16[272,512]{1,0:T(8,128)(2,1)S(1)}, bf16[272,512]{1,0:T(8,128)(2,1)S(1)}, u32[]{:S(2)}, u32[]{:S(2)}) collective-permute-start(bf16[272,512]{1,0:T(8,128)(2,1)S(1)} %fusion.1), channel_id=1, source_target_pairs={{0,8},{4,12},{8,0},{12,4},{16,24},{20,28},{24,16},{28,20},{1,9},{5... | collective-permute-start | bytes 835592 | tf_op jit(solution)/shard_map/even_step_1_left/ppermute | solution.py:522
  33.0 1.5 %collective-permute-start.10 = (bf16[272,512]{1,0:T(8,128)(2,1)}, bf16[272,512]{1,0:T(8,128)(2,1)S(1)}, u32[]{:S(2)}, u32[]{:S(2)}) collective-permute-start(bf16[272,512]{1,0:T(8,128)(2,1)} %get-tuple-element.65), channel_id=1, source_target_pairs={{0,4},{4,0},{8,12},{12,8},{16,20},{20,16},{24,28},{28,24},{1,5},{5... | collective-permute-start | bytes 835592 | tf_op jit(solution)/shard_map/across_turn_4_of/ppermute | solution.py:485
  34.5 1.1 %add_convert_fusion.5 = bf16[272,512]{1,0:T(8,128)(2,1)S(1)} fusion(bf16[272,512]{1,0:T(8,128)(2,1)S(1)} %collective-permute-done.3, bf16[272,512]{1,0:T(8,128)(2,1)} %collective-permute-done, bf16[272,512]{1,0:T(8,128)(2,1)} %get-tuple-element.54), kind=kLoop, calls=%fused_computation.10 | loop fusion | flops 835584 | bytes 1114112 | tf_op jit(solution)/shard_map/odd_step_1_left/convert_element_type | solution.py:527
  35.6 0.1 collective-permute-start.4
  35.7 7.2 %collective-permute-done.1 = bf16[544,512]{1,0:T(8,128)(2,1)S(1)} collective-permute-done((bf16[544,512]{1,0:T(8,128)(2,1)}, bf16[544,512]{1,0:T(8,128)(2,1)S(1)}, u32[]{:S(2)}, u32[]{:S(2)}) %collective-permute-start.1) | collective-permute-done | bytes 557088 | tf_op jit(solution)/shard_map/across_turn_3_of/ppermute | solution.py:485
  42.9 1.0 %fusion.2 = bf16[272,512]{1,0:T(8,128)(2,1)S(1)} fusion(bf16[272,512]{1,0:T(8,128)(2,1)} %get-tuple-element.57, bf16[544,512]{1,0:T(8,128)(2,1)S(1)} %collective-permute-done.1), kind=kLoop, calls=%fused_computation.14 | loop fusion | flops 557056 | bytes 835584 | tf_op jit(solution)/shard_map/even_step_1_right/convert_element_type | solution.py:522
  44.0 0.9 %collective-permute-start.9 = (bf16[272,512]{1,0:T(8,128)(2,1)S(1)}, bf16[272,512]{1,0:T(8,128)(2,1)S(1)}, u32[]{:S(2)}, u32[]{:S(2)}) collective-permute-start(bf16[272,512]{1,0:T(8,128)(2,1)S(1)} %fusion.2), channel_id=1, source_target_pairs={{0,8},{4,12},{8,0},{12,4},{16,24},{20,28},{24,16},{28,20},{1,9},{5... | collective-permute-start | bytes 835592 | tf_op jit(solution)/shard_map/even_step_1_right/ppermute | solution.py:522
  44.9 1.1 %add_convert_fusion.2 = bf16[272,512]{1,0:T(8,128)(2,1)S(1)} fusion(bf16[272,512]{1,0:T(8,128)(2,1)S(1)} %collective-permute-done.13, bf16[272,512]{1,0:T(8,128)(2,1)} %collective-permute-done.12, bf16[272,512]{1,0:T(8,128)(2,1)S(1)} %copy-done.4), kind=kLoop, calls=%fused_computation.3 | loop fusion | flops 835584 | bytes 1114112 | tf_op jit(solution)/shard_map/odd_step_1_right/convert_element_type | solution.py:527
  45.9 0.1 collective-permute-start.14
  46.0 0.1 add_convert_fusion.3
  46.2 0.5 collective-permute-start.8
  46.7 0.1 collective-permute-done.10
  46.8 1.7 %collective-permute-start.11 = (bf16[272,512]{1,0:T(8,128)(2,1)S(1)}, bf16[272,512]{1,0:T(8,128)(2,1)S(1)}, u32[]{:S(2)}, u32[]{:S(2)}) collective-permute-start(bf16[272,512]{1,0:T(8,128)(2,1)S(1)} %copy-done.8), channel_id=1, source_target_pairs={{0,4},{4,0},{8,12},{12,8},{16,20},{20,16},{24,28},{28,24},{1,5},{5... | collective-permute-start | bytes 835592 | tf_op jit(solution)/shard_map/across_turn_6_of/ppermute | solution.py:485
  48.6 0.3 collective-permute-start.2
  48.8 1.7 %collective-permute-done.9 = bf16[272,512]{1,0:T(8,128)(2,1)S(1)} collective-permute-done((bf16[272,512]{1,0:T(8,128)(2,1)S(1)}, bf16[272,512]{1,0:T(8,128)(2,1)S(1)}, u32[]{:S(2)}, u32[]{:S(2)}) %collective-permute-start.9) | collective-permute-done | bytes 278560 | tf_op jit(solution)/shard_map/even_step_1_right/ppermute | solution.py:522
  50.6 0.2 add_convert_fusion
  50.8 1.0 %collective-permute-start.5 = (bf16[272,512]{1,0:T(8,128)(2,1)S(1)}, bf16[272,512]{1,0:T(8,128)(2,1)S(1)}, u32[]{:S(2)}, u32[]{:S(2)}) collective-permute-start(bf16[272,512]{1,0:T(8,128)(2,1)S(1)} %get-tuple-element.79), channel_id=1, source_target_pairs={{0,8},{4,12},{8,0},{12,4},{16,24},{20,28},{24,16},{28,20},{1,9},{5... | collective-permute-start | bytes 835592 | tf_op jit(solution)/shard_map/even_step_2_left/ppermute | solution.py:522
  51.8 0.1 add_convert_fusion.1
  51.9 4.8 %collective-permute-start.15 = (bf16[272,512]{1,0:T(8,128)(2,1)S(1)}, bf16[272,512]{1,0:T(8,128)(2,1)S(1)}, u32[]{:S(2)}, u32[]{:S(2)}) collective-permute-start(bf16[272,512]{1,0:T(8,128)(2,1)S(1)} %add_convert_fusion.1), channel_id=1, source_target_pairs={{0,8},{4,12},{8,0},{12,4},{16,24},{20,28},{24,16},{28,20},{1,9},{5... | collective-permute-start | bytes 835592 | tf_op jit(solution)/shard_map/even_step_2_right/ppermute | solution.py:522
  56.8 1.8 %tables.1 = (bf16[512,544]{1,0:T(8,128)(2,1)S(1)}, bf16[512,544]{1,0:T(8,128)(2,1)S(1)}, bf16[512,512]{1,0:T(8,128)(2,1)S(1)}, bf16[512,512]{1,0:T(8,128)(2,1)S(1)}) custom-call(f32[1,25]{1,0:T(1,128)S(1)} %copy-done.2), custom_call_target="tpu_custom_call" | custom-call | flops 20000000 | bytes 2000000 | tf_op jit(solution)/shard_map/tables/pallas_call | solution.py:390
  58.6 2.7 %collective-permute-done.2.a1 = bf16[272,512]{1,0:T(8,128)(2,1)S(1)} collective-permute-done((bf16[272,512]{1,0:T(8,128)(2,1)S(1)}, bf16[272,512]{1,0:T(8,128)(2,1)S(1)}, u32[]{:S(2)}, u32[]{:S(2)}) %collective-permute-start.2) | collective-permute-done | bytes 278560 | tf_op jit(solution)/shard_map/across_turn_5_of/ppermute | solution.py:485
  61.3 1.1 %tail_left.1 = (f32[256,512]{1,0:T(8,128)S(1)}, f32[512,512]{1,0:T(8,128)S(1)}, f32[2,8,512]{2,1,0:T(8,128)S(1)}) custom-call(bf16[272,512]{1,0:T(8,128)(2,1)S(1)} %copy-done.1, bf16[272,512]{1,0:T(8,128)(2,1)S(1)} %collective-permute-done.2.a1, bf16[272,512]{1,0:T(8,128)(2,1)S(1)} %collective-permute-done.5.a2, ...), custom_call_target="tpu_custom_call" | custom-call | flops 500000000 | bytes 4000000 | tf_op jit(solution)/shard_map/tail_left/pallas_call | solution.py:413
  62.5 0.1 select_convert_fusion.b3
  62.6 0.6 collective-permute-done.15.b2
  63.1 3.2 %tail_right.1 = (f32[256,512]{1,0:T(8,128)S(1)}, f32[2,128,512]{2,1,0:T(8,128)S(1)}, f32[2,128,512]{2,1,0:T(8,128)S(1)}) custom-call(bf16[272,512]{1,0:T(8,128)(2,1)S(1)} %copy-done, bf16[272,512]{1,0:T(8,128)(2,1)S(1)} %collective-permute-done.11.b1, bf16[272,512]{1,0:T(8,128)(2,1)S(1)} %collective-permute-done.15.b2, ...), custom_call_target="tpu_custom_call" | custom-call | tf_op jit(solution)/shard_map/tail_right/pallas_call | solution.py:422
  66.4 0.1 collective-permute-start.17
  66.4 1.9 %collective-permute-done.17 = f32[2,128,512]{2,1,0:T(8,128)S(1)} collective-permute-done((f32[2,128,512]{2,1,0:T(8,128)S(1)}, f32[2,128,512]{2,1,0:T(8,128)S(1)}, u32[]{:S(2)}, u32[]{:S(2)}) %collective-permute-start.17) | collective-permute-done | bytes 524320 | tf_op jit(solution)/shard_map/ppermute | solution.py:430
  68.3 0.1 add.64
  68.4 1.6 %collective-permute-start.18 = (bf16[128,512]{1,0:T(8,128)(2,1)S(1)}, bf16[128,512]{1,0:T(8,128)(2,1)S(1)}, u32[]{:S(2)}, u32[]{:S(2)}) collective-permute-start(bf16[128,512]{1,0:T(8,128)(2,1)S(1)} %fusion.5), channel_id=1, source_target_pairs={{0,2},{1,3},{2,0},{3,1},{4,6},{5,7},{6,4},{7,5},{8,10},{9,11},{10,... | collective-permute-start | bytes 393224 | tf_op jit(solution)/shard_map/ppermute | solution.py:431
  70.0 1.3 %tail_image.1 = f32[512,512]{1,0:T(8,128)} custom-call(f32[256,512]{1,0:T(8,128)S(1)} %get-tuple-element.61.left, f32[256,512]{1,0:T(8,128)S(1)} %get-tuple-element.77.right), custom_call_target="tpu_custom_call" | custom-call | bytes 2000000 | tf_op jit(solution)/shard_map/tail_image/pallas_call | solution.py:433
  71.3 2.7 %collective-permute-done.18 = bf16[128,512]{1,0:T(8,128)(2,1)S(1)} collective-permute-done((bf16[128,512]{1,0:T(8,128)(2,1)S(1)}, bf16[128,512]{1,0:T(8,128)(2,1)S(1)}, u32[]{:S(2)}, u32[]{:S(2)}) %collective-permute-start.18) | collective-permute-done | bytes 131104 | tf_op jit(solution)/shard_map/ppermute | solution.py:431
  74.0 0.7 fusion.4
  (31 shorter events, 0.1 us)
Async XLA Ops:
  7.1 21.6 %collective-permute-start.12 = (bf16[272,512]{1,0:T(8,128)(2,1)}, bf16[272,512]{1,0:T(8,128)(2,1)}, u32[]{:S(2)}, u32[]{:S(2)}) collective-permute-start(bf16[272,512]{1,0:T(8,128)(2,1)} %get-tuple-element.69), channel_id=1, source_target_pairs={{0,4},{4,0},{8,12},{12,8},{16,20},{20,16},{24,28},{28,24},{1,5},{5... | collective-permute-start | bytes 835592 | tf_op jit(solution)/shard_map/across_turn_1_of/ppermute | solution.py:485
  10.1 13.8 %collective-permute-start = (bf16[272,512]{1,0:T(8,128)(2,1)}, bf16[272,512]{1,0:T(8,128)(2,1)}, u32[]{:S(2)}, u32[]{:S(2)}) collective-permute-start(bf16[272,512]{1,0:T(8,128)(2,1)} %get-tuple-element.43), channel_id=1, source_target_pairs={{0,4},{4,0},{8,12},{12,8},{16,20},{20,16},{24,28},{28,24},{1,5},{5... | collective-permute-start | bytes 835592 | tf_op jit(solution)/shard_map/across_turn_0_of/ppermute | solution.py:485
  18.9 25.9 %copy-start.4 = (bf16[272,512]{1,0:T(8,128)(2,1)S(1)}, bf16[272,512]{1,0:T(8,128)(2,1)}, u32[]{:S(2)}) copy-start(bf16[272,512]{1,0:T(8,128)(2,1)} %get-tuple-element.68) | copy-start | bytes 835588
  18.9 27.1 %copy-start.5 = (bf16[272,512]{1,0:T(8,128)(2,1)S(1)}, bf16[272,512]{1,0:T(8,128)(2,1)}, u32[]{:S(2)}) copy-start(bf16[272,512]{1,0:T(8,128)(2,1)} %get-tuple-element.55) | copy-start | bytes 835588
  18.9 27.9 %copy-start.8 = (bf16[272,512]{1,0:T(8,128)(2,1)S(1)}, bf16[272,512]{1,0:T(8,128)(2,1)}, u32[]{:S(2)}) copy-start(bf16[272,512]{1,0:T(8,128)(2,1)} %get-tuple-element.66) | copy-start | bytes 835588
  18.9 29.6 %copy-start.9 = (bf16[272,512]{1,0:T(8,128)(2,1)S(1)}, bf16[272,512]{1,0:T(8,128)(2,1)}, u32[]{:S(2)}) copy-start(bf16[272,512]{1,0:T(8,128)(2,1)} %get-tuple-element.52) | copy-start | bytes 835588
  19.0 31.6 %copy-start.3 = (bf16[272,512]{1,0:T(8,128)(2,1)S(1)}, bf16[272,512]{1,0:T(8,128)(2,1)}, u32[]{:S(2)}) copy-start(bf16[272,512]{1,0:T(8,128)(2,1)} %get-tuple-element.57) | copy-start | bytes 835588
  19.0 31.6 %copy-start.6 = (bf16[272,512]{1,0:T(8,128)(2,1)S(1)}, bf16[272,512]{1,0:T(8,128)(2,1)}, u32[]{:S(2)}) copy-start(bf16[272,512]{1,0:T(8,128)(2,1)} %get-tuple-element.53) | copy-start | bytes 835588
  19.0 11.3 %collective-permute-start.6 = (bf16[272,512]{1,0:T(8,128)(2,1)}, bf16[272,512]{1,0:T(8,128)(2,1)S(1)}, u32[]{:S(2)}, u32[]{:S(2)}) collective-permute-start(bf16[272,512]{1,0:T(8,128)(2,1)} %get-tuple-element.56), channel_id=1, source_target_pairs={{0,4},{4,0},{8,12},{12,8},{16,20},{20,16},{24,28},{28,24},{1,5},{5... | collective-permute-start | bytes 835592 | tf_op jit(solution)/shard_map/across_turn_2_of/ppermute | solution.py:485
  25.0 26.8 %copy-start.7 = (bf16[272,512]{1,0:T(8,128)(2,1)S(1)}, bf16[272,512]{1,0:T(8,128)(2,1)}, u32[]{:S(2)}) copy-start(bf16[272,512]{1,0:T(8,128)(2,1)} %get-tuple-element.67) | copy-start | bytes 835588
  25.0 9.5 %collective-permute-start.3 = (bf16[272,512]{1,0:T(8,128)(2,1)S(1)}, bf16[272,512]{1,0:T(8,128)(2,1)S(1)}, u32[]{:S(2)}, u32[]{:S(2)}) collective-permute-start(bf16[272,512]{1,0:T(8,128)(2,1)S(1)} %fusion), channel_id=1, source_target_pairs={{0,8},{4,12},{8,0},{12,4},{16,24},{20,28},{24,16},{28,20},{1,9},{5... | collective-permute-start | bytes 835592 | tf_op jit(solution)/shard_map/even_step_0_left/ppermute | solution.py:522
  27.2 15.8 %collective-permute-start.1 = (bf16[544,512]{1,0:T(8,128)(2,1)}, bf16[544,512]{1,0:T(8,128)(2,1)S(1)}, u32[]{:S(2)}, u32[]{:S(2)}) collective-permute-start(bf16[544,512]{1,0:T(8,128)(2,1)} %get-tuple-element.51), channel_id=1, source_target_pairs={{0,4},{4,0},{8,12},{12,8},{16,20},{20,16},{24,28},{28,24},{1,5},{5... | collective-permute-start | bytes 1671176 | tf_op jit(solution)/shard_map/across_turn_3_of/ppermute | solution.py:485
  29.8 15.1 %collective-permute-start.13 = (bf16[272,512]{1,0:T(8,128)(2,1)S(1)}, bf16[272,512]{1,0:T(8,128)(2,1)S(1)}, u32[]{:S(2)}, u32[]{:S(2)}) collective-permute-start(bf16[272,512]{1,0:T(8,128)(2,1)S(1)} %fusion.3), channel_id=1, source_target_pairs={{0,8},{4,12},{8,0},{12,4},{16,24},{20,28},{24,16},{28,20},{1,9},{5... | collective-permute-start | bytes 835592 | tf_op jit(solution)/shard_map/even_step_0_right/ppermute | solution.py:522
  31.4 25.4 %copy-start.2 = (f32[1,25]{1,0:T(1,128)S(1)}, f32[1,25]{1,0:T(1,128)}, u32[]{:S(2)}) copy-start(f32[1,25]{1,0:T(1,128)} %det) | copy-start | bytes 304
  31.4 30.0 %copy-start.1 = (bf16[272,512]{1,0:T(8,128)(2,1)S(1)}, bf16[272,512]{1,0:T(8,128)(2,1)}, u32[]{:S(2)}) copy-start(bf16[272,512]{1,0:T(8,128)(2,1)} %get-tuple-element.48.a0) | copy-start | bytes 835588
  31.4 14.7 %collective-permute-start.7 = (bf16[272,512]{1,0:T(8,128)(2,1)S(1)}, bf16[272,512]{1,0:T(8,128)(2,1)S(1)}, u32[]{:S(2)}, u32[]{:S(2)}) collective-permute-start(bf16[272,512]{1,0:T(8,128)(2,1)S(1)} %fusion.1), channel_id=1, source_target_pairs={{0,8},{4,12},{8,0},{12,4},{16,24},{20,28},{24,16},{28,20},{1,9},{5... | collective-permute-start | bytes 835592 | tf_op jit(solution)/shard_map/even_step_1_left/ppermute | solution.py:522
  33.0 13.8 %collective-permute-start.10 = (bf16[272,512]{1,0:T(8,128)(2,1)}, bf16[272,512]{1,0:T(8,128)(2,1)S(1)}, u32[]{:S(2)}, u32[]{:S(2)}) collective-permute-start(bf16[272,512]{1,0:T(8,128)(2,1)} %get-tuple-element.65), channel_id=1, source_target_pairs={{0,4},{4,0},{8,12},{12,8},{16,20},{20,16},{24,28},{28,24},{1,5},{5... | collective-permute-start | bytes 835592 | tf_op jit(solution)/shard_map/across_turn_4_of/ppermute | solution.py:485
  35.6 12.9 %collective-permute-start.4 = (bf16[272,512]{1,0:T(8,128)(2,1)S(1)}, bf16[272,512]{1,0:T(8,128)(2,1)S(1)}, u32[]{:S(2)}, u32[]{:S(2)}) collective-permute-start(bf16[272,512]{1,0:T(8,128)(2,1)S(1)} %add_convert_fusion.5), channel_id=1, source_target_pairs={{0,1},{1,0},{2,3},{3,2},{4,5},{5,4},{6,7},{7,6},{8,16},{9,17},{10,... | collective-permute-start | bytes 835592 | tf_op jit(solution)/shard_map/odd_step_1_left/ppermute | solution.py:527
  44.0 6.6 %collective-permute-start.9 = (bf16[272,512]{1,0:T(8,128)(2,1)S(1)}, bf16[272,512]{1,0:T(8,128)(2,1)S(1)}, u32[]{:S(2)}, u32[]{:S(2)}) collective-permute-start(bf16[272,512]{1,0:T(8,128)(2,1)S(1)} %fusion.2), channel_id=1, source_target_pairs={{0,8},{4,12},{8,0},{12,4},{16,24},{20,28},{24,16},{28,20},{1,9},{5... | collective-permute-start | bytes 835592 | tf_op jit(solution)/shard_map/even_step_1_right/ppermute | solution.py:522
  45.9 17.2 %copy-start = (bf16[272,512]{1,0:T(8,128)(2,1)S(1)}, bf16[272,512]{1,0:T(8,128)(2,1)}, u32[]{:S(2)}) copy-start(bf16[272,512]{1,0:T(8,128)(2,1)} %get-tuple-element.62.b0) | copy-start | bytes 835588
  45.9 5.9 %collective-permute-start.14 = (bf16[272,512]{1,0:T(8,128)(2,1)S(1)}, bf16[272,512]{1,0:T(8,128)(2,1)S(1)}, u32[]{:S(2)}, u32[]{:S(2)}) collective-permute-start(bf16[272,512]{1,0:T(8,128)(2,1)S(1)} %add_convert_fusion.2), channel_id=1, source_target_pairs={{0,1},{1,0},{2,3},{3,2},{4,5},{5,4},{6,7},{7,6},{8,16},{9,17},{10,... | collective-permute-start | bytes 835592 | tf_op jit(solution)/shard_map/odd_step_1_right/ppermute | solution.py:527
  46.2 10.5 %collective-permute-start.8 = (bf16[272,512]{1,0:T(8,128)(2,1)S(1)}, bf16[272,512]{1,0:T(8,128)(2,1)S(1)}, u32[]{:S(2)}, u32[]{:S(2)}) collective-permute-start(bf16[272,512]{1,0:T(8,128)(2,1)S(1)} %add_convert_fusion.3), channel_id=1, source_target_pairs={{0,1},{1,0},{2,3},{3,2},{4,5},{5,4},{6,7},{7,6},{8,16},{9,17},{10,... | collective-permute-start | bytes 835592 | tf_op jit(solution)/shard_map/odd_step_2_left/ppermute | solution.py:527
  46.8 15.7 %collective-permute-start.11 = (bf16[272,512]{1,0:T(8,128)(2,1)S(1)}, bf16[272,512]{1,0:T(8,128)(2,1)S(1)}, u32[]{:S(2)}, u32[]{:S(2)}) collective-permute-start(bf16[272,512]{1,0:T(8,128)(2,1)S(1)} %copy-done.8), channel_id=1, source_target_pairs={{0,4},{4,0},{8,12},{12,8},{16,20},{20,16},{24,28},{28,24},{1,5},{5... | collective-permute-start | bytes 835592 | tf_op jit(solution)/shard_map/across_turn_6_of/ppermute | solution.py:485
  48.6 12.8 %collective-permute-start.2 = (bf16[272,512]{1,0:T(8,128)(2,1)S(1)}, bf16[272,512]{1,0:T(8,128)(2,1)S(1)}, u32[]{:S(2)}, u32[]{:S(2)}) collective-permute-start(bf16[272,512]{1,0:T(8,128)(2,1)S(1)} %copy-done.9), channel_id=1, source_target_pairs={{0,4},{4,0},{8,12},{12,8},{16,20},{20,16},{24,28},{28,24},{1,5},{5... | collective-permute-start | bytes 835592 | tf_op jit(solution)/shard_map/across_turn_5_of/ppermute | solution.py:485
  50.8 10.5 %collective-permute-start.5 = (bf16[272,512]{1,0:T(8,128)(2,1)S(1)}, bf16[272,512]{1,0:T(8,128)(2,1)S(1)}, u32[]{:S(2)}, u32[]{:S(2)}) collective-permute-start(bf16[272,512]{1,0:T(8,128)(2,1)S(1)} %get-tuple-element.79), channel_id=1, source_target_pairs={{0,8},{4,12},{8,0},{12,4},{16,24},{20,28},{24,16},{28,20},{1,9},{5... | collective-permute-start | bytes 835592 | tf_op jit(solution)/shard_map/even_step_2_left/ppermute | solution.py:522
  51.9 11.2 %collective-permute-start.15 = (bf16[272,512]{1,0:T(8,128)(2,1)S(1)}, bf16[272,512]{1,0:T(8,128)(2,1)S(1)}, u32[]{:S(2)}, u32[]{:S(2)}) collective-permute-start(bf16[272,512]{1,0:T(8,128)(2,1)S(1)} %add_convert_fusion.1), channel_id=1, source_target_pairs={{0,8},{4,12},{8,0},{12,4},{16,24},{20,28},{24,16},{28,20},{1,9},{5... | collective-permute-start | bytes 835592 | tf_op jit(solution)/shard_map/even_step_2_right/ppermute | solution.py:522
  56.7 5.8 %collective-permute-start.16 = (bf16[272,512]{1,0:T(8,128)(2,1)S(1)}, bf16[272,512]{1,0:T(8,128)(2,1)S(1)}, u32[]{:S(2)}, u32[]{:S(2)}) collective-permute-start(bf16[272,512]{1,0:T(8,128)(2,1)S(1)} %get-tuple-element.78), channel_id=1, source_target_pairs={{0,1},{1,0},{2,3},{3,2},{4,5},{5,4},{6,7},{7,6},{8,16},{9,17},{10,... | collective-permute-start | bytes 835592 | tf_op jit(solution)/shard_map/odd_step_2_right/ppermute | solution.py:527
  66.4 2.0 %collective-permute-start.17 = (f32[2,128,512]{2,1,0:T(8,128)S(1)}, f32[2,128,512]{2,1,0:T(8,128)S(1)}, u32[]{:S(2)}, u32[]{:S(2)}) collective-permute-start(f32[2,128,512]{2,1,0:T(8,128)S(1)} %get-tuple-element.76), channel_id=1, source_target_pairs={{0,1},{1,0},{2,3},{3,2},{4,5},{5,4},{6,7},{7,6},{8,9},{9,8},{10,11... | collective-permute-start | bytes 1572872 | tf_op jit(solution)/shard_map/ppermute | solution.py:430
  68.4 5.6 %collective-permute-start.18 = (bf16[128,512]{1,0:T(8,128)(2,1)S(1)}, bf16[128,512]{1,0:T(8,128)(2,1)S(1)}, u32[]{:S(2)}, u32[]{:S(2)}) collective-permute-start(bf16[128,512]{1,0:T(8,128)(2,1)S(1)} %fusion.5), channel_id=1, source_target_pairs={{0,2},{1,3},{2,0},{3,1},{4,6},{5,7},{6,4},{7,5},{8,10},{9,11},{10,... | collective-permute-start | bytes 393224 | tf_op jit(solution)/shard_map/ppermute | solution.py:431

commit v3 on v2

v3 whole, which is shorter than its diff:
```python
import jax
import jax.numpy as jnp
import numpy as np
from jax import lax
from jax.experimental import pallas as pl
from jax.experimental.pallas import tpu as pltpu
from jax.sharding import PartitionSpec as P

TH = 2
TW = 2
DR = 12
CAP = 4
SLOTS = 4
PAD = 16
DIGITS = 16
UNIT = 512


def cuts(rows):
    return (0, rows // 2 + PAD, rows)


def dest_table(outer):
    table = np.zeros((outer, outer), np.int32)
    for z in range(outer):
        def due(d):
            if d > z:
                return (outer - 1 + z - d, d == z ^ 1)
            if d < z:
                return (outer - 1 - z + d, d == z ^ 1)
            return (outer, 0)

        table[z] = sorted(range(outer), key=due)
    return table


def toeplitz(row):
    half = row.shape[1] // 2
    wide = jnp.broadcast_to(row, (half, 2 * half))
    skew = pltpu.roll(wide, 0, 1, stride=1, stride_axis=0)
    diag = skew[:, :half]
    off = skew[:, half:]
    i = lax.broadcasted_iota(jnp.int32, (half, half), 0)
    j = lax.broadcasted_iota(jnp.int32, (half, half), 1)
    upper = jnp.where(j < i, off, 0.0)
    lower = jnp.where(j > i, off, 0.0)
    top = jnp.concatenate([diag, upper], axis=1)
    bottom = jnp.concatenate([lower, diag], axis=1)
    return jnp.concatenate([top, bottom], axis=0).astype(jnp.bfloat16)


def make_lists(npatch, dest, count, index):
    def clear(p, carry):
        count[p] = 0
        for r in range(CAP):
            index[p * CAP + r] = -1
        return carry

    lax.fori_loop(0, npatch, clear, 0)

    def place(n, carry):
        p = dest[0, n]
        r = count[p]
        count[p] = r + 1
        index[p * CAP + r] = n
        return carry

    lax.fori_loop(0, dest.shape[1], place, 0)


def match_patch(p, q, k, slot, units, index, block, taps, acc, pay, edges, digits):
    edge = acc.shape[-1]
    ntaps = taps.shape[-1]
    side = TH * edge
    lane = lax.broadcasted_iota(jnp.int32, (8, 128), 1)
    acc[...] = jnp.zeros(acc.shape, acc.dtype)
    row = jnp.zeros((8, 128), jnp.float32)
    for r in range(CAP):
        found = index[p * CAP + r]
        n = jnp.maximum(found, 0)
        s = slot[0, n]
        unit = jnp.where(found >= 0, units[0, n], 0)
        w = unit.astype(jnp.float32) * (1.0 / UNIT)
        tap = taps[n].astype(jnp.float32)
        tap = jnp.concatenate([tap, jnp.zeros((2, edge - ntaps), jnp.float32)], axis=1)
        tap = pltpu.roll(tap, edge - ntaps // 2, 1)
        col = toeplitz(tap[0:1])
        half = jnp.dot(col, block(n, r), preferred_element_type=jnp.float32).astype(jnp.bfloat16)
        rowm = toeplitz(tap[1:2])
        matched = lax.dot_general(
            rowm, half, (((1,), (1,)), ((), ())), preferred_element_type=jnp.float32
        ).astype(jnp.bfloat16)
        acc[s] = acc[s] + w * matched.astype(jnp.float32)
        bit = lax.shift_right_logical(jnp.full((8, 128), unit), lane % DIGITS) & 1
        row = row + jnp.where(lane // DIGITS == s, bit, 0).astype(jnp.float32)
    digits[q] = row
    for s in range(SLOTS):
        top = (s % TW) * edge
        left = (s // TW) * edge
        pay[k, PAD + top : PAD + top + edge, left : left + edge] = acc[s].astype(jnp.bfloat16)
    edges[q, 0] = pay[k, PAD : 2 * PAD, :]
    edges[q, 1] = pay[k, side : side + PAD, :]


def add_halos(k, before, q, after, pay, edges, digits):
    rows, side = pay.shape[1:]
    first = lax.broadcasted_iota(jnp.int32, (PAD, side), 0) == 0
    blank = jnp.zeros((8, side - 3 * 128), jnp.float32)
    row = jnp.concatenate([digits[q], digits[before], digits[after], blank], axis=1)
    row = jnp.concatenate([row, row], axis=0)
    pay[k, :PAD, :] = jnp.where(first, row, edges[before, 1].astype(jnp.float32)).astype(jnp.bfloat16)
    pay[k, rows - PAD :, :] = edges[after, 0]


def begin(npatch, sources, targets, wide, units, count, index, sems):
    fetched = [pltpu.make_async_copy(x, y, sems.at[i]) for i, (x, y) in enumerate(zip(sources, targets, strict=True))]
    for copy in fetched:
        copy.start()
    dest, weights = targets[:2]
    fetched[1].wait()
    wide[...] = (weights[...].astype(jnp.float32) * UNIT).astype(jnp.int32)
    convert = pltpu.make_async_copy(wide, units, sems.at[len(fetched)])
    convert.start()
    fetched[0].wait()
    make_lists(npatch, dest, count, index)
    return [*fetched[2:], convert]


def base_of(npatch, me):
    return jnp.where(2 * (me // 2) < npatch // 2, npatch - 3, npatch - 1)


def first_kernel(
    npatch, dest_in, slot_in, weights_in, blocks_in, taps_in, s_a, k_a, both, own, edges_out, digits_out,
    acc, pay, blocks, taps, weights, wide, edges, digits, dest, slot, units, count, index, sems, sends,
):
    sources = (dest_in, weights_in, slot_in, taps_in, blocks_in)
    waits = begin(npatch, sources, (dest, weights, slot, taps, blocks), wide, units, count, index, sems)
    me = lax.axis_index("patch")
    base = base_of(npatch, me)
    for copy in waits:
        copy.wait()
    rows, side = pay.shape[1:]
    copies = []

    def send(source, out):
        copies.append(pltpu.make_async_copy(source, out, sends.at[len(copies)]))
        copies[-1].start()

    def either_way(first_out, second_out, q, part):
        source = pay.at[q, cuts(rows)[part] : cuts(rows)[part + 1]]
        copy = [pltpu.make_async_copy(source, out, sends.at[len(copies)]) for out in (first_out, second_out)]
        copies.append(copy[0])
        goes = lax.rem(me, 2) == 2 - q
        pl.when(goes)(copy[0].start)
        pl.when(jnp.logical_not(goes))(copy[1].start)

    def match(q):
        p = lax.rem(base + q, npatch)
        match_patch(p, q, q, slot, units, index, lambda n, r: blocks[n], taps, acc, pay, edges, digits)

    match(0)
    match(1)
    send(pay.at[0, PAD : PAD + side], own.at[0])
    match(2)
    match(3)
    height = both.shape[0] // 2
    for q in (1, 2):
        add_halos(q, q - 1, q, q + 1, pay, edges, digits)
        either_way(s_a, k_a, q, 0)
        either_way(both.at[:height], both.at[height:], q, 1)
    send(pay.at[3, PAD : PAD + side], own.at[1])
    send(edges, edges_out)
    send(digits, digits_out)
    for copy in copies:
        copy.wait()


def make_turns(outer):
    last = outer - 1
    turns = [[(0, 0)], [(1, 0)], [(1, 1)], [(last - 1, 1)]]
    turns += [[(s, 0), (s, 1)] for s in range(2, last - 1)]
    return turns + [[(last - 1, 0)], [(last, 0)], [(last, 1)]]


def rest_kernel(
    npatch, dest_in, slot_in, weights_in, blocks_in, taps_in, orders_in, own, edges_in, digits_in, *rest
):
    turns = make_turns(npatch // 2)[1:]
    sent = {part: turn for turn, parts in enumerate(turns) for part in parts}
    number = len(turns) + npatch - 2
    outs = rest[:number]
    (
        acc, pay, blocks, taps, weights, wide, edges, digits,
        dest, slot, units, orders, count, index, place, sems, sends,
    ) = rest[number:]
    sources = (dest_in, weights_in, orders_in, slot_in, taps_in, edges_in, digits_in, blocks_in)
    targets = (dest, weights, orders, slot, taps, edges.at[:4], digits.at[:4], blocks)
    waits = begin(npatch, sources, targets, wide, units, count, index, sems)
    rows, side = pay.shape[1:]
    me = lax.axis_index("patch")
    base = base_of(npatch, me)
    waits[0].wait()

    def put(k, carry):
        place[orders[me, k]] = k - 2
        return carry

    lax.fori_loop(0, npatch, put, 0)
    for j in range(2):
        k = place[lax.rem(base + 3 * j, npatch)]
        waits.append(pltpu.make_async_copy(own.at[j], pay.at[k, PAD : PAD + side], sems.at[len(sources) + 1 + j]))
        waits[-1].start()

    def copies(k):
        result = []
        for j in range(2):
            begin, end = cuts(rows)[j : j + 2]
            if k % 2:
                out = outs[len(turns) + k - 1 + j]
            else:
                turn = sent[k // 2 + 1, j]
                out = outs[turn].at[begin:end] if len(turns[turn]) == 2 else outs[turn]
            result.append(pltpu.make_async_copy(pay.at[k, begin:end], out, sends.at[2 * k + j]))
        return result

    def send(q):
        mine = place[lax.rem(base + q, npatch)]
        add_halos(mine, lax.rem(q + npatch - 1, npatch), q, lax.rem(q + 1, npatch), pay, edges, digits)
        for k in range(npatch - 2):

            @pl.when(mine == k)
            def _():
                for copy in copies(k):
                    copy.start()

    for copy in waits[1:]:
        copy.wait()

    def match(q):
        p = lax.rem(base + q, npatch)
        match_patch(p, q, place[p], slot, units, index, lambda n, r: blocks[n], taps, acc, pay, edges, digits)

    def pair(i, carry):
        match(4 + 2 * i)
        match(5 + 2 * i)
        send(3 + 2 * i)
        send(4 + 2 * i)
        return carry

    lax.fori_loop(0, npatch // 2 - 2, pair, 0)
    send(npatch - 1)
    send(0)
    for k in range(npatch - 2):
        for copy in copies(k):
            copy.wait()


def match_blocks(dest, slot, weights, orders, blocks, taps):
    npatch, number = orders.shape[0], blocks.shape[0]
    edge = blocks.shape[-1]
    side = TH * edge
    rows = side + 2 * PAD
    hbm = pl.BlockSpec(memory_space=pltpu.HBM)
    part = [jax.ShapeDtypeStruct((end - begin, side), jnp.bfloat16) for begin, end in zip(cuts(rows), cuts(rows)[1:])]
    whole = jax.ShapeDtypeStruct((rows, side), jnp.bfloat16)
    params = pltpu.CompilerParams(vmem_limit_bytes=64 * 1024 * 1024)
    ints = pltpu.SMEM((1, number), jnp.int32)

    def scratch(payloads, patches):
        return [
            pltpu.VMEM((SLOTS, edge, edge), jnp.float32),
            pltpu.VMEM((payloads, rows, side), jnp.bfloat16),
            pltpu.VMEM(blocks.shape, jnp.bfloat16),
            pltpu.VMEM(taps.shape, jnp.bfloat16),
            pltpu.VMEM((1, number), jnp.bfloat16),
            pltpu.VMEM((1, number), jnp.int32),
            pltpu.VMEM((patches, 2, PAD, side), jnp.bfloat16),
            pltpu.VMEM((patches, 8, 128), jnp.float32),
            ints,
            ints,
            ints,
        ]

    count = pltpu.SMEM((npatch,), jnp.int32)
    index = pltpu.SMEM((npatch * CAP,), jnp.int32)
    s_a, k_a, both, own, edges, digits = pl.pallas_call(
        lambda *refs: first_kernel(npatch, *refs),
        out_shape=[part[0]] * 2
        + [
            jax.ShapeDtypeStruct((2 * part[1].shape[0], side), jnp.bfloat16),
            jax.ShapeDtypeStruct((2, side, side), jnp.bfloat16),
            jax.ShapeDtypeStruct((4, 2, PAD, side), jnp.bfloat16),
            jax.ShapeDtypeStruct((4, 8, 128), jnp.float32),
        ],
        in_specs=[hbm] * 5,
        out_specs=[hbm] * 6,
        scratch_shapes=[
            *scratch(4, 4),
            count,
            index,
            pltpu.SemaphoreType.DMA((6,)),
            pltpu.SemaphoreType.DMA((8,)),
        ],
        compiler_params=params,
        name="match_first",
    )(dest, slot, weights, blocks, taps)
    turns = make_turns(npatch // 2)
    outs = pl.pallas_call(
        lambda *refs: rest_kernel(npatch, *refs),
        out_shape=[whole if len(turn) == 2 else part[turn[0][1]] for turn in turns[1:]] + part * (npatch // 2 - 1),
        in_specs=[hbm] * 9,
        out_specs=[hbm] * (len(turns) - 1 + npatch - 2),
        scratch_shapes=[
            *scratch(npatch - 2, npatch),
            pltpu.SMEM(orders.shape, jnp.int32),
            count,
            index,
            pltpu.SMEM((npatch,), jnp.int32),
            pltpu.SemaphoreType.DMA((11,)),
            pltpu.SemaphoreType.DMA((2 * (npatch - 2),)),
        ],
        compiler_params=params,
        cost_estimate=pl.CostEstimate(flops=2_000_000_000, bytes_accessed=8_000_000, transcendentals=0),
        name="match_rest",
    )(dest, slot, weights, blocks, taps, jnp.asarray(orders), own, edges, digits)
    sends = [s_a] + list(outs[: len(turns) - 1])
    kept = outs[len(turns) - 1 :]
    return sends, [(k_a, None)] + [(kept[2 * k], kept[2 * k + 1]) for k in range(npatch // 2 - 1)], both


def split(value):
    high = value.astype(jnp.bfloat16)
    return high, (value - high.astype(jnp.float32)).astype(jnp.bfloat16)


def dot3(ah, al, bh, bl, dims):
    def one(a, b):
        return lax.dot_general(a, b, (dims, ((), ())), preferred_element_type=jnp.float32)

    return one(ah, bh) + (one(ah, bl) + one(al, bh))


def chi_rows(place, rowh, rowl, ch, cl, noise):
    rows = pl.ds(pl.multiple_of(place * 128, 128), 128)
    row_pass = dot3(rowh[rows, :], rowl[rows, :], ch, cl, ((1,), (1,)))
    return row_pass * row_pass * (1.0 / noise[0])


def total(x0, x1, x2, x3):
    f32 = jnp.float32
    return x0[...].astype(f32) + x1[...].astype(f32) + (x2[...].astype(f32) + x3[...].astype(f32))


def column_pass(colh, coll, padded):
    high, low = split(padded)
    return split(dot3(colh[...], coll[...], high, low, ((1,), (0,))))


def tail_left(a0, a1, a2, a3, noise, band, colh, coll, rowh, rowl, normed, seam, factor, give, stay):
    f32 = jnp.float32
    rows, side = a0.shape
    edge = side // TH
    left = total(a0, a1, a2, a3)
    lane = lax.broadcasted_iota(jnp.int32, (1, side), 1)
    power = lax.shift_left(jnp.ones((1, side), jnp.int32), lane % DIGITS).astype(f32) * (1.0 / UNIT)
    value = left[0:1, :] * power

    def scale(group, s):
        here = (lane >= group * 128 + s * DIGITS) & (lane < group * 128 + (s + 1) * DIGITS)
        weight_sum = jnp.sum(jnp.where(here, value, 0.0), axis=1, keepdims=True)
        return jnp.broadcast_to(1.0 / jnp.maximum(weight_sum, 1.0), (1, edge))

    def factors(group, column):
        return jnp.concatenate([scale(group, r * TW + column) for r in range(TH)], axis=1)

    right = factors(0, 1)
    left = jnp.concatenate(
        [left[:PAD] * factors(1, TW - 1), left[PAD : PAD + edge] * factors(0, 0), left[PAD + edge :] * right], axis=0
    )
    normed[...] = left[PAD : PAD + edge]
    seam[...] = left[edge:]
    factor[0] = jnp.broadcast_to(right, (8, side))
    factor[1] = jnp.broadcast_to(factors(2, 0), (8, side))
    ch, cl = column_pass(colh, coll, left)
    for j, place in enumerate((band[0], band[0] ^ 2)):
        give[j] = chi_rows(place ^ 1, rowh, rowl, ch, cl, noise)
        stay[j] = chi_rows(place, rowh, rowl, ch, cl, noise)


def tail_right(
    b0, b1, b2, b3, seam, factor, give_left, stay_left, noise, band, colh, coll, rowh, rowl, normed, give, stay
):
    rows, side = b0.shape
    edge = side // TH
    right = total(b0, b1, b2, b3)
    inner = edge - PAD
    right = jnp.concatenate([seam[...], right[:inner] * factor[0, 0:1], right[inner:] * factor[1, 0:1]], axis=0)
    normed[...] = right[PAD : PAD + edge]
    ch, cl = column_pass(colh, coll, right)
    for j, place in enumerate((band[0], band[0] ^ 2)):
        give[j, :, edge:] = chi_rows(place ^ 1, rowh, rowl, ch, cl, noise).astype(give.dtype)
        stay[j, :, edge:] = chi_rows(place, rowh, rowl, ch, cl, noise)
        give[j, :, :edge] = give_left[j].astype(give.dtype)
        stay[j, :, :edge] = stay_left[j]


def tail_image(left, right, image):
    edge = left.shape[0]
    image[:, :edge] = left[...].T
    image[:, edge:] = right[...].T


def tables_kernel(det, colh, coll, rowh, rowl):
    for high, low, start in ((colh, coll, DR - PAD), (rowh, rowl, DR)):
        offsets = (
            lax.broadcasted_iota(jnp.int32, high.shape, 1)
            - lax.broadcasted_iota(jnp.int32, high.shape, 0)
            + start
        )
        table = jnp.zeros(high.shape, jnp.float32)
        for tap in range(det.shape[1]):
            table = jnp.where(offsets == tap, det[0, tap], table)
        high[...], low[...] = split(table)


def filter_tables(det, rows, side):
    return pl.pallas_call(
        tables_kernel,
        out_shape=[jax.ShapeDtypeStruct(s, jnp.bfloat16) for s in [(side // TW, rows)] * 2 + [(side, side)] * 2],
        in_specs=[pl.BlockSpec(memory_space=pltpu.SMEM)],
        out_specs=[pl.BlockSpec(memory_space=pltpu.VMEM)] * 4,
        compiler_params=pltpu.CompilerParams(vmem_limit_bytes=40 * 1024 * 1024),
        cost_estimate=pl.CostEstimate(flops=20_000_000, bytes_accessed=2_000_000, transcendentals=0),
        name="tables",
    )(det)


def finish(left, right, noise, det):
    rows, side = left[0].shape
    f32, bf16 = jnp.float32, jnp.bfloat16
    colh, coll, rowh, rowl = filter_tables(det, rows, side)
    band = lax.axis_index("band")
    where = band.reshape(1).astype(jnp.int32)
    smem = pl.BlockSpec(memory_space=pltpu.SMEM)
    vmem = pl.BlockSpec(memory_space=pltpu.VMEM)
    params = pltpu.CompilerParams(vmem_limit_bytes=40 * 1024 * 1024)
    quarters = jax.ShapeDtypeStruct((2, side // 4, side // TW), f32)
    tile = jax.ShapeDtypeStruct((side // TW, side), f32)
    tables = (colh, coll, rowh, rowl)

    normed_left, seam, factor, give, stay = pl.pallas_call(
        tail_left,
        out_shape=[
            tile,
            jax.ShapeDtypeStruct((2 * PAD, side), f32),
            jax.ShapeDtypeStruct((2, 8, side), f32),
            quarters,
            quarters,
        ],
        in_specs=[vmem] * 4 + [smem] * 2 + [vmem] * 4,
        out_specs=[vmem] * 5,
        compiler_params=params,
        cost_estimate=pl.CostEstimate(flops=500_000_000, bytes_accessed=4_000_000, transcendentals=0),
        name="tail_left",
    )(*left, noise, where, *tables)
    normed_right, give, stay = pl.pallas_call(
        tail_right,
        out_shape=[
            tile,
            jax.ShapeDtypeStruct((2, side // 4, side), bf16),
            jax.ShapeDtypeStruct((2, side // 4, side), f32),
        ],
        in_specs=[vmem] * 8 + [smem] * 2 + [vmem] * 4,
        out_specs=[vmem] * 3,
        compiler_params=params,
        name="tail_right",
    )(*right, seam, factor, give, stay, noise, where, *tables)
    pair = stay + lax.ppermute(give, "band", [(i, i ^ 1) for i in range(4)]).astype(f32)
    beyond = lax.ppermute(pair[1].astype(bf16), "band", [(i, i ^ 2) for i in range(4)])
    normed_right, _ = lax.optimization_barrier((normed_right, pair))
    image = pl.pallas_call(
        tail_image,
        out_shape=jax.ShapeDtypeStruct((side, side), f32),
        in_specs=[vmem] * 2,
        out_specs=vmem,
        compiler_params=params,
        cost_estimate=pl.CostEstimate(flops=0, bytes_accessed=2_000_000, transcendentals=0),
        name="tail_image",
    )(normed_left, normed_right)
    return image, pair[0] + beyond.astype(f32)


def either(flags):
    result = flags[0]
    for flag in flags[1:]:
        result = result | flag
    return result


def local(blocks, dest_patch, dest_slot, weights, psf_taps, det_taps, noise_var):
    f32, bf16 = jnp.float32, jnp.bfloat16
    npatch = lax.axis_size("patch")
    outer = npatch // 2
    me = lax.axis_index("patch")
    z = me // 2
    table = dest_table(outer)
    where_is = np.argsort(table, axis=1)
    order = np.zeros((npatch, npatch), np.int32)
    for i in range(npatch):
        for s in range(outer):
            order[i, 2 * s] = table[i // 2, s] * 2 + 1 - i % 2
            order[i, 2 * s + 1] = table[i // 2, s] * 2 + i % 2
    sends, kept, both = match_blocks(dest_patch, dest_slot, weights, order, blocks[0], psf_taps[0])
    last = outer - 1
    nband = lax.axis_size("band")
    across = [(i, i ^ 1) for i in range(npatch)]
    even = [(i, i ^ 2) for i in range(npatch)]
    odd = []
    for i in range(npatch):
        q = i // 2
        to = q + 1 if q % 2 else q - 1
        for j in range(nband):
            if 0 <= to < outer:
                odd.append((i * nband + j, (2 * to + i % 2) * nband + j))
            else:
                odd.append((i * nband + j, i * nband + (j ^ 1)))
    ends, beside_ends = (0, last), (1, last - 1)

    def place_in(places):
        return either([z == q for q in places])

    def only(places, value):
        return jnp.where(place_in(places), value.astype(f32), 0.0)

    half = both.shape[0] // 2
    with jax.named_scope("even_step_0_right"):
        direct = lax.ppermute(both, "patch", even)
    came = {}
    got = []

    def across_y(send):
        i = len(got)
        if i in (1, 2):
            send, _ = lax.optimization_barrier((send, got[0]))
        if i > 3:
            send, _, _ = lax.optimization_barrier((send, got[i - 2], got[i - 3]))
        with jax.named_scope(f"across_turn_{i}_of"):
            got.append(lax.ppermute(send, "patch", across))

    turns = make_turns(outer)
    for parts, send in zip(turns[:-1], sends, strict=False):
        if len(got) == 3:
            paired = both[:half].astype(f32) + only(beside_ends, direct[:half])
            send = jnp.where(place_in(ends), send.astype(f32), paired).astype(bf16)
        across_y(send)
        for part in parts:
            begin, end = cuts(got[-1].shape[0])[part[1] :][:2]
            came[part] = got[-1][begin:end] if len(parts) == 2 else got[-1]

    def combined(s, c):
        if (s, c) == (0, 1):
            mine = both[half:].astype(f32) + only(beside_ends, direct[half:])
            return mine + came[last - 1, 1].astype(f32)
        if (s, c) == (last - 1, 1):
            return kept[s][c].astype(f32) + only(ends, came[s, c])
        mine, other = kept[s][c], came[s, c]
        if s == 0:
            other, _ = lax.optimization_barrier((other, sends[1]))
        return mine.astype(f32) + other.astype(f32)

    def chosen(places, c):
        values = sorted(set(places.values()))
        result = combined(values[-1], c)
        for v in values[:-1]:
            result = jnp.where(either([z == q for q, s in places.items() if s == v]), combined(v, c), result)
        return result

    def step(t, parity, c):
        places = {}
        for q in range(outer):
            rising = q % 2 == parity
            hops = q if rising else last - q
            d = last - t + q if rising else t - hops
            if hops <= t and 0 <= d < outer and d != q:
                places[q] = int(where_is[q][d])
        return chosen(places, c)

    def masked(value):
        return jnp.where(place_in(ends), 0.0, value.astype(f32))

    evens, odds, send_even = [None, None], [None, None], [None, None]
    for t in range(last):
        for c in range(2):
            side = "left" if c == 0 else "right"
            send = None if (t, c) == (0, 1) else step(t, 0, c)
            if t > 1:
                send = send + masked(odds[c])
            send_odd = step(t, 1, c) if t else None
            if (t, c) == (2, 1):
                send, _ = lax.optimization_barrier((send, came[last, 0]))
            if t and (t, c) != (1, 1):
                send_odd = send_odd + evens[c].astype(f32)
            if (t, c) == (1, 1):
                passing, _ = lax.optimization_barrier((sends[3], got[1]))
                send = jnp.where(place_in(ends), send, passing.astype(f32))
            if send is not None:
                with jax.named_scope(f"even_step_{t}_{side}"):
                    send_even[c] = send.astype(bf16)
                    evens[c] = lax.ppermute(send_even[c], "patch", even)
            if (t, c) == (1, 1):
                passed = jnp.where(place_in(beside_ends), 0.0, evens[c].astype(f32))
                across_y((sends[-1].astype(f32) + passed).astype(bf16))
                came[last, 1] = got[-1]
            if (t, c) == (1, 1):
                det_taps, _ = lax.optimization_barrier((det_taps, evens[c]))
            if (t, c) == (2, 1):
                send_odd, _ = lax.optimization_barrier((send_odd.astype(bf16), send_even[0]))
            if t:
                with jax.named_scope(f"odd_step_{t}_{side}"):
                    odds[c] = lax.ppermute(send_odd.astype(bf16), ("patch", "band"), odd)
    for c in range(2):
        odds[c] = masked(odds[c]).astype(bf16)
    parts = [(kept[last][c], came[last, c], evens[c], odds[c]) for c in range(2)]
    image, chi = finish(*parts, noise_var, det_taps)
    return image[None], chi


def solution(mesh):
    in_specs = (
        P("band", "patch", None, None),
        P("band", "patch"),
        P("band", "patch"),
        P("band", "patch"),
        P("band", "patch", None, None),
        P("band", None),
        P("band"),
    )
    out_specs = (P("band", None, "patch"), P("band", "patch"))
    return jax.shard_map(local, mesh=mesh, in_specs=in_specs, out_specs=out_specs, check_vma=False)
```

time: 76 us -> 73.3 us (0.964)
  the two profiles are of different devices: /device:TPU:0 before, /device:TPU:18 now
where the time goes in v3:
time: 73.3 us; the launch traced here: 73.1 us
  waiting for transfers between devices  32.7 us (45%)
  Pallas kernels  19.6 us (27%)
  starting transfers between devices  12 us (16%)
  other arithmetic  7.22 us (10%)
  between operations  1.57 us (2%)
    ppermute x4, waiting for transfers between devices, local(): odds[c] = lax.ppermute(send_odd.astype(bf16), ('patch', 'band'), odd)  11.5 us
    ppermute x7, waiting for transfers between devices, across_y(): got.append(lax.ppermute(send, 'patch', across))  11.2 us
    pallas_call x1, Pallas kernels, match_blocks(): pl.pallas_call(lambda *refs: rest_kernel(npatch, *refs), out_shape=[whole...  7.24 us
    pallas_call x1, Pallas kernels, match_blocks(): pl.pallas_call(lambda *refs: first_kernel(npatch, *refs), out_shape=[part...  5.98 us
    ppermute x7, starting transfers between devices, across_y(): got.append(lax.ppermute(send, 'patch', across))  5.29 us
    ppermute x5, waiting for transfers between devices, local(): evens[c] = lax.ppermute(send_even[c], 'patch', even)  4.37 us
    ppermute x1, waiting for transfers between devices, finish(): lax.ppermute(pair[1].astype(bf16), 'band', [(i, i ^ 2) for i in range(4)])  3.72 us
    convert_element_type x4, other arithmetic, local(): send_even[c] = send.astype(bf16)  2.46 us
  transfers between devices with their start and end apart: 19, of which 13 were waited for; matrix products, arithmetic and copies ran while one was open for 9% of the time, Pallas kernels for 16%

profile of v3, /device:TPU:18, one launch (start us, length us, event | category | flops | bytes accessed | tf_op | source)
XLA Modules:
  0.0 73.1 jit_solution(8918063272521676655)
XLA Ops:
  0.6 6.0 %match_first.1 = (bf16[288,512]{1,0:T(8,128)(2,1)}, bf16[288,512]{1,0:T(8,128)(2,1)}, bf16[512,512]{1,0:T(8,128)(2,1)}, bf16[2,512,512]{2,1,0:T(8,128)(2,1)}, bf...) custom-call(s32[1,32]{1,0:T(1,128)} %refs_0_.3, s32[1,32]{1,0:T(1,128)} %refs_1_.3, bf16[1,32]{1,0:T(2,128)(2,1)} %refs_2_.3, ...), custom_call_target="tpu_custom_call" | custom-call | tf_op jit(solution)/shard_map/match_first/pallas_call | solution.py:287
  6.6 1.6 %collective-permute-start.2 = (bf16[288,512]{1,0:T(8,128)(2,1)}, bf16[288,512]{1,0:T(8,128)(2,1)}, u32[]{:S(2)}, u32[]{:S(2)}) collective-permute-start(bf16[288,512]{1,0:T(8,128)(2,1)} %get-tuple-element.51), channel_id=1, source_target_pairs={{0,4},{4,0},{8,12},{12,8},{16,20},{20,16},{24,28},{28,24},{1,5},{5... | collective-permute-start | bytes 884744 | tf_op jit(solution)/shard_map/across_turn_0_of/ppermute | solution.py:549
  8.2 1.6 %collective-permute-start = (bf16[512,512]{1,0:T(8,128)(2,1)}, bf16[512,512]{1,0:T(8,128)(2,1)}, u32[]{:S(2)}, u32[]{:S(2)}) collective-permute-start(bf16[512,512]{1,0:T(8,128)(2,1)} %get-tuple-element.49), channel_id=1, source_target_pairs={{0,8},{4,12},{8,0},{12,4},{16,24},{20,28},{24,16},{28,20},{1,9},{5... | collective-permute-start | bytes 1572872 | tf_op jit(solution)/shard_map/even_step_0_right/ppermute | solution.py:538
  10.4 7.2 %match_rest.1 = (bf16[288,512]{1,0:T(8,128)(2,1)}, bf16[256,512]{1,0:T(8,128)(2,1)}, bf16[256,512]{1,0:T(8,128)(2,1)}, bf16[288,512]{1,0:T(8,128)(2,1)}, bf16[28...) custom-call(s32[1,32]{1,0:T(1,128)} %refs_0_.3, ...), custom_call_target="tpu_custom_call" | custom-call | flops 2000000000 | bytes 8000000 | tf_op jit(solution)/shard_map/match_rest/pallas_call | solution.py:309
  17.8 0.6 collective-permute-start.5
  18.4 1.5 %collective-permute-start.3 = (bf16[256,512]{1,0:T(8,128)(2,1)}, bf16[256,512]{1,0:T(8,128)(2,1)S(1)}, u32[]{:S(2)}, u32[]{:S(2)}) collective-permute-start(bf16[256,512]{1,0:T(8,128)(2,1)} %get-tuple-element.52), channel_id=1, source_target_pairs={{0,4},{4,0},{8,12},{12,8},{16,20},{20,16},{24,28},{28,24},{1,5},{5... | collective-permute-start | bytes 786440 | tf_op jit(solution)/shard_map/across_turn_2_of/ppermute | solution.py:549
  19.9 1.1 %fusion = bf16[288,512]{1,0:T(8,128)(2,1)S(1)} fusion(bf16[288,512]{1,0:T(8,128)(2,1)} %collective-permute-done.2, bf16[288,512]{1,0:T(8,128)(2,1)} %get-tuple-element.59), kind=kLoop, calls=%fused_computation.10 | loop fusion | flops 589824 | bytes 884736 | tf_op jit(solution)/shard_map/even_step_0_left/convert_element_type | solution.py:609
  21.0 0.5 collective-permute-start.7
  21.5 0.4 collective-permute-done
  21.9 1.2 %select_convert_fusion.3 = bf16[256,512]{1,0:T(8,128)(2,1)S(1)} fusion(bf16[256,512]{1,0:T(8,128)(2,1)} %get-tuple-element.63, bf16[512,512]{1,0:T(8,128)(2,1)} %collective-permute-done, bf16[512,512]{1,0:T(8,128)(2,1)} %get-tuple-element.49, pred[]{:T(512)S(6)} %or.5, pred[]{:T(512)S(6)} %or.4), kind=kLoop, calls=%fused_computation.22 | loop fusion | flops 917504 | bytes 1048578 | tf_op jit(solution)/shard_map/convert_element_type | solution.py:555
  23.1 0.6 collective-permute-start.1
  23.7 4.3 %collective-permute-done.5 = bf16[288,512]{1,0:T(8,128)(2,1)S(1)} collective-permute-done((bf16[288,512]{1,0:T(8,128)(2,1)}, bf16[288,512]{1,0:T(8,128)(2,1)S(1)}, u32[]{:S(2)}, u32[]{:S(2)}) %collective-permute-start.5) | collective-permute-done | bytes 294944 | tf_op jit(solution)/shard_map/across_turn_1_of/ppermute | solution.py:549
  28.0 5.6 %collective-permute-done.3 = bf16[256,512]{1,0:T(8,128)(2,1)S(1)} collective-permute-done((bf16[256,512]{1,0:T(8,128)(2,1)}, bf16[256,512]{1,0:T(8,128)(2,1)S(1)}, u32[]{:S(2)}, u32[]{:S(2)}) %collective-permute-start.3) | collective-permute-done | bytes 262176 | tf_op jit(solution)/shard_map/across_turn_2_of/ppermute | solution.py:549
  33.6 1.1 %select_convert_fusion.2 = bf16[256,512]{1,0:T(8,128)(2,1)S(1)} fusion(bf16[256,512]{1,0:T(8,128)(2,1)} %get-tuple-element.63, bf16[256,512]{1,0:T(8,128)(2,1)S(1)} %collective-permute-done.3, bf16[256,512]{1,0:T(8,128)(2,1)} %get-tuple-element.62, pred[]{:T(512)S(6)} %or.4), kind=kLoop, calls=%fused_computation.20 | loop fusion | flops 786432 | bytes 1048577 | tf_op jit(solution)/shard_map/even_step_1_right/convert_element_type | solution.py:609
  34.7 0.5 collective-permute-start.12
  35.3 0.5 collective-permute-start.6
  35.8 1.2 %add_convert_fusion.2 = bf16[288,512]{1,0:T(8,128)(2,1)S(1)} fusion(bf16[288,512]{1,0:T(8,128)(2,1)S(1)} %collective-permute-done.7, bf16[288,512]{1,0:T(8,128)(2,1)} %collective-permute-done.2, bf16[288,512]{1,0:T(8,128)(2,1)} %get-tuple-element.59), kind=kLoop, calls=%fused_computation.8 | loop fusion | flops 884736 | bytes 1179648 | tf_op jit(solution)/shard_map/odd_step_1_left/convert_element_type | solution.py:621
  37.0 0.5 collective-permute-start.8
  37.5 0.1 fusion.1
  37.5 1.2 %collective-permute-start.10 = (bf16[288,512]{1,0:T(8,128)(2,1)S(1)}, bf16[288,512]{1,0:T(8,128)(2,1)S(1)}, u32[]{:S(2)}, u32[]{:S(2)}) collective-permute-start(bf16[288,512]{1,0:T(8,128)(2,1)S(1)} %fusion.1), channel_id=1, source_target_pairs={{0,8},{4,12},{8,0},{12,4},{16,24},{20,28},{24,16},{28,20},{1,9},{5... | collective-permute-start | bytes 884744 | tf_op jit(solution)/shard_map/even_step_1_left/ppermute | solution.py:610
  38.8 0.4 collective-permute-done.1
  39.2 1.1 %fusion.7 = bf16[256,512]{1,0:T(8,128)(2,1)S(1)} fusion(bf16[256,512]{1,0:T(8,128)(2,1)S(1)} %collective-permute-done.1, bf16[512,512]{1,0:T(8,128)(2,1)} %collective-permute-done, bf16[512,512]{1,0:T(8,128)(2,1)S(1)} %copy-done.5, pred[]{:T(512)S(6)} %or.5), kind=kLoop, calls=%fused_computation.17 | loop fusion | flops 917504 | bytes 1048577 | tf_op jit(solution)/shard_map/odd_step_1_right/convert_element_type | solution.py:621
  40.3 0.1 collective-permute-start.14
  40.4 1.8 %collective-permute-done.12 = bf16[256,512]{1,0:T(8,128)(2,1)S(1)} collective-permute-done((bf16[256,512]{1,0:T(8,128)(2,1)S(1)}, bf16[256,512]{1,0:T(8,128)(2,1)S(1)}, u32[]{:S(2)}, u32[]{:S(2)}) %collective-permute-start.12) | collective-permute-done | bytes 262176 | tf_op jit(solution)/shard_map/even_step_1_right/ppermute | solution.py:610
  42.2 0.2 fusion.4
  42.4 1.5 %tables.1 = (bf16[256,288]{1,0:T(8,128)(2,1)S(1)}, bf16[256,288]{1,0:T(8,128)(2,1)S(1)}, bf16[512,512]{1,0:T(8,128)(2,1)S(1)}, bf16[512,512]{1,0:T(8,128)(2,1)S(1)}) custom-call(f32[1,25]{1,0:T(1,128)S(1)} %copy-done.2), custom_call_target="tpu_custom_call" | custom-call | flops 20000000 | bytes 2000000 | tf_op jit(solution)/shard_map/tables/pallas_call | solution.py:428
  43.9 0.8 %collective-permute-done.6 = bf16[288,512]{1,0:T(8,128)(2,1)S(1)} collective-permute-done((bf16[288,512]{1,0:T(8,128)(2,1)}, bf16[288,512]{1,0:T(8,128)(2,1)S(1)}, u32[]{:S(2)}, u32[]{:S(2)}) %collective-permute-start.6) | collective-permute-done | bytes 294944 | tf_op jit(solution)/shard_map/across_turn_4_of/ppermute | solution.py:549
  44.7 0.1 collective-permute-done.8
  44.8 0.1 add_convert_fusion.1
  44.9 0.1 collective-permute-start.9
  45.0 0.9 %collective-permute-start.16 = (bf16[256,512]{1,0:T(8,128)(2,1)S(1)}, bf16[256,512]{1,0:T(8,128)(2,1)S(1)}, u32[]{:S(2)}, u32[]{:S(2)}) collective-permute-start(bf16[256,512]{1,0:T(8,128)(2,1)S(1)} %get-tuple-element.75), channel_id=1, source_target_pairs={{0,1},{1,0},{2,3},{3,2},{4,5},{5,4},{6,7},{7,6},{8,16},{9,17},{10,... | collective-permute-start | bytes 786440 | tf_op jit(solution)/shard_map/odd_step_2_right/ppermute | solution.py:621
  45.9 2.6 %collective-permute-done.10 = bf16[288,512]{1,0:T(8,128)(2,1)S(1)} collective-permute-done((bf16[288,512]{1,0:T(8,128)(2,1)S(1)}, bf16[288,512]{1,0:T(8,128)(2,1)S(1)}, u32[]{:S(2)}, u32[]{:S(2)}) %collective-permute-start.10) | collective-permute-done | bytes 294944 | tf_op jit(solution)/shard_map/even_step_1_left/ppermute | solution.py:610
  48.5 0.5 collective-permute-start.13
  49.0 0.1 add_convert_fusion
  49.1 1.3 %collective-permute-done.14 = bf16[256,512]{1,0:T(8,128)(2,1)S(1)} collective-permute-done((bf16[256,512]{1,0:T(8,128)(2,1)S(1)}, bf16[256,512]{1,0:T(8,128)(2,1)S(1)}, u32[]{:S(2)}, u32[]{:S(2)}) %collective-permute-start.14) | collective-permute-done | bytes 262176 | tf_op jit(solution)/shard_map/odd_step_1_right/ppermute | solution.py:621
  50.4 0.5 collective-permute-start.11
  50.9 0.1 fusion.6
  51.1 0.1 collective-permute-start.15
  51.1 4.9 %collective-permute-done.16 = bf16[256,512]{1,0:T(8,128)(2,1)S(1)} collective-permute-done((bf16[256,512]{1,0:T(8,128)(2,1)S(1)}, bf16[256,512]{1,0:T(8,128)(2,1)S(1)}, u32[]{:S(2)}, u32[]{:S(2)}) %collective-permute-start.16) | collective-permute-done | bytes 262176 | tf_op jit(solution)/shard_map/odd_step_2_right/ppermute | solution.py:621
  56.1 5.3 %collective-permute-done.11 = bf16[288,512]{1,0:T(8,128)(2,1)S(1)} collective-permute-done((bf16[288,512]{1,0:T(8,128)(2,1)S(1)}, bf16[288,512]{1,0:T(8,128)(2,1)S(1)}, u32[]{:S(2)}, u32[]{:S(2)}) %collective-permute-start.11) | collective-permute-done | bytes 294944 | tf_op jit(solution)/shard_map/odd_step_2_left/ppermute | solution.py:621
  61.4 1.8 %tail_left.1 = (f32[256,512]{1,0:T(8,128)S(1)}, f32[32,512]{1,0:T(8,128)S(1)}, f32[2,8,512]{2,1,0:T(8,128)S(1)}, f32[2,128,256]{2,1,0:T(8,128)S(1)}, f32[2,128,256]{2,1,0:T(8,128)S(1)}) custom-call(bf16[288,512]{1,0:T(8,128)(2,1)S(1)} %copy-done, bf16[288,512]{1,0:T(8,128)(2,1)S(1)} %collective-permute-done.4.a1, ...), custom_call_target="tpu_custom_call" | custom-call | flops 500000000 | bytes 4000000 | tf_op jit(solution)/shard_map/tail_left/pallas_call | solution.py:452
  63.3 1.8 %tail_right.1 = (f32[256,512]{1,0:T(8,128)S(1)}, bf16[2,128,512]{2,1,0:T(8,128)(2,1)S(1)}, f32[2,128,512]{2,1,0:T(8,128)S(1)}) custom-call(bf16[256,512]{1,0:T(8,128)(2,1)S(1)} %copy-done.1, bf16[256,512]{1,0:T(8,128)(2,1)S(1)} %collective-permute-done.13.b1, bf16[256,512]{1,0:T(8,128)(2,1)S(1)} %collective-permute-done.15.b2, ...), custom_call_target="tpu_custom_call" | custom-call | tf_op jit(solution)/shard_map/tail_right/pallas_call | solution.py:467
  65.0 0.1 collective-permute-start.17
  65.1 1.5 %collective-permute-done.17 = bf16[2,128,512]{2,1,0:T(8,128)(2,1)S(1)} collective-permute-done((bf16[2,128,512]{2,1,0:T(8,128)(2,1)S(1)}, bf16[2,128,512]{2,1,0:T(8,128)(2,1)S(1)}, u32[]{:S(2)}, u32[]{:S(2)}) %collective-permute-start.17) | collective-permute-done | bytes 262176 | tf_op jit(solution)/shard_map/ppermute | solution.py:479
  66.7 0.6 collective-permute-start.18
  67.3 1.3 %tail_image.1 = f32[512,512]{1,0:T(8,128)} custom-call(f32[256,512]{1,0:T(8,128)S(1)} %get-tuple-element.69.left, f32[256,512]{1,0:T(8,128)S(1)} %get-tuple-element.83.right), custom_call_target="tpu_custom_call" | custom-call | bytes 2000000 | tf_op jit(solution)/shard_map/tail_image/pallas_call | solution.py:482
  68.6 3.7 %collective-permute-done.18 = bf16[128,512]{1,0:T(8,128)(2,1)S(1)} collective-permute-done((bf16[128,512]{1,0:T(8,128)(2,1)S(1)}, bf16[128,512]{1,0:T(8,128)(2,1)S(1)}, u32[]{:S(2)}, u32[]{:S(2)}) %collective-permute-start.18) | collective-permute-done | bytes 131104 | tf_op jit(solution)/shard_map/ppermute | solution.py:480
  72.3 0.7 %fusion.8 = f32[128,512]{1,0:T(8,128)} fusion(f32[2,128,512]{2,1,0:T(8,128)S(1)} %convert_add_fusion.4, bf16[128,512]{1,0:T(8,128)(2,1)S(1)} %collective-permute-done.18), kind=kLoop, calls=%fused_computation.25 | loop fusion | flops 131072 | bytes 655360 | tf_op jit(solution)/shard_map/add | solution.py:491
  (31 shorter events, 0.2 us)
Async XLA Ops:
  6.6 11.1 %collective-permute-start.2 = (bf16[288,512]{1,0:T(8,128)(2,1)}, bf16[288,512]{1,0:T(8,128)(2,1)}, u32[]{:S(2)}, u32[]{:S(2)}) collective-permute-start(bf16[288,512]{1,0:T(8,128)(2,1)} %get-tuple-element.51), channel_id=1, source_target_pairs={{0,4},{4,0},{8,12},{12,8},{16,20},{20,16},{24,28},{28,24},{1,5},{5... | collective-permute-start | bytes 884744 | tf_op jit(solution)/shard_map/across_turn_0_of/ppermute | solution.py:549
  8.2 13.7 %collective-permute-start = (bf16[512,512]{1,0:T(8,128)(2,1)}, bf16[512,512]{1,0:T(8,128)(2,1)}, u32[]{:S(2)}, u32[]{:S(2)}) collective-permute-start(bf16[512,512]{1,0:T(8,128)(2,1)} %get-tuple-element.49), channel_id=1, source_target_pairs={{0,8},{4,12},{8,0},{12,4},{16,24},{20,28},{24,16},{28,20},{1,9},{5... | collective-permute-start | bytes 1572872 | tf_op jit(solution)/shard_map/even_step_0_right/ppermute | solution.py:538
  17.7 19.8 %copy-start.3 = (bf16[288,512]{1,0:T(8,128)(2,1)S(1)}, bf16[288,512]{1,0:T(8,128)(2,1)}, u32[]{:S(2)}) copy-start(bf16[288,512]{1,0:T(8,128)(2,1)} %get-tuple-element.61) | copy-start | bytes 884740
  17.7 21.5 %copy-start.5 = (bf16[512,512]{1,0:T(8,128)(2,1)S(1)}, bf16[512,512]{1,0:T(8,128)(2,1)}, u32[]{:S(2)}) copy-start(bf16[512,512]{1,0:T(8,128)(2,1)} %get-tuple-element.49) | copy-start | bytes 1572868
  17.7 24.5 %copy-start.9 = (bf16[288,512]{1,0:T(8,128)(2,1)S(1)}, bf16[288,512]{1,0:T(8,128)(2,1)}, u32[]{:S(2)}) copy-start(bf16[288,512]{1,0:T(8,128)(2,1)} %get-tuple-element.53) | copy-start | bytes 884740
  17.7 24.5 %copy-start.4 = (bf16[256,512]{1,0:T(8,128)(2,1)S(1)}, bf16[256,512]{1,0:T(8,128)(2,1)}, u32[]{:S(2)}) copy-start(bf16[256,512]{1,0:T(8,128)(2,1)} %get-tuple-element.62) | copy-start | bytes 786436
  17.7 24.5 %copy-start.8 = (bf16[256,512]{1,0:T(8,128)(2,1)S(1)}, bf16[256,512]{1,0:T(8,128)(2,1)}, u32[]{:S(2)}) copy-start(bf16[256,512]{1,0:T(8,128)(2,1)} %get-tuple-element.71) | copy-start | bytes 786436
  17.7 24.6 %copy-start.2 = (f32[1,25]{1,0:T(1,128)S(1)}, f32[1,25]{1,0:T(1,128)}, u32[]{:S(2)}) copy-start(f32[1,25]{1,0:T(1,128)} %det) | copy-start | bytes 304
  17.7 27.0 %copy-start.6 = (bf16[288,512]{1,0:T(8,128)(2,1)S(1)}, bf16[288,512]{1,0:T(8,128)(2,1)}, u32[]{:S(2)}) copy-start(bf16[288,512]{1,0:T(8,128)(2,1)} %get-tuple-element.54) | copy-start | bytes 884740
  17.8 10.2 %collective-permute-start.5 = (bf16[288,512]{1,0:T(8,128)(2,1)}, bf16[288,512]{1,0:T(8,128)(2,1)S(1)}, u32[]{:S(2)}, u32[]{:S(2)}) collective-permute-start(bf16[288,512]{1,0:T(8,128)(2,1)} %get-tuple-element.57), channel_id=1, source_target_pairs={{0,4},{4,0},{8,12},{12,8},{16,20},{20,16},{24,28},{28,24},{1,5},{5... | collective-permute-start | bytes 884744 | tf_op jit(solution)/shard_map/across_turn_1_of/ppermute | solution.py:549
  18.4 15.2 %collective-permute-start.3 = (bf16[256,512]{1,0:T(8,128)(2,1)}, bf16[256,512]{1,0:T(8,128)(2,1)S(1)}, u32[]{:S(2)}, u32[]{:S(2)}) collective-permute-start(bf16[256,512]{1,0:T(8,128)(2,1)} %get-tuple-element.52), channel_id=1, source_target_pairs={{0,4},{4,0},{8,12},{12,8},{16,20},{20,16},{24,28},{28,24},{1,5},{5... | collective-permute-start | bytes 786440 | tf_op jit(solution)/shard_map/across_turn_2_of/ppermute | solution.py:549
  21.0 14.8 %collective-permute-start.7 = (bf16[288,512]{1,0:T(8,128)(2,1)S(1)}, bf16[288,512]{1,0:T(8,128)(2,1)S(1)}, u32[]{:S(2)}, u32[]{:S(2)}) collective-permute-start(bf16[288,512]{1,0:T(8,128)(2,1)S(1)} %fusion), channel_id=1, source_target_pairs={{0,8},{4,12},{8,0},{12,4},{16,24},{20,28},{24,16},{28,20},{1,9},{5... | collective-permute-start | bytes 884744 | tf_op jit(solution)/shard_map/even_step_0_left/ppermute | solution.py:610
  23.1 27.8 %copy-start.7 = (bf16[256,512]{1,0:T(8,128)(2,1)S(1)}, bf16[256,512]{1,0:T(8,128)(2,1)}, u32[]{:S(2)}) copy-start(bf16[256,512]{1,0:T(8,128)(2,1)} %get-tuple-element.73) | copy-start | bytes 786436
  23.1 16.1 %collective-permute-start.1 = (bf16[256,512]{1,0:T(8,128)(2,1)S(1)}, bf16[256,512]{1,0:T(8,128)(2,1)S(1)}, u32[]{:S(2)}, u32[]{:S(2)}) collective-permute-start(bf16[256,512]{1,0:T(8,128)(2,1)S(1)} %select_convert_fusion.3), channel_id=1, source_target_pairs={{0,4},{4,0},{8,12},{12,8},{16,20},{20,16},{24,28},{28,24},{1,5},{5... | collective-permute-start | bytes 786440 | tf_op jit(solution)/shard_map/across_turn_3_of/ppermute | solution.py:549
  34.7 7.4 %collective-permute-start.12 = (bf16[256,512]{1,0:T(8,128)(2,1)S(1)}, bf16[256,512]{1,0:T(8,128)(2,1)S(1)}, u32[]{:S(2)}, u32[]{:S(2)}) collective-permute-start(bf16[256,512]{1,0:T(8,128)(2,1)S(1)} %select_convert_fusion.2), channel_id=1, source_target_pairs={{0,8},{4,12},{8,0},{12,4},{16,24},{20,28},{24,16},{28,20},{1,9},{5... | collective-permute-start | bytes 786440 | tf_op jit(solution)/shard_map/even_step_1_right/ppermute | solution.py:610
  35.3 9.4 %collective-permute-start.6 = (bf16[288,512]{1,0:T(8,128)(2,1)}, bf16[288,512]{1,0:T(8,128)(2,1)S(1)}, u32[]{:S(2)}, u32[]{:S(2)}) collective-permute-start(bf16[288,512]{1,0:T(8,128)(2,1)} %get-tuple-element.58), channel_id=1, source_target_pairs={{0,4},{4,0},{8,12},{12,8},{16,20},{20,16},{24,28},{28,24},{1,5},{5... | collective-permute-start | bytes 884744 | tf_op jit(solution)/shard_map/across_turn_4_of/ppermute | solution.py:549
  37.0 24.4 %copy-start = (bf16[288,512]{1,0:T(8,128)(2,1)S(1)}, bf16[288,512]{1,0:T(8,128)(2,1)}, u32[]{:S(2)}) copy-start(bf16[288,512]{1,0:T(8,128)(2,1)} %get-tuple-element.46.a0) | copy-start | bytes 884740
  37.0 7.8 %collective-permute-start.8 = (bf16[288,512]{1,0:T(8,128)(2,1)S(1)}, bf16[288,512]{1,0:T(8,128)(2,1)S(1)}, u32[]{:S(2)}, u32[]{:S(2)}) collective-permute-start(bf16[288,512]{1,0:T(8,128)(2,1)S(1)} %add_convert_fusion.2), channel_id=1, source_target_pairs={{0,1},{1,0},{2,3},{3,2},{4,5},{5,4},{6,7},{7,6},{8,16},{9,17},{10,... | collective-permute-start | bytes 884744 | tf_op jit(solution)/shard_map/odd_step_1_left/ppermute | solution.py:621
  37.5 10.9 %collective-permute-start.10 = (bf16[288,512]{1,0:T(8,128)(2,1)S(1)}, bf16[288,512]{1,0:T(8,128)(2,1)S(1)}, u32[]{:S(2)}, u32[]{:S(2)}) collective-permute-start(bf16[288,512]{1,0:T(8,128)(2,1)S(1)} %fusion.1), channel_id=1, source_target_pairs={{0,8},{4,12},{8,0},{12,4},{16,24},{20,28},{24,16},{28,20},{1,9},{5... | collective-permute-start | bytes 884744 | tf_op jit(solution)/shard_map/even_step_1_left/ppermute | solution.py:610
  40.3 10.1 %collective-permute-start.14 = (bf16[256,512]{1,0:T(8,128)(2,1)S(1)}, bf16[256,512]{1,0:T(8,128)(2,1)S(1)}, u32[]{:S(2)}, u32[]{:S(2)}) collective-permute-start(bf16[256,512]{1,0:T(8,128)(2,1)S(1)} %fusion.7), channel_id=1, source_target_pairs={{0,1},{1,0},{2,3},{3,2},{4,5},{5,4},{6,7},{7,6},{8,16},{9,17},{10,... | collective-permute-start | bytes 786440 | tf_op jit(solution)/shard_map/odd_step_1_right/ppermute | solution.py:621
  42.2 8.9 %collective-permute-start.4 = (bf16[288,512]{1,0:T(8,128)(2,1)S(1)}, bf16[288,512]{1,0:T(8,128)(2,1)S(1)}, u32[]{:S(2)}, u32[]{:S(2)}) collective-permute-start(bf16[288,512]{1,0:T(8,128)(2,1)S(1)} %copy-done.9), channel_id=1, source_target_pairs={{0,4},{4,0},{8,12},{12,8},{16,20},{20,16},{24,28},{28,24},{1,5},{5... | collective-permute-start | bytes 884744 | tf_op jit(solution)/shard_map/across_turn_5_of/ppermute | solution.py:549
  42.2 21.1 %copy-start.1 = (bf16[256,512]{1,0:T(8,128)(2,1)S(1)}, bf16[256,512]{1,0:T(8,128)(2,1)}, u32[]{:S(2)}) copy-start(bf16[256,512]{1,0:T(8,128)(2,1)} %get-tuple-element.70.b0) | copy-start | bytes 786436
  44.9 16.5 %collective-permute-start.9 = (bf16[288,512]{1,0:T(8,128)(2,1)S(1)}, bf16[288,512]{1,0:T(8,128)(2,1)S(1)}, u32[]{:S(2)}, u32[]{:S(2)}) collective-permute-start(bf16[288,512]{1,0:T(8,128)(2,1)S(1)} %add_convert_fusion.1), channel_id=1, source_target_pairs={{0,8},{4,12},{8,0},{12,4},{16,24},{20,28},{24,16},{28,20},{1,9},{5... | collective-permute-start | bytes 884744 | tf_op jit(solution)/shard_map/even_step_2_left/ppermute | solution.py:610
  45.0 11.0 %collective-permute-start.16 = (bf16[256,512]{1,0:T(8,128)(2,1)S(1)}, bf16[256,512]{1,0:T(8,128)(2,1)S(1)}, u32[]{:S(2)}, u32[]{:S(2)}) collective-permute-start(bf16[256,512]{1,0:T(8,128)(2,1)S(1)} %get-tuple-element.75), channel_id=1, source_target_pairs={{0,1},{1,0},{2,3},{3,2},{4,5},{5,4},{6,7},{7,6},{8,16},{9,17},{10,... | collective-permute-start | bytes 786440 | tf_op jit(solution)/shard_map/odd_step_2_right/ppermute | solution.py:621
  48.5 14.7 %collective-permute-start.13 = (bf16[256,512]{1,0:T(8,128)(2,1)S(1)}, bf16[256,512]{1,0:T(8,128)(2,1)S(1)}, u32[]{:S(2)}, u32[]{:S(2)}) collective-permute-start(bf16[256,512]{1,0:T(8,128)(2,1)S(1)} %get-tuple-element.72), channel_id=1, source_target_pairs={{0,4},{4,0},{8,12},{12,8},{16,20},{20,16},{24,28},{28,24},{1,5},{5... | collective-permute-start | bytes 786440 | tf_op jit(solution)/shard_map/across_turn_6_of/ppermute | solution.py:549
  50.4 10.9 %collective-permute-start.11 = (bf16[288,512]{1,0:T(8,128)(2,1)S(1)}, bf16[288,512]{1,0:T(8,128)(2,1)S(1)}, u32[]{:S(2)}, u32[]{:S(2)}) collective-permute-start(bf16[288,512]{1,0:T(8,128)(2,1)S(1)} %add_convert_fusion), channel_id=1, source_target_pairs={{0,1},{1,0},{2,3},{3,2},{4,5},{5,4},{6,7},{7,6},{8,16},{9,17},{10,... | collective-permute-start | bytes 884744 | tf_op jit(solution)/shard_map/odd_step_2_left/ppermute | solution.py:621
  51.1 12.2 %collective-permute-start.15 = (bf16[256,512]{1,0:T(8,128)(2,1)S(1)}, bf16[256,512]{1,0:T(8,128)(2,1)S(1)}, u32[]{:S(2)}, u32[]{:S(2)}) collective-permute-start(bf16[256,512]{1,0:T(8,128)(2,1)S(1)} %fusion.6), channel_id=1, source_target_pairs={{0,8},{4,12},{8,0},{12,4},{16,24},{20,28},{24,16},{28,20},{1,9},{5... | collective-permute-start | bytes 786440 | tf_op jit(solution)/shard_map/even_step_2_right/ppermute | solution.py:610
  65.0 1.6 %collective-permute-start.17 = (bf16[2,128,512]{2,1,0:T(8,128)(2,1)S(1)}, bf16[2,128,512]{2,1,0:T(8,128)(2,1)S(1)}, u32[]{:S(2)}, u32[]{:S(2)}) collective-permute-start(bf16[2,128,512]{2,1,0:T(8,128)(2,1)S(1)} %get-tuple-element.82), channel_id=1, source_target_pairs={{0,1},{1,0},{2,3},{3,2},{4,5},{5,4},{6,7},{7,6},{8,9},{9,8},{10,11... | collective-permute-start | bytes 786440 | tf_op jit(solution)/shard_map/ppermute | solution.py:479
  66.7 5.6 %collective-permute-start.18 = (bf16[128,512]{1,0:T(8,128)(2,1)S(1)}, bf16[128,512]{1,0:T(8,128)(2,1)S(1)}, u32[]{:S(2)}, u32[]{:S(2)}) collective-permute-start(bf16[128,512]{1,0:T(8,128)(2,1)S(1)} %fusion.9), channel_id=1, source_target_pairs={{0,2},{1,3},{2,0},{3,1},{4,6},{5,7},{6,4},{7,5},{8,10},{9,11},{10,... | collective-permute-start | bytes 393224 | tf_op jit(solution)/shard_map/ppermute | solution.py:480

commit v4 on v3

--- a/solution.py
+++ b/solution.py
@@ -593,13 +593,22 @@
     for t in range(last):
         for c in range(2):
             side = "left" if c == 0 else "right"
+            if (t, c) == (1, 1):
+                came[1, 1], *_ = lax.optimization_barrier((came[1, 1], *earlier))
             send = None if (t, c) == (0, 1) else step(t, 0, c)
+            if (t, c) == (2, 0):
+                odds[0], _ = lax.optimization_barrier((odds[0], sent_odd))
             if t > 1:
                 send = send + masked(odds[c])
+            if (t, c) == (1, 1):
+                ahead = (step(2, 1, 0) + evens[0].astype(f32)).astype(bf16)
+                came[last - 1, 1], *_ = lax.optimization_barrier((came[last - 1, 1], ahead, odds[0]))
             send_odd = step(t, 1, c) if t else None
             if (t, c) == (2, 1):
                 send, _ = lax.optimization_barrier((send, came[last, 0]))
-            if t and (t, c) != (1, 1):
+            if (t, c) == (2, 0):
+                send_odd = ahead
+            elif t and (t, c) != (1, 1):
                 send_odd = send_odd + evens[c].astype(f32)
             if (t, c) == (1, 1):
                 passing, _ = lax.optimization_barrier((sends[3], got[1]))
@@ -609,16 +618,24 @@
                     send_even[c] = send.astype(bf16)
                     evens[c] = lax.ppermute(send_even[c], "patch", even)
             if (t, c) == (1, 1):
+                evens[c], *_ = lax.optimization_barrier((evens[c], ahead, odds[0]))
                 passed = jnp.where(place_in(beside_ends), 0.0, evens[c].astype(f32))
-                across_y((sends[-1].astype(f32) + passed).astype(bf16))
-                came[last, 1] = got[-1]
+                final = (sends[-1].astype(f32) + passed).astype(bf16)
             if (t, c) == (1, 1):
                 det_taps, _ = lax.optimization_barrier((det_taps, evens[c]))
             if (t, c) == (2, 1):
                 send_odd, _ = lax.optimization_barrier((send_odd.astype(bf16), send_even[0]))
+            if (t, c) == (1, 0):
+                earlier = send_even[0], send_odd.astype(bf16)
             if t:
+                sent_odd = send_odd.astype(bf16)
                 with jax.named_scope(f"odd_step_{t}_{side}"):
                     odds[c] = lax.ppermute(send_odd.astype(bf16), ("patch", "band"), odd)
+            if (t, c) == (2, 1):
+                final, _ = lax.optimization_barrier((final, send_even[1]))
+                across_y(final)
+                came[last, 1] = got[-1]
+    odds[1], _ = lax.optimization_barrier((odds[1], evens[0]))
     for c in range(2):
         odds[c] = masked(odds[c]).astype(bf16)
     parts = [(kept[last][c], came[last, c], evens[c], odds[c]) for c in range(2)]

time: 73.3 us -> 71.8 us (0.980)
  the two profiles are of different devices: /device:TPU:18 before, /device:TPU:0 now
where the time goes in v4:
time: 71.8 us; the launch traced here: 71.5 us
  waiting for transfers between devices  21.4 us (30%)
  Pallas kernels  19.5 us (27%)
  starting transfers between devices  19.4 us (27%)
  other arithmetic  9.65 us (13%)
  between operations  1.55 us (2%)
    ppermute x7, waiting for transfers between devices, across_y(): got.append(lax.ppermute(send, 'patch', across))  13 us
    ppermute x7, starting transfers between devices, across_y(): got.append(lax.ppermute(send, 'patch', across))  8.5 us
    ppermute x5, starting transfers between devices, local(): evens[c] = lax.ppermute(send_even[c], 'patch', even)  7.48 us
    pallas_call x1, Pallas kernels, match_blocks(): pl.pallas_call(lambda *refs: rest_kernel(npatch, *refs), out_shape=[whole...  7.21 us
    pallas_call x1, Pallas kernels, match_blocks(): pl.pallas_call(lambda *refs: first_kernel(npatch, *refs), out_shape=[part...  5.98 us
    convert_element_type x4, other arithmetic, local(): send_even[c] = send.astype(bf16)  3.48 us
    ppermute x1, waiting for transfers between devices, finish(): lax.ppermute(pair[1].astype(bf16), 'band', [(i, i ^ 2) for i in range(4)])  2.72 us
    ppermute x1, waiting for transfers between devices, local(): direct = lax.ppermute(both, 'patch', even)  2.29 us
  transfers between devices with their start and end apart: 19, of which 9 were waited for; matrix products, arithmetic and copies ran while one was open for 12% of the time, Pallas kernels for 16%

profile of v4, /device:TPU:0, one launch (start us, length us, event | category | flops | bytes accessed | tf_op | source)
XLA Modules:
  0.0 71.5 jit_solution(12099259797024454288)
XLA Ops:
  0.6 6.0 %match_first.1 = (bf16[288,512]{1,0:T(8,128)(2,1)}, bf16[288,512]{1,0:T(8,128)(2,1)}, bf16[512,512]{1,0:T(8,128)(2,1)}, bf16[2,512,512]{2,1,0:T(8,128)(2,1)}, bf...) custom-call(s32[1,32]{1,0:T(1,128)} %refs_0_.3, s32[1,32]{1,0:T(1,128)} %refs_1_.3, bf16[1,32]{1,0:T(2,128)(2,1)} %refs_2_.3, ...), custom_call_target="tpu_custom_call" | custom-call | tf_op jit(solution)/shard_map/match_first/pallas_call | solution.py:287
  6.6 3.0 %collective-permute-start.2 = (bf16[288,512]{1,0:T(8,128)(2,1)}, bf16[288,512]{1,0:T(8,128)(2,1)}, u32[]{:S(2)}, u32[]{:S(2)}) collective-permute-start(bf16[288,512]{1,0:T(8,128)(2,1)} %get-tuple-element.57), channel_id=1, source_target_pairs={{0,4},{4,0},{8,12},{12,8},{16,20},{20,16},{24,28},{28,24},{1,5},{5... | collective-permute-start | bytes 884744 | tf_op jit(solution)/shard_map/across_turn_0_of/ppermute | solution.py:549
  9.6 1.6 %collective-permute-start = (bf16[512,512]{1,0:T(8,128)(2,1)}, bf16[512,512]{1,0:T(8,128)(2,1)}, u32[]{:S(2)}, u32[]{:S(2)}) collective-permute-start(bf16[512,512]{1,0:T(8,128)(2,1)} %get-tuple-element.55), channel_id=1, source_target_pairs={{0,8},{4,12},{8,0},{12,4},{16,24},{20,28},{24,16},{28,20},{1,9},{5... | collective-permute-start | bytes 1572872 | tf_op jit(solution)/shard_map/even_step_0_right/ppermute | solution.py:538
  11.2 7.2 %match_rest.1 = (bf16[288,512]{1,0:T(8,128)(2,1)}, bf16[256,512]{1,0:T(8,128)(2,1)}, bf16[256,512]{1,0:T(8,128)(2,1)}, bf16[288,512]{1,0:T(8,128)(2,1)}, bf16[28...) custom-call(s32[1,32]{1,0:T(1,128)} %refs_0_.3, ...), custom_call_target="tpu_custom_call" | custom-call | flops 2000000000 | bytes 8000000 | tf_op jit(solution)/shard_map/match_rest/pallas_call | solution.py:309
  18.5 0.6 collective-permute-start.5
  19.1 1.2 %fusion = bf16[288,512]{1,0:T(8,128)(2,1)S(1)} fusion(bf16[288,512]{1,0:T(8,128)(2,1)} %collective-permute-done.2, bf16[288,512]{1,0:T(8,128)(2,1)} %get-tuple-element.65), kind=kLoop, calls=%fused_computation.10 | loop fusion | flops 589824 | bytes 884736 | tf_op jit(solution)/shard_map/even_step_0_left/convert_element_type | solution.py:618
  20.3 1.3 %collective-permute-start.7 = (bf16[288,512]{1,0:T(8,128)(2,1)S(1)}, bf16[288,512]{1,0:T(8,128)(2,1)S(1)}, u32[]{:S(2)}, u32[]{:S(2)}) collective-permute-start(bf16[288,512]{1,0:T(8,128)(2,1)S(1)} %fusion), channel_id=1, source_target_pairs={{0,8},{4,12},{8,0},{12,4},{16,24},{20,28},{24,16},{28,20},{1,9},{5... | collective-permute-start | bytes 884744 | tf_op jit(solution)/shard_map/even_step_0_left/ppermute | solution.py:619
  21.5 0.7 %collective-permute-start.3 = (bf16[256,512]{1,0:T(8,128)(2,1)}, bf16[256,512]{1,0:T(8,128)(2,1)S(1)}, u32[]{:S(2)}, u32[]{:S(2)}) collective-permute-start(bf16[256,512]{1,0:T(8,128)(2,1)} %get-tuple-element.58), channel_id=1, source_target_pairs={{0,4},{4,0},{8,12},{12,8},{16,20},{20,16},{24,28},{28,24},{1,5},{5... | collective-permute-start | bytes 786440 | tf_op jit(solution)/shard_map/across_turn_2_of/ppermute | solution.py:549
  22.3 2.3 %collective-permute-done = bf16[512,512]{1,0:T(8,128)(2,1)} collective-permute-done((bf16[512,512]{1,0:T(8,128)(2,1)}, bf16[512,512]{1,0:T(8,128)(2,1)}, u32[]{:S(2)}, u32[]{:S(2)}) %collective-permute-start) | collective-permute-done | bytes 524320 | tf_op jit(solution)/shard_map/even_step_0_right/ppermute | solution.py:538
  24.6 1.2 %select_convert_fusion.3 = bf16[256,512]{1,0:T(8,128)(2,1)S(1)} fusion(bf16[256,512]{1,0:T(8,128)(2,1)} %get-tuple-element.72, bf16[512,512]{1,0:T(8,128)(2,1)} %collective-permute-done, bf16[512,512]{1,0:T(8,128)(2,1)} %get-tuple-element.55, pred[]{:T(512)S(6)} %or.5, pred[]{:T(512)S(6)} %or.4), kind=kLoop, calls=%fused_computation.22 | loop fusion | flops 917504 | bytes 1048578 | tf_op jit(solution)/shard_map/convert_element_type | solution.py:555
  25.8 0.0 copy-start.2
  25.8 0.1 collective-permute-start.1
  25.9 2.8 %collective-permute-done.5 = bf16[288,512]{1,0:T(8,128)(2,1)S(1)} collective-permute-done((bf16[288,512]{1,0:T(8,128)(2,1)}, bf16[288,512]{1,0:T(8,128)(2,1)S(1)}, u32[]{:S(2)}, u32[]{:S(2)}) %collective-permute-start.5) | collective-permute-done | bytes 294944 | tf_op jit(solution)/shard_map/across_turn_1_of/ppermute | solution.py:549
  28.7 1.0 %fusion.1 = bf16[288,512]{1,0:T(8,128)(2,1)S(1)} fusion(bf16[288,512]{1,0:T(8,128)(2,1)S(1)} %collective-permute-done.5, bf16[288,512]{1,0:T(8,128)(2,1)} %get-tuple-element.67), kind=kLoop, calls=%fused_computation.11 | loop fusion | flops 589824 | bytes 884736 | tf_op jit(solution)/shard_map/even_step_1_left/convert_element_type | solution.py:618
  29.8 0.5 collective-permute-start.9
  30.3 1.2 %add_convert_fusion.2 = bf16[288,512]{1,0:T(8,128)(2,1)S(1)} fusion(bf16[288,512]{1,0:T(8,128)(2,1)S(1)} %collective-permute-done.7, bf16[288,512]{1,0:T(8,128)(2,1)} %collective-permute-done.2, bf16[288,512]{1,0:T(8,128)(2,1)} %get-tuple-element.65), kind=kLoop, calls=%fused_computation.8 | loop fusion | flops 884736 | bytes 1179648 | tf_op jit(solution)/shard_map/odd_step_1_left/convert_element_type | solution.py:633
  31.5 0.1 collective-permute-start.8
  31.5 2.8 %collective-permute-done.3 = bf16[256,512]{1,0:T(8,128)(2,1)S(1)} collective-permute-done((bf16[256,512]{1,0:T(8,128)(2,1)}, bf16[256,512]{1,0:T(8,128)(2,1)S(1)}, u32[]{:S(2)}, u32[]{:S(2)}) %collective-permute-start.3) | collective-permute-done | bytes 262176 | tf_op jit(solution)/shard_map/across_turn_2_of/ppermute | solution.py:549
  34.3 1.1 %select_convert_fusion.2 = bf16[256,512]{1,0:T(8,128)(2,1)S(1)} fusion(bf16[256,512]{1,0:T(8,128)(2,1)} %get-tuple-element.72, bf16[256,512]{1,0:T(8,128)(2,1)S(1)} %collective-permute-done.3, bf16[256,512]{1,0:T(8,128)(2,1)} %get-tuple-element.70, pred[]{:T(512)S(6)} %or.4), kind=kLoop, calls=%fused_computation.20 | loop fusion | flops 786432 | bytes 1048577 | tf_op jit(solution)/shard_map/even_step_1_right/convert_element_type | solution.py:618
  35.5 0.5 collective-permute-start.12
  36.0 1.3 %collective-permute-start.6 = (bf16[288,512]{1,0:T(8,128)(2,1)S(1)}, bf16[288,512]{1,0:T(8,128)(2,1)S(1)}, u32[]{:S(2)}, u32[]{:S(2)}) collective-permute-start(bf16[288,512]{1,0:T(8,128)(2,1)S(1)} %copy-done.9), channel_id=1, source_target_pairs={{0,4},{4,0},{8,12},{12,8},{16,20},{20,16},{24,28},{28,24},{1,5},{5... | collective-permute-start | bytes 884744 | tf_op jit(solution)/shard_map/across_turn_4_of/ppermute | solution.py:549
  37.3 2.7 %collective-permute-done.1 = bf16[256,512]{1,0:T(8,128)(2,1)S(1)} collective-permute-done((bf16[256,512]{1,0:T(8,128)(2,1)S(1)}, bf16[256,512]{1,0:T(8,128)(2,1)S(1)}, u32[]{:S(2)}, u32[]{:S(2)}) %collective-permute-start.1) | collective-permute-done | bytes 262176 | tf_op jit(solution)/shard_map/across_turn_3_of/ppermute | solution.py:549
  40.0 0.2 collective-permute-start.4
  40.2 0.1 add_convert_fusion.1
  40.3 0.1 collective-permute-start.11
  40.4 1.8 %collective-permute-done.12 = bf16[256,512]{1,0:T(8,128)(2,1)S(1)} collective-permute-done((bf16[256,512]{1,0:T(8,128)(2,1)S(1)}, bf16[256,512]{1,0:T(8,128)(2,1)S(1)}, u32[]{:S(2)}, u32[]{:S(2)}) %collective-permute-start.12) | collective-permute-done | bytes 262176 | tf_op jit(solution)/shard_map/even_step_1_right/ppermute | solution.py:619
  42.2 1.8 %fusion.2 = bf16[256,512]{1,0:T(8,128)(2,1)} fusion(bf16[256,512]{1,0:T(8,128)(2,1)S(1)} %collective-permute-done.1, bf16[512,512]{1,0:T(8,128)(2,1)} %collective-permute-done, bf16[512,512]{1,0:T(8,128)(2,1)S(1)} %copy-done.5, pred[]{:T(512)S(6)} %or.5), kind=kLoop, calls=%fused_computation.12 | loop fusion | flops 917504 | bytes 1048577 | tf_op jit(solution)/shard_map/convert_element_type | solution.py:631
  44.0 2.3 %collective-permute-done.6 = bf16[288,512]{1,0:T(8,128)(2,1)S(1)} collective-permute-done((bf16[288,512]{1,0:T(8,128)(2,1)S(1)}, bf16[288,512]{1,0:T(8,128)(2,1)S(1)}, u32[]{:S(2)}, u32[]{:S(2)}) %collective-permute-start.6) | collective-permute-done | bytes 294944 | tf_op jit(solution)/shard_map/across_turn_4_of/ppermute | solution.py:549
  46.3 0.1 add_convert_fusion
  46.4 1.3 %collective-permute-start.10 = (bf16[288,512]{1,0:T(8,128)(2,1)S(1)}, bf16[288,512]{1,0:T(8,128)(2,1)S(1)}, u32[]{:S(2)}, u32[]{:S(2)}) collective-permute-start(bf16[288,512]{1,0:T(8,128)(2,1)S(1)} %add_convert_fusion), channel_id=1, source_target_pairs={{0,8},{4,12},{8,0},{12,4},{16,24},{20,28},{24,16},{28,20},{1,9},{5... | collective-permute-start | bytes 884744 | tf_op jit(solution)/shard_map/even_step_2_left/ppermute | solution.py:619
  47.7 0.9 %fusion.7 = (bf16[256,512]{1,0:T(8,128)(2,1)}, bf16[256,512]{1,0:T(8,128)(2,1)S(1)}) fusion(bf16[256,512]{1,0:T(8,128)(2,1)S(1)} %collective-permute-done.12, bf16[256,512]{1,0:T(8,128)(2,1)S(1)} %collective-permute-done.3, bf16[256,512]{1,0:T(8,128)(2,1)S(1)} %copy-done.4, pred[]{:T(512)S(6)} %or.5, bf16[256,512]{1,0:T(8,128)(2,1)S(1)} %copy-done.8), kind=kLoop, calls=%fused_computation.17 | loop fusion | flops 1310720 | bytes 1572865 | tf_op jit(solution)/shard_map/convert_element_type | solution.py:627
  49.2 1.5 %tables.1 = (bf16[256,288]{1,0:T(8,128)(2,1)S(1)}, bf16[256,288]{1,0:T(8,128)(2,1)S(1)}, bf16[512,512]{1,0:T(8,128)(2,1)S(1)}, bf16[512,512]{1,0:T(8,128)(2,1)S(1)}) custom-call(f32[1,25]{1,0:T(1,128)S(1)} %copy-done.2), custom_call_target="tpu_custom_call" | custom-call | flops 20000000 | bytes 2000000 | tf_op jit(solution)/shard_map/tables/pallas_call | solution.py:428
  50.7 0.0 collective-permute-done.13
  50.7 0.1 fusion.4
  50.9 0.0 collective-permute-done.4.a1
  50.9 3.9 %collective-permute-start.15 = (bf16[256,512]{1,0:T(8,128)(2,1)S(1)}, bf16[256,512]{1,0:T(8,128)(2,1)S(1)}, u32[]{:S(2)}, u32[]{:S(2)}) collective-permute-start(bf16[256,512]{1,0:T(8,128)(2,1)S(1)} %fusion.4), channel_id=1, source_target_pairs={{0,8},{4,12},{8,0},{12,4},{16,24},{20,28},{24,16},{28,20},{1,9},{5... | collective-permute-start | bytes 786440 | tf_op jit(solution)/shard_map/even_step_2_right/ppermute | solution.py:619
  54.8 2.6 %collective-permute-start.14 = (bf16[256,512]{1,0:T(8,128)(2,1)S(1)}, bf16[256,512]{1,0:T(8,128)(2,1)S(1)}, u32[]{:S(2)}, u32[]{:S(2)}) collective-permute-start(bf16[256,512]{1,0:T(8,128)(2,1)S(1)} %get-tuple-element.85), channel_id=1, source_target_pairs={{0,4},{4,0},{8,12},{12,8},{16,20},{20,16},{24,28},{28,24},{1,5},{5... | collective-permute-start | bytes 786440 | tf_op jit(solution)/shard_map/across_turn_6_of/ppermute | solution.py:549
  57.4 0.1 select_convert_fusion.a3
  57.4 1.8 %tail_left.1 = (f32[256,512]{1,0:T(8,128)S(1)}, f32[32,512]{1,0:T(8,128)S(1)}, f32[2,8,512]{2,1,0:T(8,128)S(1)}, f32[2,128,256]{2,1,0:T(8,128)S(1)}, f32[2,128,256]{2,1,0:T(8,128)S(1)}) custom-call(bf16[288,512]{1,0:T(8,128)(2,1)S(1)} %copy-done, bf16[288,512]{1,0:T(8,128)(2,1)S(1)} %collective-permute-done.4.a1, ...), custom_call_target="tpu_custom_call" | custom-call | flops 500000000 | bytes 4000000 | tf_op jit(solution)/shard_map/tail_left/pallas_call | solution.py:452
  59.3 2.4 %collective-permute-done.14.b1 = bf16[256,512]{1,0:T(8,128)(2,1)S(1)} collective-permute-done((bf16[256,512]{1,0:T(8,128)(2,1)S(1)}, bf16[256,512]{1,0:T(8,128)(2,1)S(1)}, u32[]{:S(2)}, u32[]{:S(2)}) %collective-permute-start.14) | collective-permute-done | bytes 262176 | tf_op jit(solution)/shard_map/across_turn_6_of/ppermute | solution.py:549
  61.7 1.7 %tail_right.1 = (f32[256,512]{1,0:T(8,128)S(1)}, bf16[2,128,512]{2,1,0:T(8,128)(2,1)S(1)}, f32[2,128,512]{2,1,0:T(8,128)S(1)}) custom-call(bf16[256,512]{1,0:T(8,128)(2,1)S(1)} %copy-done.1, bf16[256,512]{1,0:T(8,128)(2,1)S(1)} %collective-permute-done.14.b1, bf16[256,512]{1,0:T(8,128)(2,1)S(1)} %collective-permute-done.15.b2, ...), custom_call_target="tpu_custom_call" | custom-call | tf_op jit(solution)/shard_map/tail_right/pallas_call | solution.py:467
  63.4 0.1 collective-permute-start.17
  63.5 1.5 %collective-permute-done.17 = bf16[2,128,512]{2,1,0:T(8,128)(2,1)S(1)} collective-permute-done((bf16[2,128,512]{2,1,0:T(8,128)(2,1)S(1)}, bf16[2,128,512]{2,1,0:T(8,128)(2,1)S(1)}, u32[]{:S(2)}, u32[]{:S(2)}) %collective-permute-start.17) | collective-permute-done | bytes 262176 | tf_op jit(solution)/shard_map/ppermute | solution.py:479
  65.0 0.1 convert_add_fusion.4
  65.1 1.6 %collective-permute-start.18 = (bf16[128,512]{1,0:T(8,128)(2,1)S(1)}, bf16[128,512]{1,0:T(8,128)(2,1)S(1)}, u32[]{:S(2)}, u32[]{:S(2)}) collective-permute-start(bf16[128,512]{1,0:T(8,128)(2,1)S(1)} %fusion.9), channel_id=1, source_target_pairs={{0,2},{1,3},{2,0},{3,1},{4,6},{5,7},{6,4},{7,5},{8,10},{9,11},{10,... | collective-permute-start | bytes 393224 | tf_op jit(solution)/shard_map/ppermute | solution.py:480
  66.7 1.3 %tail_image.1 = f32[512,512]{1,0:T(8,128)} custom-call(f32[256,512]{1,0:T(8,128)S(1)} %get-tuple-element.79.left, f32[256,512]{1,0:T(8,128)S(1)} %get-tuple-element.95.right), custom_call_target="tpu_custom_call" | custom-call | bytes 2000000 | tf_op jit(solution)/shard_map/tail_image/pallas_call | solution.py:482
  68.0 2.7 %collective-permute-done.18 = bf16[128,512]{1,0:T(8,128)(2,1)S(1)} collective-permute-done((bf16[128,512]{1,0:T(8,128)(2,1)S(1)}, bf16[128,512]{1,0:T(8,128)(2,1)S(1)}, u32[]{:S(2)}, u32[]{:S(2)}) %collective-permute-start.18) | collective-permute-done | bytes 131104 | tf_op jit(solution)/shard_map/ppermute | solution.py:480
  70.7 0.7 %fusion.8 = f32[128,512]{1,0:T(8,128)} fusion(f32[2,128,512]{2,1,0:T(8,128)S(1)} %convert_add_fusion.4, bf16[128,512]{1,0:T(8,128)(2,1)S(1)} %collective-permute-done.18), kind=kLoop, calls=%fused_computation.25 | loop fusion | flops 131072 | bytes 655360 | tf_op jit(solution)/shard_map/add | solution.py:491
  (31 shorter events, 0.1 us)
Async XLA Ops:
  6.6 11.9 %collective-permute-start.2 = (bf16[288,512]{1,0:T(8,128)(2,1)}, bf16[288,512]{1,0:T(8,128)(2,1)}, u32[]{:S(2)}, u32[]{:S(2)}) collective-permute-start(bf16[288,512]{1,0:T(8,128)(2,1)} %get-tuple-element.57), channel_id=1, source_target_pairs={{0,4},{4,0},{8,12},{12,8},{16,20},{20,16},{24,28},{28,24},{1,5},{5... | collective-permute-start | bytes 884744 | tf_op jit(solution)/shard_map/across_turn_0_of/ppermute | solution.py:549
  9.6 14.9 %collective-permute-start = (bf16[512,512]{1,0:T(8,128)(2,1)}, bf16[512,512]{1,0:T(8,128)(2,1)}, u32[]{:S(2)}, u32[]{:S(2)}) collective-permute-start(bf16[512,512]{1,0:T(8,128)(2,1)} %get-tuple-element.55), channel_id=1, source_target_pairs={{0,8},{4,12},{8,0},{12,4},{16,24},{20,28},{24,16},{28,20},{1,9},{5... | collective-permute-start | bytes 1572872 | tf_op jit(solution)/shard_map/even_step_0_right/ppermute | solution.py:538
  18.4 17.5 %copy-start.9 = (bf16[288,512]{1,0:T(8,128)(2,1)S(1)}, bf16[288,512]{1,0:T(8,128)(2,1)}, u32[]{:S(2)}) copy-start(bf16[288,512]{1,0:T(8,128)(2,1)} %get-tuple-element.64) | copy-start | bytes 884740
  18.5 21.7 %copy-start.3 = (bf16[288,512]{1,0:T(8,128)(2,1)S(1)}, bf16[288,512]{1,0:T(8,128)(2,1)}, u32[]{:S(2)}) copy-start(bf16[288,512]{1,0:T(8,128)(2,1)} %get-tuple-element.67) | copy-start | bytes 884740
  18.5 23.7 %copy-start.5 = (bf16[512,512]{1,0:T(8,128)(2,1)S(1)}, bf16[512,512]{1,0:T(8,128)(2,1)}, u32[]{:S(2)}) copy-start(bf16[512,512]{1,0:T(8,128)(2,1)} %get-tuple-element.55) | copy-start | bytes 1572868
  18.5 27.8 %copy-start.6 = (bf16[288,512]{1,0:T(8,128)(2,1)S(1)}, bf16[288,512]{1,0:T(8,128)(2,1)}, u32[]{:S(2)}) copy-start(bf16[288,512]{1,0:T(8,128)(2,1)} %get-tuple-element.60) | copy-start | bytes 884740
  18.5 10.2 %collective-permute-start.5 = (bf16[288,512]{1,0:T(8,128)(2,1)}, bf16[288,512]{1,0:T(8,128)(2,1)S(1)}, u32[]{:S(2)}, u32[]{:S(2)}) collective-permute-start(bf16[288,512]{1,0:T(8,128)(2,1)} %get-tuple-element.63), channel_id=1, source_target_pairs={{0,4},{4,0},{8,12},{12,8},{16,20},{20,16},{24,28},{28,24},{1,5},{5... | collective-permute-start | bytes 884744 | tf_op jit(solution)/shard_map/across_turn_1_of/ppermute | solution.py:549
  19.1 28.6 %copy-start.4 = (bf16[256,512]{1,0:T(8,128)(2,1)S(1)}, bf16[256,512]{1,0:T(8,128)(2,1)}, u32[]{:S(2)}) copy-start(bf16[256,512]{1,0:T(8,128)(2,1)} %get-tuple-element.70) | copy-start | bytes 786436
  19.1 28.6 %copy-start.8 = (bf16[256,512]{1,0:T(8,128)(2,1)S(1)}, bf16[256,512]{1,0:T(8,128)(2,1)}, u32[]{:S(2)}) copy-start(bf16[256,512]{1,0:T(8,128)(2,1)} %get-tuple-element.81) | copy-start | bytes 786436
  20.3 10.0 %collective-permute-start.7 = (bf16[288,512]{1,0:T(8,128)(2,1)S(1)}, bf16[288,512]{1,0:T(8,128)(2,1)S(1)}, u32[]{:S(2)}, u32[]{:S(2)}) collective-permute-start(bf16[288,512]{1,0:T(8,128)(2,1)S(1)} %fusion), channel_id=1, source_target_pairs={{0,8},{4,12},{8,0},{12,4},{16,24},{20,28},{24,16},{28,20},{1,9},{5... | collective-permute-start | bytes 884744 | tf_op jit(solution)/shard_map/even_step_0_left/ppermute | solution.py:619
  21.5 12.8 %collective-permute-start.3 = (bf16[256,512]{1,0:T(8,128)(2,1)}, bf16[256,512]{1,0:T(8,128)(2,1)S(1)}, u32[]{:S(2)}, u32[]{:S(2)}) collective-permute-start(bf16[256,512]{1,0:T(8,128)(2,1)} %get-tuple-element.58), channel_id=1, source_target_pairs={{0,4},{4,0},{8,12},{12,8},{16,20},{20,16},{24,28},{28,24},{1,5},{5... | collective-permute-start | bytes 786440 | tf_op jit(solution)/shard_map/across_turn_2_of/ppermute | solution.py:549
  25.8 23.4 %copy-start.2 = (f32[1,25]{1,0:T(1,128)S(1)}, f32[1,25]{1,0:T(1,128)}, u32[]{:S(2)}) copy-start(f32[1,25]{1,0:T(1,128)} %det) | copy-start | bytes 304
  25.8 24.9 %copy-start.7 = (bf16[256,512]{1,0:T(8,128)(2,1)S(1)}, bf16[256,512]{1,0:T(8,128)(2,1)}, u32[]{:S(2)}) copy-start(bf16[256,512]{1,0:T(8,128)(2,1)} %get-tuple-element.82) | copy-start | bytes 786436
  25.8 14.1 %collective-permute-start.1 = (bf16[256,512]{1,0:T(8,128)(2,1)S(1)}, bf16[256,512]{1,0:T(8,128)(2,1)S(1)}, u32[]{:S(2)}, u32[]{:S(2)}) collective-permute-start(bf16[256,512]{1,0:T(8,128)(2,1)S(1)} %select_convert_fusion.3), channel_id=1, source_target_pairs={{0,4},{4,0},{8,12},{12,8},{16,20},{20,16},{24,28},{28,24},{1,5},{5... | collective-permute-start | bytes 786440 | tf_op jit(solution)/shard_map/across_turn_3_of/ppermute | solution.py:549
  29.8 27.7 %copy-start = (bf16[288,512]{1,0:T(8,128)(2,1)S(1)}, bf16[288,512]{1,0:T(8,128)(2,1)}, u32[]{:S(2)}) copy-start(bf16[288,512]{1,0:T(8,128)(2,1)} %get-tuple-element.52.a0) | copy-start | bytes 884740
  29.8 10.4 %collective-permute-start.9 = (bf16[288,512]{1,0:T(8,128)(2,1)S(1)}, bf16[288,512]{1,0:T(8,128)(2,1)S(1)}, u32[]{:S(2)}, u32[]{:S(2)}) collective-permute-start(bf16[288,512]{1,0:T(8,128)(2,1)S(1)} %fusion.1), channel_id=1, source_target_pairs={{0,8},{4,12},{8,0},{12,4},{16,24},{20,28},{24,16},{28,20},{1,9},{5... | collective-permute-start | bytes 884744 | tf_op jit(solution)/shard_map/even_step_1_left/ppermute | solution.py:619
  31.5 10.7 %collective-permute-start.8 = (bf16[288,512]{1,0:T(8,128)(2,1)S(1)}, bf16[288,512]{1,0:T(8,128)(2,1)S(1)}, u32[]{:S(2)}, u32[]{:S(2)}) collective-permute-start(bf16[288,512]{1,0:T(8,128)(2,1)S(1)} %add_convert_fusion.2), channel_id=1, source_target_pairs={{0,1},{1,0},{2,3},{3,2},{4,5},{5,4},{6,7},{7,6},{8,16},{9,17},{10,... | collective-permute-start | bytes 884744 | tf_op jit(solution)/shard_map/odd_step_1_left/ppermute | solution.py:633
  35.5 6.7 %collective-permute-start.12 = (bf16[256,512]{1,0:T(8,128)(2,1)S(1)}, bf16[256,512]{1,0:T(8,128)(2,1)S(1)}, u32[]{:S(2)}, u32[]{:S(2)}) collective-permute-start(bf16[256,512]{1,0:T(8,128)(2,1)S(1)} %select_convert_fusion.2), channel_id=1, source_target_pairs={{0,8},{4,12},{8,0},{12,4},{16,24},{20,28},{24,16},{28,20},{1,9},{5... | collective-permute-start | bytes 786440 | tf_op jit(solution)/shard_map/even_step_1_right/ppermute | solution.py:619
  36.0 10.3 %collective-permute-start.6 = (bf16[288,512]{1,0:T(8,128)(2,1)S(1)}, bf16[288,512]{1,0:T(8,128)(2,1)S(1)}, u32[]{:S(2)}, u32[]{:S(2)}) collective-permute-start(bf16[288,512]{1,0:T(8,128)(2,1)S(1)} %copy-done.9), channel_id=1, source_target_pairs={{0,4},{4,0},{8,12},{12,8},{16,20},{20,16},{24,28},{28,24},{1,5},{5... | collective-permute-start | bytes 884744 | tf_op jit(solution)/shard_map/across_turn_4_of/ppermute | solution.py:549
  40.0 10.9 %collective-permute-start.4 = (bf16[288,512]{1,0:T(8,128)(2,1)}, bf16[288,512]{1,0:T(8,128)(2,1)S(1)}, u32[]{:S(2)}, u32[]{:S(2)}) collective-permute-start(bf16[288,512]{1,0:T(8,128)(2,1)} %get-tuple-element.59), channel_id=1, source_target_pairs={{0,4},{4,0},{8,12},{12,8},{16,20},{20,16},{24,28},{28,24},{1,5},{5... | collective-permute-start | bytes 884744 | tf_op jit(solution)/shard_map/across_turn_5_of/ppermute | solution.py:549
  40.3 21.4 %copy-start.1 = (bf16[256,512]{1,0:T(8,128)(2,1)S(1)}, bf16[256,512]{1,0:T(8,128)(2,1)}, u32[]{:S(2)}) copy-start(bf16[256,512]{1,0:T(8,128)(2,1)} %get-tuple-element.80.b0) | copy-start | bytes 786436
  40.3 17.1 %collective-permute-start.11 = (bf16[288,512]{1,0:T(8,128)(2,1)S(1)}, bf16[288,512]{1,0:T(8,128)(2,1)S(1)}, u32[]{:S(2)}, u32[]{:S(2)}) collective-permute-start(bf16[288,512]{1,0:T(8,128)(2,1)S(1)} %add_convert_fusion.1), channel_id=1, source_target_pairs={{0,1},{1,0},{2,3},{3,2},{4,5},{5,4},{6,7},{7,6},{8,16},{9,17},{10,... | collective-permute-start | bytes 884744 | tf_op jit(solution)/shard_map/odd_step_2_left/ppermute | solution.py:633
  44.0 6.8 %collective-permute-start.13 = (bf16[256,512]{1,0:T(8,128)(2,1)}, bf16[256,512]{1,0:T(8,128)(2,1)S(1)}, u32[]{:S(2)}, u32[]{:S(2)}) collective-permute-start(bf16[256,512]{1,0:T(8,128)(2,1)} %fusion.2), channel_id=1, source_target_pairs={{0,1},{1,0},{2,3},{3,2},{4,5},{5,4},{6,7},{7,6},{8,16},{9,17},{10,... | collective-permute-start | bytes 786440 | tf_op jit(solution)/shard_map/odd_step_1_right/ppermute | solution.py:633
  46.4 10.9 %collective-permute-start.10 = (bf16[288,512]{1,0:T(8,128)(2,1)S(1)}, bf16[288,512]{1,0:T(8,128)(2,1)S(1)}, u32[]{:S(2)}, u32[]{:S(2)}) collective-permute-start(bf16[288,512]{1,0:T(8,128)(2,1)S(1)} %add_convert_fusion), channel_id=1, source_target_pairs={{0,8},{4,12},{8,0},{12,4},{16,24},{20,28},{24,16},{28,20},{1,9},{5... | collective-permute-start | bytes 884744 | tf_op jit(solution)/shard_map/even_step_2_left/ppermute | solution.py:619
  48.6 8.8 %collective-permute-start.16 = (bf16[256,512]{1,0:T(8,128)(2,1)}, bf16[256,512]{1,0:T(8,128)(2,1)S(1)}, u32[]{:S(2)}, u32[]{:S(2)}) collective-permute-start(bf16[256,512]{1,0:T(8,128)(2,1)} %get-tuple-element.86), channel_id=1, source_target_pairs={{0,1},{1,0},{2,3},{3,2},{4,5},{5,4},{6,7},{7,6},{8,16},{9,17},{10,... | collective-permute-start | bytes 786440 | tf_op jit(solution)/shard_map/odd_step_2_right/ppermute | solution.py:633
  50.9 10.8 %collective-permute-start.15 = (bf16[256,512]{1,0:T(8,128)(2,1)S(1)}, bf16[256,512]{1,0:T(8,128)(2,1)S(1)}, u32[]{:S(2)}, u32[]{:S(2)}) collective-permute-start(bf16[256,512]{1,0:T(8,128)(2,1)S(1)} %fusion.4), channel_id=1, source_target_pairs={{0,8},{4,12},{8,0},{12,4},{16,24},{20,28},{24,16},{28,20},{1,9},{5... | collective-permute-start | bytes 786440 | tf_op jit(solution)/shard_map/even_step_2_right/ppermute | solution.py:619
  54.8 6.9 %collective-permute-start.14 = (bf16[256,512]{1,0:T(8,128)(2,1)S(1)}, bf16[256,512]{1,0:T(8,128)(2,1)S(1)}, u32[]{:S(2)}, u32[]{:S(2)}) collective-permute-start(bf16[256,512]{1,0:T(8,128)(2,1)S(1)} %get-tuple-element.85), channel_id=1, source_target_pairs={{0,4},{4,0},{8,12},{12,8},{16,20},{20,16},{24,28},{28,24},{1,5},{5... | collective-permute-start | bytes 786440 | tf_op jit(solution)/shard_map/across_turn_6_of/ppermute | solution.py:549
  63.4 1.6 %collective-permute-start.17 = (bf16[2,128,512]{2,1,0:T(8,128)(2,1)S(1)}, bf16[2,128,512]{2,1,0:T(8,128)(2,1)S(1)}, u32[]{:S(2)}, u32[]{:S(2)}) collective-permute-start(bf16[2,128,512]{2,1,0:T(8,128)(2,1)S(1)} %get-tuple-element.94), channel_id=1, source_target_pairs={{0,1},{1,0},{2,3},{3,2},{4,5},{5,4},{6,7},{7,6},{8,9},{9,8},{10,11... | collective-permute-start | bytes 786440 | tf_op jit(solution)/shard_map/ppermute | solution.py:479
  65.1 5.6 %collective-permute-start.18 = (bf16[128,512]{1,0:T(8,128)(2,1)S(1)}, bf16[128,512]{1,0:T(8,128)(2,1)S(1)}, u32[]{:S(2)}, u32[]{:S(2)}) collective-permute-start(bf16[128,512]{1,0:T(8,128)(2,1)S(1)} %fusion.9), channel_id=1, source_target_pairs={{0,2},{1,3},{2,0},{3,1},{4,6},{5,7},{6,4},{7,5},{8,10},{9,11},{10,... | collective-permute-start | bytes 393224 | tf_op jit(solution)/shard_map/ppermute | solution.py:480

commit v5 on v4

--- a/solution.py
+++ b/solution.py
@@ -163,12 +163,14 @@
     match(1)
     send(pay.at[0, PAD : PAD + side], own.at[0])
     match(2)
+    add_halos(1, 0, 1, 2, pay, edges, digits)
+    height = both.shape[0] // 2
+    either_way(s_a, k_a, 1, 0)
+    either_way(both.at[:height], both.at[height:], 1, 1)
     match(3)
-    height = both.shape[0] // 2
-    for q in (1, 2):
-        add_halos(q, q - 1, q, q + 1, pay, edges, digits)
-        either_way(s_a, k_a, q, 0)
-        either_way(both.at[:height], both.at[height:], q, 1)
+    add_halos(2, 1, 2, 3, pay, edges, digits)
+    either_way(s_a, k_a, 2, 0)
+    either_way(both.at[:height], both.at[height:], 2, 1)
     send(pay.at[3, PAD : PAD + side], own.at[1])
     send(edges, edges_out)
     send(digits, digits_out)
@@ -602,7 +604,6 @@
                 send = send + masked(odds[c])
             if (t, c) == (1, 1):
                 ahead = (step(2, 1, 0) + evens[0].astype(f32)).astype(bf16)
-                came[last - 1, 1], *_ = lax.optimization_barrier((came[last - 1, 1], ahead, odds[0]))
             send_odd = step(t, 1, c) if t else None
             if (t, c) == (2, 1):
                 send, _ = lax.optimization_barrier((send, came[last, 0]))

time: 71.8 us -> 69.2 us (0.964)
  starting transfers between devices: 19.4 us -> 15.7 us
  waiting for transfers between devices: 21.4 us -> 22.6 us
    ppermute x7, waiting for transfers between devices: 13 us -> 16 us  [across_y(): got.append(lax.ppermute(send, 'patch', across))]
    ppermute x5, starting transfers between devices: 7.48 us -> 4.87 us  [local(): evens[c] = lax.ppermute(send_even[c], 'patch', even)]
    ppermute x5, waiting for transfers between devices: 1.8 us -> 0.05 us  [local(): evens[c] = lax.ppermute(send_even[c], 'patch', even)]
    ppermute x7, starting transfers between devices: 8.5 us -> 7.22 us  [across_y(): got.append(lax.ppermute(send, 'patch', across))]
  transfers between devices with their start and end apart: 19 -> 19, of which waited for: 9 -> 9; matrix products, arithmetic and copies ran while one was open for 12% -> 13% of each run, Pallas kernels for 16% -> 17%
where the time goes in v5:
time: 69.2 us; the launch traced here: 68.8 us
  waiting for transfers between devices  22.6 us (33%)
  Pallas kernels  19.3 us (28%)
  starting transfers between devices  15.7 us (23%)
  other arithmetic  9.65 us (14%)
  between operations  1.53 us (2%)
    ppermute x7, waiting for transfers between devices, across_y(): got.append(lax.ppermute(send, 'patch', across))  16 us
    ppermute x7, starting transfers between devices, across_y(): got.append(lax.ppermute(send, 'patch', across))  7.22 us
    pallas_call x1, Pallas kernels, match_blocks(): pl.pallas_call(lambda *refs: rest_kernel(npatch, *refs), out_shape=[whole...  7.21 us
    pallas_call x1, Pallas kernels, match_blocks(): pl.pallas_call(lambda *refs: first_kernel(npatch, *refs), out_shape=[part...  5.8 us
    ppermute x5, starting transfers between devices, local(): evens[c] = lax.ppermute(send_even[c], 'patch', even)  4.87 us
    convert_element_type x4, other arithmetic, local(): send_even[c] = send.astype(bf16)  3.48 us
    ppermute x1, waiting for transfers between devices, finish(): lax.ppermute(pair[1].astype(bf16), 'band', [(i, i ^ 2) for i in range(4)])  2.74 us
    ppermute x1, waiting for transfers between devices, local(): direct = lax.ppermute(both, 'patch', even)  2.29 us
  transfers between devices with their start and end apart: 19, of which 9 were waited for; matrix products, arithmetic and copies ran while one was open for 13% of the time, Pallas kernels for 17%

profile of v5, /device:TPU:0, one launch (start us, length us, event | category | flops | bytes accessed | tf_op | source)
XLA Modules:
  0.0 68.8 jit_solution(11540821052292891727)
XLA Ops:
  0.6 5.8 %match_first.1 = (bf16[288,512]{1,0:T(8,128)(2,1)}, bf16[288,512]{1,0:T(8,128)(2,1)}, bf16[512,512]{1,0:T(8,128)(2,1)}, bf16[2,512,512]{2,1,0:T(8,128)(2,1)}, bf...) custom-call(s32[1,32]{1,0:T(1,128)} %refs_0_.3, s32[1,32]{1,0:T(1,128)} %refs_1_.3, bf16[1,32]{1,0:T(2,128)(2,1)} %refs_2_.3, ...), custom_call_target="tpu_custom_call" | custom-call | tf_op jit(solution)/shard_map/match_first/pallas_call | solution.py:289
  6.4 3.0 %collective-permute-start.2 = (bf16[288,512]{1,0:T(8,128)(2,1)}, bf16[288,512]{1,0:T(8,128)(2,1)}, u32[]{:S(2)}, u32[]{:S(2)}) collective-permute-start(bf16[288,512]{1,0:T(8,128)(2,1)} %get-tuple-element.56), channel_id=1, source_target_pairs={{0,4},{4,0},{8,12},{12,8},{16,20},{20,16},{24,28},{28,24},{1,5},{5... | collective-permute-start | bytes 884744 | tf_op jit(solution)/shard_map/across_turn_0_of/ppermute | solution.py:551
  9.5 1.6 %collective-permute-start = (bf16[512,512]{1,0:T(8,128)(2,1)}, bf16[512,512]{1,0:T(8,128)(2,1)}, u32[]{:S(2)}, u32[]{:S(2)}) collective-permute-start(bf16[512,512]{1,0:T(8,128)(2,1)} %get-tuple-element.54), channel_id=1, source_target_pairs={{0,8},{4,12},{8,0},{12,4},{16,24},{20,28},{24,16},{28,20},{1,9},{5... | collective-permute-start | bytes 1572872 | tf_op jit(solution)/shard_map/even_step_0_right/ppermute | solution.py:540
  11.0 7.2 %match_rest.1 = (bf16[288,512]{1,0:T(8,128)(2,1)}, bf16[256,512]{1,0:T(8,128)(2,1)}, bf16[256,512]{1,0:T(8,128)(2,1)}, bf16[288,512]{1,0:T(8,128)(2,1)}, bf16[28...) custom-call(s32[1,32]{1,0:T(1,128)} %refs_0_.3, ...), custom_call_target="tpu_custom_call" | custom-call | flops 2000000000 | bytes 8000000 | tf_op jit(solution)/shard_map/match_rest/pallas_call | solution.py:311
  18.3 0.0 collective-permute-done.2
  18.3 0.6 collective-permute-start.5
  18.9 1.2 %fusion = bf16[288,512]{1,0:T(8,128)(2,1)S(1)} fusion(bf16[288,512]{1,0:T(8,128)(2,1)} %collective-permute-done.2, bf16[288,512]{1,0:T(8,128)(2,1)} %get-tuple-element.64), kind=kLoop, calls=%fused_computation.10 | loop fusion | flops 589824 | bytes 884736 | tf_op jit(solution)/shard_map/even_step_0_left/convert_element_type | solution.py:619
  20.1 1.3 %collective-permute-start.7 = (bf16[288,512]{1,0:T(8,128)(2,1)S(1)}, bf16[288,512]{1,0:T(8,128)(2,1)S(1)}, u32[]{:S(2)}, u32[]{:S(2)}) collective-permute-start(bf16[288,512]{1,0:T(8,128)(2,1)S(1)} %fusion), channel_id=1, source_target_pairs={{0,8},{4,12},{8,0},{12,4},{16,24},{20,28},{24,16},{28,20},{1,9},{5... | collective-permute-start | bytes 884744 | tf_op jit(solution)/shard_map/even_step_0_left/ppermute | solution.py:620
  21.4 0.8 %collective-permute-start.3 = (bf16[256,512]{1,0:T(8,128)(2,1)}, bf16[256,512]{1,0:T(8,128)(2,1)S(1)}, u32[]{:S(2)}, u32[]{:S(2)}) collective-permute-start(bf16[256,512]{1,0:T(8,128)(2,1)} %get-tuple-element.57), channel_id=1, source_target_pairs={{0,4},{4,0},{8,12},{12,8},{16,20},{20,16},{24,28},{28,24},{1,5},{5... | collective-permute-start | bytes 786440 | tf_op jit(solution)/shard_map/across_turn_2_of/ppermute | solution.py:551
  22.1 2.3 %collective-permute-done = bf16[512,512]{1,0:T(8,128)(2,1)} collective-permute-done((bf16[512,512]{1,0:T(8,128)(2,1)}, bf16[512,512]{1,0:T(8,128)(2,1)}, u32[]{:S(2)}, u32[]{:S(2)}) %collective-permute-start) | collective-permute-done | bytes 524320 | tf_op jit(solution)/shard_map/even_step_0_right/ppermute | solution.py:540
  24.4 1.2 %select_convert_fusion.3 = bf16[256,512]{1,0:T(8,128)(2,1)S(1)} fusion(bf16[256,512]{1,0:T(8,128)(2,1)} %get-tuple-element.70, bf16[512,512]{1,0:T(8,128)(2,1)} %collective-permute-done, bf16[512,512]{1,0:T(8,128)(2,1)} %get-tuple-element.54, pred[]{:T(512)S(6)} %or.5, pred[]{:T(512)S(6)} %or.4), kind=kLoop, calls=%fused_computation.22 | loop fusion | flops 917504 | bytes 1048578 | tf_op jit(solution)/shard_map/convert_element_type | solution.py:557
  25.6 0.0 copy-start.2
  25.7 0.1 collective-permute-start.1
  25.7 2.8 %collective-permute-done.5 = bf16[288,512]{1,0:T(8,128)(2,1)S(1)} collective-permute-done((bf16[288,512]{1,0:T(8,128)(2,1)}, bf16[288,512]{1,0:T(8,128)(2,1)S(1)}, u32[]{:S(2)}, u32[]{:S(2)}) %collective-permute-start.5) | collective-permute-done | bytes 294944 | tf_op jit(solution)/shard_map/across_turn_1_of/ppermute | solution.py:551
  28.5 1.0 %fusion.1 = bf16[288,512]{1,0:T(8,128)(2,1)S(1)} fusion(bf16[288,512]{1,0:T(8,128)(2,1)S(1)} %collective-permute-done.5, bf16[288,512]{1,0:T(8,128)(2,1)} %get-tuple-element.67), kind=kLoop, calls=%fused_computation.11 | loop fusion | flops 589824 | bytes 884736 | tf_op jit(solution)/shard_map/even_step_1_left/convert_element_type | solution.py:619
  29.6 0.5 collective-permute-start.10
  30.1 1.2 %add_convert_fusion.2 = bf16[288,512]{1,0:T(8,128)(2,1)S(1)} fusion(bf16[288,512]{1,0:T(8,128)(2,1)S(1)} %collective-permute-done.7, bf16[288,512]{1,0:T(8,128)(2,1)} %collective-permute-done.2, bf16[288,512]{1,0:T(8,128)(2,1)} %get-tuple-element.64), kind=kLoop, calls=%fused_computation.8 | loop fusion | flops 884736 | bytes 1179648 | tf_op jit(solution)/shard_map/odd_step_1_left/convert_element_type | solution.py:634
  31.3 0.1 collective-permute-start.8
  31.4 2.8 %collective-permute-done.3 = bf16[256,512]{1,0:T(8,128)(2,1)S(1)} collective-permute-done((bf16[256,512]{1,0:T(8,128)(2,1)}, bf16[256,512]{1,0:T(8,128)(2,1)S(1)}, u32[]{:S(2)}, u32[]{:S(2)}) %collective-permute-start.3) | collective-permute-done | bytes 262176 | tf_op jit(solution)/shard_map/across_turn_2_of/ppermute | solution.py:551
  34.2 1.1 %select_convert_fusion.2 = bf16[256,512]{1,0:T(8,128)(2,1)S(1)} fusion(bf16[256,512]{1,0:T(8,128)(2,1)} %get-tuple-element.70, bf16[256,512]{1,0:T(8,128)(2,1)S(1)} %collective-permute-done.3, bf16[256,512]{1,0:T(8,128)(2,1)} %get-tuple-element.68, pred[]{:T(512)S(6)} %or.4), kind=kLoop, calls=%fused_computation.20 | loop fusion | flops 786432 | bytes 1048577 | tf_op jit(solution)/shard_map/even_step_1_right/convert_element_type | solution.py:619
  35.3 0.5 collective-permute-start.12
  35.8 1.3 %collective-permute-start.6 = (bf16[288,512]{1,0:T(8,128)(2,1)S(1)}, bf16[288,512]{1,0:T(8,128)(2,1)S(1)}, u32[]{:S(2)}, u32[]{:S(2)}) collective-permute-start(bf16[288,512]{1,0:T(8,128)(2,1)S(1)} %copy-done.9), channel_id=1, source_target_pairs={{0,4},{4,0},{8,12},{12,8},{16,20},{20,16},{24,28},{28,24},{1,5},{5... | collective-permute-start | bytes 884744 | tf_op jit(solution)/shard_map/across_turn_4_of/ppermute | solution.py:551
  37.1 2.7 %collective-permute-done.1 = bf16[256,512]{1,0:T(8,128)(2,1)S(1)} collective-permute-done((bf16[256,512]{1,0:T(8,128)(2,1)S(1)}, bf16[256,512]{1,0:T(8,128)(2,1)S(1)}, u32[]{:S(2)}, u32[]{:S(2)}) %collective-permute-start.1) | collective-permute-done | bytes 262176 | tf_op jit(solution)/shard_map/across_turn_3_of/ppermute | solution.py:551
  39.8 1.8 %fusion.2 = bf16[256,512]{1,0:T(8,128)(2,1)} fusion(bf16[256,512]{1,0:T(8,128)(2,1)S(1)} %collective-permute-done.1, bf16[512,512]{1,0:T(8,128)(2,1)} %collective-permute-done, bf16[512,512]{1,0:T(8,128)(2,1)S(1)} %copy-done.5, pred[]{:T(512)S(6)} %or.5), kind=kLoop, calls=%fused_computation.12 | loop fusion | flops 917504 | bytes 1048577 | tf_op jit(solution)/shard_map/convert_element_type | solution.py:632
  41.6 0.3 collective-permute-start.4
  41.8 0.1 add_convert_fusion
  42.0 0.0 collective-permute-done.12
  42.0 0.3 collective-permute-start.11
  42.3 2.0 %collective-permute-done.6 = bf16[288,512]{1,0:T(8,128)(2,1)S(1)} collective-permute-done((bf16[288,512]{1,0:T(8,128)(2,1)S(1)}, bf16[288,512]{1,0:T(8,128)(2,1)S(1)}, u32[]{:S(2)}, u32[]{:S(2)}) %collective-permute-start.6) | collective-permute-done | bytes 294944 | tf_op jit(solution)/shard_map/across_turn_4_of/ppermute | solution.py:551
  44.3 0.1 add_convert_fusion.1
  44.5 1.3 %collective-permute-start.9 = (bf16[288,512]{1,0:T(8,128)(2,1)S(1)}, bf16[288,512]{1,0:T(8,128)(2,1)S(1)}, u32[]{:S(2)}, u32[]{:S(2)}) collective-permute-start(bf16[288,512]{1,0:T(8,128)(2,1)S(1)} %add_convert_fusion.1), channel_id=1, source_target_pairs={{0,8},{4,12},{8,0},{12,4},{16,24},{20,28},{24,16},{28,20},{1,9},{5... | collective-permute-start | bytes 884744 | tf_op jit(solution)/shard_map/even_step_2_left/ppermute | solution.py:620
  45.8 0.9 %fusion.7 = (bf16[256,512]{1,0:T(8,128)(2,1)}, bf16[256,512]{1,0:T(8,128)(2,1)S(1)}) fusion(bf16[256,512]{1,0:T(8,128)(2,1)S(1)} %collective-permute-done.12, bf16[256,512]{1,0:T(8,128)(2,1)S(1)} %collective-permute-done.3, bf16[256,512]{1,0:T(8,128)(2,1)S(1)} %copy-done.4, pred[]{:T(512)S(6)} %or.5, bf16[256,512]{1,0:T(8,128)(2,1)S(1)} %copy-done.8), kind=kLoop, calls=%fused_computation.17 | loop fusion | flops 1310720 | bytes 1572865 | tf_op jit(solution)/shard_map/convert_element_type | solution.py:628
  47.3 1.5 %tables.1 = (bf16[256,288]{1,0:T(8,128)(2,1)S(1)}, bf16[256,288]{1,0:T(8,128)(2,1)S(1)}, bf16[512,512]{1,0:T(8,128)(2,1)S(1)}, bf16[512,512]{1,0:T(8,128)(2,1)S(1)}) custom-call(f32[1,25]{1,0:T(1,128)S(1)} %copy-done.2), custom_call_target="tpu_custom_call" | custom-call | flops 20000000 | bytes 2000000 | tf_op jit(solution)/shard_map/tables/pallas_call | solution.py:430
  48.8 0.1 fusion.4
  49.0 2.2 %collective-permute-done.4.a1 = bf16[288,512]{1,0:T(8,128)(2,1)S(1)} collective-permute-done((bf16[288,512]{1,0:T(8,128)(2,1)}, bf16[288,512]{1,0:T(8,128)(2,1)S(1)}, u32[]{:S(2)}, u32[]{:S(2)}) %collective-permute-start.4) | collective-permute-done | bytes 294944 | tf_op jit(solution)/shard_map/across_turn_5_of/ppermute | solution.py:551
  51.2 1.2 %collective-permute-start.15 = (bf16[256,512]{1,0:T(8,128)(2,1)S(1)}, bf16[256,512]{1,0:T(8,128)(2,1)S(1)}, u32[]{:S(2)}, u32[]{:S(2)}) collective-permute-start(bf16[256,512]{1,0:T(8,128)(2,1)S(1)} %fusion.4), channel_id=1, source_target_pairs={{0,8},{4,12},{8,0},{12,4},{16,24},{20,28},{24,16},{28,20},{1,9},{5... | collective-permute-start | bytes 786440 | tf_op jit(solution)/shard_map/even_step_2_right/ppermute | solution.py:620
  52.4 1.2 %collective-permute-start.14 = (bf16[256,512]{1,0:T(8,128)(2,1)S(1)}, bf16[256,512]{1,0:T(8,128)(2,1)S(1)}, u32[]{:S(2)}, u32[]{:S(2)}) collective-permute-start(bf16[256,512]{1,0:T(8,128)(2,1)S(1)} %get-tuple-element.83), channel_id=1, source_target_pairs={{0,4},{4,0},{8,12},{12,8},{16,20},{20,16},{24,28},{28,24},{1,5},{5... | collective-permute-start | bytes 786440 | tf_op jit(solution)/shard_map/across_turn_6_of/ppermute | solution.py:551
  53.7 0.1 select_convert_fusion.a3
  53.7 1.8 %tail_left.1 = (f32[256,512]{1,0:T(8,128)S(1)}, f32[32,512]{1,0:T(8,128)S(1)}, f32[2,8,512]{2,1,0:T(8,128)S(1)}, f32[2,128,256]{2,1,0:T(8,128)S(1)}, f32[2,128,256]{2,1,0:T(8,128)S(1)}) custom-call(bf16[288,512]{1,0:T(8,128)(2,1)S(1)} %copy-done, bf16[288,512]{1,0:T(8,128)(2,1)S(1)} %collective-permute-done.4.a1, ...), custom_call_target="tpu_custom_call" | custom-call | flops 500000000 | bytes 4000000 | tf_op jit(solution)/shard_map/tail_left/pallas_call | solution.py:454
  55.6 3.5 %collective-permute-done.14.b1 = bf16[256,512]{1,0:T(8,128)(2,1)S(1)} collective-permute-done((bf16[256,512]{1,0:T(8,128)(2,1)S(1)}, bf16[256,512]{1,0:T(8,128)(2,1)S(1)}, u32[]{:S(2)}, u32[]{:S(2)}) %collective-permute-start.14) | collective-permute-done | bytes 262176 | tf_op jit(solution)/shard_map/across_turn_6_of/ppermute | solution.py:551
  59.1 1.7 %tail_right.1 = (f32[256,512]{1,0:T(8,128)S(1)}, bf16[2,128,512]{2,1,0:T(8,128)(2,1)S(1)}, f32[2,128,512]{2,1,0:T(8,128)S(1)}) custom-call(bf16[256,512]{1,0:T(8,128)(2,1)S(1)} %copy-done.1, bf16[256,512]{1,0:T(8,128)(2,1)S(1)} %collective-permute-done.14.b1, bf16[256,512]{1,0:T(8,128)(2,1)S(1)} %collective-permute-done.15.b2, ...), custom_call_target="tpu_custom_call" | custom-call | tf_op jit(solution)/shard_map/tail_right/pallas_call | solution.py:469
  60.8 0.1 collective-permute-start.17
  60.9 1.5 %collective-permute-done.17 = bf16[2,128,512]{2,1,0:T(8,128)(2,1)S(1)} collective-permute-done((bf16[2,128,512]{2,1,0:T(8,128)(2,1)S(1)}, bf16[2,128,512]{2,1,0:T(8,128)(2,1)S(1)}, u32[]{:S(2)}, u32[]{:S(2)}) %collective-permute-start.17) | collective-permute-done | bytes 262176 | tf_op jit(solution)/shard_map/ppermute | solution.py:481
  62.4 0.1 convert_add_fusion.4
  62.5 1.6 %collective-permute-start.18 = (bf16[128,512]{1,0:T(8,128)(2,1)S(1)}, bf16[128,512]{1,0:T(8,128)(2,1)S(1)}, u32[]{:S(2)}, u32[]{:S(2)}) collective-permute-start(bf16[128,512]{1,0:T(8,128)(2,1)S(1)} %fusion.9), channel_id=1, source_target_pairs={{0,2},{1,3},{2,0},{3,1},{4,6},{5,7},{6,4},{7,5},{8,10},{9,11},{10,... | collective-permute-start | bytes 393224 | tf_op jit(solution)/shard_map/ppermute | solution.py:482
  64.1 1.3 %tail_image.1 = f32[512,512]{1,0:T(8,128)} custom-call(f32[256,512]{1,0:T(8,128)S(1)} %get-tuple-element.77.left, f32[256,512]{1,0:T(8,128)S(1)} %get-tuple-element.93.right), custom_call_target="tpu_custom_call" | custom-call | bytes 2000000 | tf_op jit(solution)/shard_map/tail_image/pallas_call | solution.py:484
  65.4 2.7 %collective-permute-done.18 = bf16[128,512]{1,0:T(8,128)(2,1)S(1)} collective-permute-done((bf16[128,512]{1,0:T(8,128)(2,1)S(1)}, bf16[128,512]{1,0:T(8,128)(2,1)S(1)}, u32[]{:S(2)}, u32[]{:S(2)}) %collective-permute-start.18) | collective-permute-done | bytes 131104 | tf_op jit(solution)/shard_map/ppermute | solution.py:482
  68.1 0.7 %fusion.8 = f32[128,512]{1,0:T(8,128)} fusion(f32[2,128,512]{2,1,0:T(8,128)S(1)} %convert_add_fusion.4, bf16[128,512]{1,0:T(8,128)(2,1)S(1)} %collective-permute-done.18), kind=kLoop, calls=%fused_computation.25 | loop fusion | flops 131072 | bytes 655360 | tf_op jit(solution)/shard_map/add | solution.py:493
  (31 shorter events, 0.1 us)
Async XLA Ops:
  6.4 11.9 %collective-permute-start.2 = (bf16[288,512]{1,0:T(8,128)(2,1)}, bf16[288,512]{1,0:T(8,128)(2,1)}, u32[]{:S(2)}, u32[]{:S(2)}) collective-permute-start(bf16[288,512]{1,0:T(8,128)(2,1)} %get-tuple-element.56), channel_id=1, source_target_pairs={{0,4},{4,0},{8,12},{12,8},{16,20},{20,16},{24,28},{28,24},{1,5},{5... | collective-permute-start | bytes 884744 | tf_op jit(solution)/shard_map/across_turn_0_of/ppermute | solution.py:551
  9.5 14.9 %collective-permute-start = (bf16[512,512]{1,0:T(8,128)(2,1)}, bf16[512,512]{1,0:T(8,128)(2,1)}, u32[]{:S(2)}, u32[]{:S(2)}) collective-permute-start(bf16[512,512]{1,0:T(8,128)(2,1)} %get-tuple-element.54), channel_id=1, source_target_pairs={{0,8},{4,12},{8,0},{12,4},{16,24},{20,28},{24,16},{28,20},{1,9},{5... | collective-permute-start | bytes 1572872 | tf_op jit(solution)/shard_map/even_step_0_right/ppermute | solution.py:540
  18.3 17.5 %copy-start.9 = (bf16[288,512]{1,0:T(8,128)(2,1)S(1)}, bf16[288,512]{1,0:T(8,128)(2,1)}, u32[]{:S(2)}) copy-start(bf16[288,512]{1,0:T(8,128)(2,1)} %get-tuple-element.63) | copy-start | bytes 884740
  18.3 21.5 %copy-start.5 = (bf16[512,512]{1,0:T(8,128)(2,1)S(1)}, bf16[512,512]{1,0:T(8,128)(2,1)}, u32[]{:S(2)}) copy-start(bf16[512,512]{1,0:T(8,128)(2,1)} %get-tuple-element.54) | copy-start | bytes 1572868
  18.3 23.6 %copy-start.3 = (bf16[288,512]{1,0:T(8,128)(2,1)S(1)}, bf16[288,512]{1,0:T(8,128)(2,1)}, u32[]{:S(2)}) copy-start(bf16[288,512]{1,0:T(8,128)(2,1)} %get-tuple-element.67) | copy-start | bytes 884740
  18.3 26.0 %copy-start.6 = (bf16[288,512]{1,0:T(8,128)(2,1)S(1)}, bf16[288,512]{1,0:T(8,128)(2,1)}, u32[]{:S(2)}) copy-start(bf16[288,512]{1,0:T(8,128)(2,1)} %get-tuple-element.59) | copy-start | bytes 884740
  18.3 10.2 %collective-permute-start.5 = (bf16[288,512]{1,0:T(8,128)(2,1)}, bf16[288,512]{1,0:T(8,128)(2,1)S(1)}, u32[]{:S(2)}, u32[]{:S(2)}) collective-permute-start(bf16[288,512]{1,0:T(8,128)(2,1)} %get-tuple-element.62), channel_id=1, source_target_pairs={{0,4},{4,0},{8,12},{12,8},{16,20},{20,16},{24,28},{28,24},{1,5},{5... | collective-permute-start | bytes 884744 | tf_op jit(solution)/shard_map/across_turn_1_of/ppermute | solution.py:551
  18.9 26.9 %copy-start.4 = (bf16[256,512]{1,0:T(8,128)(2,1)S(1)}, bf16[256,512]{1,0:T(8,128)(2,1)}, u32[]{:S(2)}) copy-start(bf16[256,512]{1,0:T(8,128)(2,1)} %get-tuple-element.68) | copy-start | bytes 786436
  18.9 26.9 %copy-start.8 = (bf16[256,512]{1,0:T(8,128)(2,1)S(1)}, bf16[256,512]{1,0:T(8,128)(2,1)}, u32[]{:S(2)}) copy-start(bf16[256,512]{1,0:T(8,128)(2,1)} %get-tuple-element.79) | copy-start | bytes 786436
  20.1 10.0 %collective-permute-start.7 = (bf16[288,512]{1,0:T(8,128)(2,1)S(1)}, bf16[288,512]{1,0:T(8,128)(2,1)S(1)}, u32[]{:S(2)}, u32[]{:S(2)}) collective-permute-start(bf16[288,512]{1,0:T(8,128)(2,1)S(1)} %fusion), channel_id=1, source_target_pairs={{0,8},{4,12},{8,0},{12,4},{16,24},{20,28},{24,16},{28,20},{1,9},{5... | collective-permute-start | bytes 884744 | tf_op jit(solution)/shard_map/even_step_0_left/ppermute | solution.py:620
  21.4 12.8 %collective-permute-start.3 = (bf16[256,512]{1,0:T(8,128)(2,1)}, bf16[256,512]{1,0:T(8,128)(2,1)S(1)}, u32[]{:S(2)}, u32[]{:S(2)}) collective-permute-start(bf16[256,512]{1,0:T(8,128)(2,1)} %get-tuple-element.57), channel_id=1, source_target_pairs={{0,4},{4,0},{8,12},{12,8},{16,20},{20,16},{24,28},{28,24},{1,5},{5... | collective-permute-start | bytes 786440 | tf_op jit(solution)/shard_map/across_turn_2_of/ppermute | solution.py:551
  25.6 21.7 %copy-start.2 = (f32[1,25]{1,0:T(1,128)S(1)}, f32[1,25]{1,0:T(1,128)}, u32[]{:S(2)}) copy-start(f32[1,25]{1,0:T(1,128)} %det) | copy-start | bytes 304
  25.7 23.2 %copy-start.7 = (bf16[256,512]{1,0:T(8,128)(2,1)S(1)}, bf16[256,512]{1,0:T(8,128)(2,1)}, u32[]{:S(2)}) copy-start(bf16[256,512]{1,0:T(8,128)(2,1)} %get-tuple-element.80) | copy-start | bytes 786436
  25.7 14.1 %collective-permute-start.1 = (bf16[256,512]{1,0:T(8,128)(2,1)S(1)}, bf16[256,512]{1,0:T(8,128)(2,1)S(1)}, u32[]{:S(2)}, u32[]{:S(2)}) collective-permute-start(bf16[256,512]{1,0:T(8,128)(2,1)S(1)} %select_convert_fusion.3), channel_id=1, source_target_pairs={{0,4},{4,0},{8,12},{12,8},{16,20},{20,16},{24,28},{28,24},{1,5},{5... | collective-permute-start | bytes 786440 | tf_op jit(solution)/shard_map/across_turn_3_of/ppermute | solution.py:551
  29.6 24.1 %copy-start = (bf16[288,512]{1,0:T(8,128)(2,1)S(1)}, bf16[288,512]{1,0:T(8,128)(2,1)}, u32[]{:S(2)}) copy-start(bf16[288,512]{1,0:T(8,128)(2,1)} %get-tuple-element.51.a0) | copy-start | bytes 884740
  29.6 12.0 %collective-permute-start.10 = (bf16[288,512]{1,0:T(8,128)(2,1)S(1)}, bf16[288,512]{1,0:T(8,128)(2,1)S(1)}, u32[]{:S(2)}, u32[]{:S(2)}) collective-permute-start(bf16[288,512]{1,0:T(8,128)(2,1)S(1)} %fusion.1), channel_id=1, source_target_pairs={{0,8},{4,12},{8,0},{12,4},{16,24},{20,28},{24,16},{28,20},{1,9},{5... | collective-permute-start | bytes 884744 | tf_op jit(solution)/shard_map/even_step_1_left/ppermute | solution.py:620
  31.3 11.0 %collective-permute-start.8 = (bf16[288,512]{1,0:T(8,128)(2,1)S(1)}, bf16[288,512]{1,0:T(8,128)(2,1)S(1)}, u32[]{:S(2)}, u32[]{:S(2)}) collective-permute-start(bf16[288,512]{1,0:T(8,128)(2,1)S(1)} %add_convert_fusion.2), channel_id=1, source_target_pairs={{0,1},{1,0},{2,3},{3,2},{4,5},{5,4},{6,7},{7,6},{8,16},{9,17},{10,... | collective-permute-start | bytes 884744 | tf_op jit(solution)/shard_map/odd_step_1_left/ppermute | solution.py:634
  35.3 6.7 %collective-permute-start.12 = (bf16[256,512]{1,0:T(8,128)(2,1)S(1)}, bf16[256,512]{1,0:T(8,128)(2,1)S(1)}, u32[]{:S(2)}, u32[]{:S(2)}) collective-permute-start(bf16[256,512]{1,0:T(8,128)(2,1)S(1)} %select_convert_fusion.2), channel_id=1, source_target_pairs={{0,8},{4,12},{8,0},{12,4},{16,24},{20,28},{24,16},{28,20},{1,9},{5... | collective-permute-start | bytes 786440 | tf_op jit(solution)/shard_map/even_step_1_right/ppermute | solution.py:620
  35.8 8.5 %collective-permute-start.6 = (bf16[288,512]{1,0:T(8,128)(2,1)S(1)}, bf16[288,512]{1,0:T(8,128)(2,1)S(1)}, u32[]{:S(2)}, u32[]{:S(2)}) collective-permute-start(bf16[288,512]{1,0:T(8,128)(2,1)S(1)} %copy-done.9), channel_id=1, source_target_pairs={{0,4},{4,0},{8,12},{12,8},{16,20},{20,16},{24,28},{28,24},{1,5},{5... | collective-permute-start | bytes 884744 | tf_op jit(solution)/shard_map/across_turn_4_of/ppermute | solution.py:551
  41.5 7.3 %collective-permute-start.13 = (bf16[256,512]{1,0:T(8,128)(2,1)}, bf16[256,512]{1,0:T(8,128)(2,1)S(1)}, u32[]{:S(2)}, u32[]{:S(2)}) collective-permute-start(bf16[256,512]{1,0:T(8,128)(2,1)} %fusion.2), channel_id=1, source_target_pairs={{0,1},{1,0},{2,3},{3,2},{4,5},{5,4},{6,7},{7,6},{8,16},{9,17},{10,... | collective-permute-start | bytes 786440 | tf_op jit(solution)/shard_map/odd_step_1_right/ppermute | solution.py:634
  41.6 17.5 %copy-start.1 = (bf16[256,512]{1,0:T(8,128)(2,1)S(1)}, bf16[256,512]{1,0:T(8,128)(2,1)}, u32[]{:S(2)}) copy-start(bf16[256,512]{1,0:T(8,128)(2,1)} %get-tuple-element.78.b0) | copy-start | bytes 786436
  41.6 9.6 %collective-permute-start.4 = (bf16[288,512]{1,0:T(8,128)(2,1)}, bf16[288,512]{1,0:T(8,128)(2,1)S(1)}, u32[]{:S(2)}, u32[]{:S(2)}) collective-permute-start(bf16[288,512]{1,0:T(8,128)(2,1)} %get-tuple-element.58), channel_id=1, source_target_pairs={{0,4},{4,0},{8,12},{12,8},{16,20},{20,16},{24,28},{28,24},{1,5},{5... | collective-permute-start | bytes 884744 | tf_op jit(solution)/shard_map/across_turn_5_of/ppermute | solution.py:551
  42.0 11.7 %collective-permute-start.11 = (bf16[288,512]{1,0:T(8,128)(2,1)S(1)}, bf16[288,512]{1,0:T(8,128)(2,1)S(1)}, u32[]{:S(2)}, u32[]{:S(2)}) collective-permute-start(bf16[288,512]{1,0:T(8,128)(2,1)S(1)} %add_convert_fusion), channel_id=1, source_target_pairs={{0,1},{1,0},{2,3},{3,2},{4,5},{5,4},{6,7},{7,6},{8,16},{9,17},{10,... | collective-permute-start | bytes 884744 | tf_op jit(solution)/shard_map/odd_step_2_left/ppermute | solution.py:634
  44.5 9.2 %collective-permute-start.9 = (bf16[288,512]{1,0:T(8,128)(2,1)S(1)}, bf16[288,512]{1,0:T(8,128)(2,1)S(1)}, u32[]{:S(2)}, u32[]{:S(2)}) collective-permute-start(bf16[288,512]{1,0:T(8,128)(2,1)S(1)} %add_convert_fusion.1), channel_id=1, source_target_pairs={{0,8},{4,12},{8,0},{12,4},{16,24},{20,28},{24,16},{28,20},{1,9},{5... | collective-permute-start | bytes 884744 | tf_op jit(solution)/shard_map/even_step_2_left/ppermute | solution.py:620
  46.7 7.0 %collective-permute-start.16 = (bf16[256,512]{1,0:T(8,128)(2,1)}, bf16[256,512]{1,0:T(8,128)(2,1)S(1)}, u32[]{:S(2)}, u32[]{:S(2)}) collective-permute-start(bf16[256,512]{1,0:T(8,128)(2,1)} %get-tuple-element.84), channel_id=1, source_target_pairs={{0,1},{1,0},{2,3},{3,2},{4,5},{5,4},{6,7},{7,6},{8,16},{9,17},{10,... | collective-permute-start | bytes 786440 | tf_op jit(solution)/shard_map/odd_step_2_right/ppermute | solution.py:634
  51.2 7.9 %collective-permute-start.15 = (bf16[256,512]{1,0:T(8,128)(2,1)S(1)}, bf16[256,512]{1,0:T(8,128)(2,1)S(1)}, u32[]{:S(2)}, u32[]{:S(2)}) collective-permute-start(bf16[256,512]{1,0:T(8,128)(2,1)S(1)} %fusion.4), channel_id=1, source_target_pairs={{0,8},{4,12},{8,0},{12,4},{16,24},{20,28},{24,16},{28,20},{1,9},{5... | collective-permute-start | bytes 786440 | tf_op jit(solution)/shard_map/even_step_2_right/ppermute | solution.py:620
  52.4 6.6 %collective-permute-start.14 = (bf16[256,512]{1,0:T(8,128)(2,1)S(1)}, bf16[256,512]{1,0:T(8,128)(2,1)S(1)}, u32[]{:S(2)}, u32[]{:S(2)}) collective-permute-start(bf16[256,512]{1,0:T(8,128)(2,1)S(1)} %get-tuple-element.83), channel_id=1, source_target_pairs={{0,4},{4,0},{8,12},{12,8},{16,20},{20,16},{24,28},{28,24},{1,5},{5... | collective-permute-start | bytes 786440 | tf_op jit(solution)/shard_map/across_turn_6_of/ppermute | solution.py:551
  60.8 1.6 %collective-permute-start.17 = (bf16[2,128,512]{2,1,0:T(8,128)(2,1)S(1)}, bf16[2,128,512]{2,1,0:T(8,128)(2,1)S(1)}, u32[]{:S(2)}, u32[]{:S(2)}) collective-permute-start(bf16[2,128,512]{2,1,0:T(8,128)(2,1)S(1)} %get-tuple-element.92), channel_id=1, source_target_pairs={{0,1},{1,0},{2,3},{3,2},{4,5},{5,4},{6,7},{7,6},{8,9},{9,8},{10,11... | collective-permute-start | bytes 786440 | tf_op jit(solution)/shard_map/ppermute | solution.py:481
  62.5 5.6 %collective-permute-start.18 = (bf16[128,512]{1,0:T(8,128)(2,1)S(1)}, bf16[128,512]{1,0:T(8,128)(2,1)S(1)}, u32[]{:S(2)}, u32[]{:S(2)}) collective-permute-start(bf16[128,512]{1,0:T(8,128)(2,1)S(1)} %fusion.9), channel_id=1, source_target_pairs={{0,2},{1,3},{2,0},{3,1},{4,6},{5,7},{6,4},{7,5},{8,10},{9,11},{10,... | collective-permute-start | bytes 393224 | tf_op jit(solution)/shard_map/ppermute | solution.py:482

commit v6 on v5

--- a/solution.py
+++ b/solution.py
@@ -391,7 +391,7 @@
 
 
 def tail_right(
-    b0, b1, b2, b3, seam, factor, give_left, stay_left, noise, band, colh, coll, rowh, rowl, normed, give, stay
+    b0, b1, b2, b3, seam, factor, give_left, stay_left, noise, band, colh, coll, rowh, rowl, normed, give_near, give_far, stay
 ):
     rows, side = b0.shape
     edge = side // TH
@@ -400,10 +400,10 @@
     right = jnp.concatenate([seam[...], right[:inner] * factor[0, 0:1], right[inner:] * factor[1, 0:1]], axis=0)
     normed[...] = right[PAD : PAD + edge]
     ch, cl = column_pass(colh, coll, right)
-    for j, place in enumerate((band[0], band[0] ^ 2)):
-        give[j, :, edge:] = chi_rows(place ^ 1, rowh, rowl, ch, cl, noise).astype(give.dtype)
+    for j, (place, give) in enumerate(((band[0], give_near), (band[0] ^ 2, give_far))):
+        give[:, edge:] = chi_rows(place ^ 1, rowh, rowl, ch, cl, noise).astype(give.dtype)
         stay[j, :, edge:] = chi_rows(place, rowh, rowl, ch, cl, noise)
-        give[j, :, :edge] = give_left[j].astype(give.dtype)
+        give[:, :edge] = give_left[j].astype(give.dtype)
         stay[j, :, :edge] = stay_left[j]
 
 
@@ -438,7 +438,7 @@
     )(det)
 
 
-def finish(left, right, noise, det):
+def finish(left, right, masked, noise, det):
     rows, side = left[0].shape
     f32, bf16 = jnp.float32, jnp.bfloat16
     colh, coll, rowh, rowl = filter_tables(det, rows, side)
@@ -466,21 +466,23 @@
         cost_estimate=pl.CostEstimate(flops=500_000_000, bytes_accessed=4_000_000, transcendentals=0),
         name="tail_left",
     )(*left, noise, where, *tables)
-    normed_right, give, stay = pl.pallas_call(
+    *right, odd_right = right
+    odd_right, _ = lax.optimization_barrier((odd_right, seam))
+    right = [*right, masked(odd_right).astype(bf16)]
+    quarter = jax.ShapeDtypeStruct((side // 4, side), bf16)
+    normed_right, give_near, give_far, stay = pl.pallas_call(
         tail_right,
-        out_shape=[
-            tile,
-            jax.ShapeDtypeStruct((2, side // 4, side), bf16),
-            jax.ShapeDtypeStruct((2, side // 4, side), f32),
-        ],
+        out_shape=[tile, quarter, quarter, jax.ShapeDtypeStruct((2, side // 4, side), f32)],
         in_specs=[vmem] * 8 + [smem] * 2 + [vmem] * 4,
-        out_specs=[vmem] * 3,
+        out_specs=[vmem] * 4,
         compiler_params=params,
         name="tail_right",
     )(*right, seam, factor, give, stay, noise, where, *tables)
-    pair = stay + lax.ppermute(give, "band", [(i, i ^ 1) for i in range(4)]).astype(f32)
-    beyond = lax.ppermute(pair[1].astype(bf16), "band", [(i, i ^ 2) for i in range(4)])
-    normed_right, _ = lax.optimization_barrier((normed_right, pair))
+    core, across_x = [(i, i ^ 1) for i in range(4)], [(i, i ^ 2) for i in range(4)]
+    far = (stay[1] + lax.ppermute(give_far, "band", core).astype(f32)).astype(bf16)
+    beyond = lax.ppermute(far, "band", across_x)
+    normed_right, give_near, _ = lax.optimization_barrier((normed_right, give_near, far))
+    near = stay[0] + lax.ppermute(give_near, "band", core).astype(f32)
     image = pl.pallas_call(
         tail_image,
         out_shape=jax.ShapeDtypeStruct((side, side), f32),
@@ -490,7 +492,7 @@
         cost_estimate=pl.CostEstimate(flops=0, bytes_accessed=2_000_000, transcendentals=0),
         name="tail_image",
     )(normed_left, normed_right)
-    return image, pair[0] + beyond.astype(f32)
+    return image, near + beyond.astype(f32)
 
 
 def either(flags):
@@ -636,11 +638,9 @@
                 final, _ = lax.optimization_barrier((final, send_even[1]))
                 across_y(final)
                 came[last, 1] = got[-1]
-    odds[1], _ = lax.optimization_barrier((odds[1], evens[0]))
-    for c in range(2):
-        odds[c] = masked(odds[c]).astype(bf16)
+    odds[0] = masked(odds[0]).astype(bf16)
     parts = [(kept[last][c], came[last, c], evens[c], odds[c]) for c in range(2)]
-    image, chi = finish(*parts, noise_var, det_taps)
+    image, chi = finish(*parts, masked, noise_var, det_taps)
     return image[None], chi
 
 

time: 69.2 us -> 70 us (1.012)
  waiting for transfers between devices: 22.6 us -> 25.1 us
  other arithmetic: 9.65 us -> 8.22 us
    ppermute x7, waiting for transfers between devices: 16 us -> 19.3 us  [across_y(): got.append(lax.ppermute(send, 'patch', across))]
    ppermute x1, waiting for transfers between devices: 2.29 us -> 0.93 us  [local(): direct = lax.ppermute(both, 'patch', even)]
    convert_element_type x1, other arithmetic: 1.77 us -> 1.07 us  [local(): sent_odd = send_odd.astype(bf16)]
    ppermute x2 -> x3, starting transfers between devices: 1.63 us -> 1.79 us  [the longest x1 1.5 us: finish(): beyond = lax.ppermute(far, 'band', across_x)]
    ppermute x2 -> x3, waiting for transfers between devices: 4.27 us -> 4.29 us  [the longest x1 2.95 us: finish(): beyond = lax.ppermute(far, 'band', across_x)]
  transfers between devices with their start and end apart: 19 -> 20, of which waited for: 9 -> 11; matrix products, arithmetic and copies ran while one was open for 13% -> 11% of each run, Pallas kernels for 17% -> 17%
where the time goes in v6:
time: 70 us; the launch traced here: 69.7 us
  waiting for transfers between devices  25.1 us (36%)
  Pallas kernels  19.4 us (28%)
  starting transfers between devices  15.4 us (22%)
  other arithmetic  8.22 us (12%)
  between operations  1.57 us (2%)
    ppermute x7, waiting for transfers between devices, across_y(): got.append(lax.ppermute(send, 'patch', across))  19.3 us
    pallas_call x1, Pallas kernels, match_blocks(): pl.pallas_call(lambda *refs: rest_kernel(npatch, *refs), out_shape=[whole...  7.23 us
    ppermute x7, starting transfers between devices, across_y(): got.append(lax.ppermute(send, 'patch', across))  6.74 us
    pallas_call x1, Pallas kernels, match_blocks(): pl.pallas_call(lambda *refs: first_kernel(npatch, *refs), out_shape=[part...  5.82 us
    ppermute x5, starting transfers between devices, local(): evens[c] = lax.ppermute(send_even[c], 'patch', even)  4.95 us
    convert_element_type x4, other arithmetic, local(): send_even[c] = send.astype(bf16)  3.48 us
    ppermute x1, waiting for transfers between devices, finish(): beyond = lax.ppermute(far, 'band', across_x)  2.95 us
    pallas_call x1, Pallas kernels, finish(): pl.pallas_call(tail_left, out_shape=[tile, jax.ShapeDtypeStruct((2 * PAD,...  1.81 us
  transfers between devices with their start and end apart: 20, of which 11 were waited for; matrix products, arithmetic and copies ran while one was open for 11% of the time, Pallas kernels for 17%

profile of v6, /device:TPU:0, one launch (start us, length us, event | category | flops | bytes accessed | tf_op | source)
XLA Modules:
  0.0 69.7 jit_solution(2624672658006593681)
XLA Ops:
  0.6 5.8 %match_first.1 = (bf16[288,512]{1,0:T(8,128)(2,1)}, bf16[288,512]{1,0:T(8,128)(2,1)}, bf16[512,512]{1,0:T(8,128)(2,1)}, bf16[2,512,512]{2,1,0:T(8,128)(2,1)}, bf...) custom-call(s32[1,32]{1,0:T(1,128)} %refs_0_.3, s32[1,32]{1,0:T(1,128)} %refs_1_.3, bf16[1,32]{1,0:T(2,128)(2,1)} %refs_2_.3, ...), custom_call_target="tpu_custom_call" | custom-call | tf_op jit(solution)/shard_map/match_first/pallas_call | solution.py:289
  6.5 3.0 %collective-permute-start.2 = (bf16[288,512]{1,0:T(8,128)(2,1)}, bf16[288,512]{1,0:T(8,128)(2,1)}, u32[]{:S(2)}, u32[]{:S(2)}) collective-permute-start(bf16[288,512]{1,0:T(8,128)(2,1)} %get-tuple-element.58), channel_id=1, source_target_pairs={{0,4},{4,0},{8,12},{12,8},{16,20},{20,16},{24,28},{28,24},{1,5},{5... | collective-permute-start | bytes 884744 | tf_op jit(solution)/shard_map/across_turn_0_of/ppermute | solution.py:553
  9.5 1.6 %collective-permute-start = (bf16[512,512]{1,0:T(8,128)(2,1)}, bf16[512,512]{1,0:T(8,128)(2,1)}, u32[]{:S(2)}, u32[]{:S(2)}) collective-permute-start(bf16[512,512]{1,0:T(8,128)(2,1)} %get-tuple-element.56), channel_id=1, source_target_pairs={{0,8},{4,12},{8,0},{12,4},{16,24},{20,28},{24,16},{28,20},{1,9},{5... | collective-permute-start | bytes 1572872 | tf_op jit(solution)/shard_map/even_step_0_right/ppermute | solution.py:542
  11.7 7.2 %match_rest.1 = (bf16[288,512]{1,0:T(8,128)(2,1)}, bf16[256,512]{1,0:T(8,128)(2,1)}, bf16[256,512]{1,0:T(8,128)(2,1)}, bf16[288,512]{1,0:T(8,128)(2,1)}, bf16[28...) custom-call(s32[1,32]{1,0:T(1,128)} %refs_0_.3, ...), custom_call_target="tpu_custom_call" | custom-call | flops 2000000000 | bytes 8000000 | tf_op jit(solution)/shard_map/match_rest/pallas_call | solution.py:311
  19.0 0.6 collective-permute-start.5
  19.6 1.2 %fusion = bf16[288,512]{1,0:T(8,128)(2,1)S(1)} fusion(bf16[288,512]{1,0:T(8,128)(2,1)} %collective-permute-done.2, bf16[288,512]{1,0:T(8,128)(2,1)} %get-tuple-element.66), kind=kLoop, calls=%fused_computation.10 | loop fusion | flops 589824 | bytes 884736 | tf_op jit(solution)/shard_map/even_step_0_left/convert_element_type | solution.py:621
  20.8 0.6 collective-permute-start.7
  21.4 1.4 %collective-permute-start.3 = (bf16[256,512]{1,0:T(8,128)(2,1)}, bf16[256,512]{1,0:T(8,128)(2,1)S(1)}, u32[]{:S(2)}, u32[]{:S(2)}) collective-permute-start(bf16[256,512]{1,0:T(8,128)(2,1)} %get-tuple-element.59), channel_id=1, source_target_pairs={{0,4},{4,0},{8,12},{12,8},{16,20},{20,16},{24,28},{28,24},{1,5},{5... | collective-permute-start | bytes 786440 | tf_op jit(solution)/shard_map/across_turn_2_of/ppermute | solution.py:553
  22.8 0.9 %collective-permute-done = bf16[512,512]{1,0:T(8,128)(2,1)} collective-permute-done((bf16[512,512]{1,0:T(8,128)(2,1)}, bf16[512,512]{1,0:T(8,128)(2,1)}, u32[]{:S(2)}, u32[]{:S(2)}) %collective-permute-start) | collective-permute-done | bytes 524320 | tf_op jit(solution)/shard_map/even_step_0_right/ppermute | solution.py:542
  23.8 1.2 %select_convert_fusion.3 = bf16[256,512]{1,0:T(8,128)(2,1)S(1)} fusion(bf16[256,512]{1,0:T(8,128)(2,1)} %get-tuple-element.72, bf16[512,512]{1,0:T(8,128)(2,1)} %collective-permute-done, bf16[512,512]{1,0:T(8,128)(2,1)} %get-tuple-element.56, pred[]{:T(512)S(6)} %or.5, pred[]{:T(512)S(6)} %or.4), kind=kLoop, calls=%fused_computation.21 | loop fusion | flops 917504 | bytes 1048578 | tf_op jit(solution)/shard_map/convert_element_type | solution.py:559
  25.0 0.1 collective-permute-start.1
  25.1 4.2 %collective-permute-done.5 = bf16[288,512]{1,0:T(8,128)(2,1)S(1)} collective-permute-done((bf16[288,512]{1,0:T(8,128)(2,1)}, bf16[288,512]{1,0:T(8,128)(2,1)S(1)}, u32[]{:S(2)}, u32[]{:S(2)}) %collective-permute-start.5) | collective-permute-done | bytes 294944 | tf_op jit(solution)/shard_map/across_turn_1_of/ppermute | solution.py:553
  29.2 1.0 %fusion.1 = bf16[288,512]{1,0:T(8,128)(2,1)S(1)} fusion(bf16[288,512]{1,0:T(8,128)(2,1)S(1)} %collective-permute-done.5, bf16[288,512]{1,0:T(8,128)(2,1)} %get-tuple-element.69), kind=kLoop, calls=%fused_computation.11 | loop fusion | flops 589824 | bytes 884736 | tf_op jit(solution)/shard_map/even_step_1_left/convert_element_type | solution.py:621
  30.3 0.5 collective-permute-start.10
  30.8 1.2 %add_convert_fusion.2 = bf16[288,512]{1,0:T(8,128)(2,1)S(1)} fusion(bf16[288,512]{1,0:T(8,128)(2,1)S(1)} %collective-permute-done.7, bf16[288,512]{1,0:T(8,128)(2,1)} %collective-permute-done.2, bf16[288,512]{1,0:T(8,128)(2,1)} %get-tuple-element.66), kind=kLoop, calls=%fused_computation.8 | loop fusion | flops 884736 | bytes 1179648 | tf_op jit(solution)/shard_map/odd_step_1_left/convert_element_type | solution.py:636
  32.0 0.1 collective-permute-start.8
  32.1 2.8 %collective-permute-done.3 = bf16[256,512]{1,0:T(8,128)(2,1)S(1)} collective-permute-done((bf16[256,512]{1,0:T(8,128)(2,1)}, bf16[256,512]{1,0:T(8,128)(2,1)S(1)}, u32[]{:S(2)}, u32[]{:S(2)}) %collective-permute-start.3) | collective-permute-done | bytes 262176 | tf_op jit(solution)/shard_map/across_turn_2_of/ppermute | solution.py:553
  34.9 1.1 %select_convert_fusion.2 = bf16[256,512]{1,0:T(8,128)(2,1)S(1)} fusion(bf16[256,512]{1,0:T(8,128)(2,1)} %get-tuple-element.72, bf16[256,512]{1,0:T(8,128)(2,1)S(1)} %collective-permute-done.3, bf16[256,512]{1,0:T(8,128)(2,1)} %get-tuple-element.70, pred[]{:T(512)S(6)} %or.4), kind=kLoop, calls=%fused_computation.19 | loop fusion | flops 786432 | bytes 1048577 | tf_op jit(solution)/shard_map/even_step_1_right/convert_element_type | solution.py:621
  36.0 0.5 collective-permute-start.12
  36.5 0.6 collective-permute-start.6
  37.1 3.4 %collective-permute-done.1 = bf16[256,512]{1,0:T(8,128)(2,1)S(1)} collective-permute-done((bf16[256,512]{1,0:T(8,128)(2,1)S(1)}, bf16[256,512]{1,0:T(8,128)(2,1)S(1)}, u32[]{:S(2)}, u32[]{:S(2)}) %collective-permute-start.1) | collective-permute-done | bytes 262176 | tf_op jit(solution)/shard_map/across_turn_3_of/ppermute | solution.py:553
  40.5 0.5 collective-permute-start.4
  41.0 1.1 %fusion.2 = bf16[256,512]{1,0:T(8,128)(2,1)S(1)} fusion(bf16[256,512]{1,0:T(8,128)(2,1)S(1)} %collective-permute-done.1, bf16[512,512]{1,0:T(8,128)(2,1)} %collective-permute-done, bf16[512,512]{1,0:T(8,128)(2,1)S(1)} %copy-done.5, pred[]{:T(512)S(6)} %or.5), kind=kLoop, calls=%fused_computation.12 | loop fusion | flops 917504 | bytes 1048577 | tf_op jit(solution)/shard_map/convert_element_type | solution.py:634
  42.1 0.1 collective-permute-start.13
  42.2 0.1 add_convert_fusion
  42.3 0.4 collective-permute-done.12
  42.7 0.2 collective-permute-start.11
  42.9 3.9 %collective-permute-done.6 = bf16[288,512]{1,0:T(8,128)(2,1)S(1)} collective-permute-done((bf16[288,512]{1,0:T(8,128)(2,1)S(1)}, bf16[288,512]{1,0:T(8,128)(2,1)S(1)}, u32[]{:S(2)}, u32[]{:S(2)}) %collective-permute-start.6) | collective-permute-done | bytes 294944 | tf_op jit(solution)/shard_map/across_turn_4_of/ppermute | solution.py:553
  46.8 0.1 add_convert_fusion.1
  46.9 1.3 %collective-permute-start.9 = (bf16[288,512]{1,0:T(8,128)(2,1)S(1)}, bf16[288,512]{1,0:T(8,128)(2,1)S(1)}, u32[]{:S(2)}, u32[]{:S(2)}) collective-permute-start(bf16[288,512]{1,0:T(8,128)(2,1)S(1)} %add_convert_fusion.1), channel_id=1, source_target_pairs={{0,8},{4,12},{8,0},{12,4},{16,24},{20,28},{24,16},{28,20},{1,9},{5... | collective-permute-start | bytes 884744 | tf_op jit(solution)/shard_map/even_step_2_left/ppermute | solution.py:622
  48.2 0.2 fusion.7
  48.4 0.1 collective-permute-start.16
  48.5 1.5 %tables.1 = (bf16[256,288]{1,0:T(8,128)(2,1)S(1)}, bf16[256,288]{1,0:T(8,128)(2,1)S(1)}, bf16[512,512]{1,0:T(8,128)(2,1)S(1)}, bf16[512,512]{1,0:T(8,128)(2,1)S(1)}) custom-call(f32[1,25]{1,0:T(1,128)S(1)} %copy-done.2), custom_call_target="tpu_custom_call" | custom-call | flops 20000000 | bytes 2000000 | tf_op jit(solution)/shard_map/tables/pallas_call | solution.py:430
  50.0 0.1 fusion.4
  50.1 1.2 %collective-permute-done.4.a1 = bf16[288,512]{1,0:T(8,128)(2,1)S(1)} collective-permute-done((bf16[288,512]{1,0:T(8,128)(2,1)S(1)}, bf16[288,512]{1,0:T(8,128)(2,1)S(1)}, u32[]{:S(2)}, u32[]{:S(2)}) %collective-permute-start.4) | collective-permute-done | bytes 294944 | tf_op jit(solution)/shard_map/across_turn_5_of/ppermute | solution.py:553
  51.4 2.0 %collective-permute-start.15 = (bf16[256,512]{1,0:T(8,128)(2,1)S(1)}, bf16[256,512]{1,0:T(8,128)(2,1)S(1)}, u32[]{:S(2)}, u32[]{:S(2)}) collective-permute-start(bf16[256,512]{1,0:T(8,128)(2,1)S(1)} %fusion.4), channel_id=1, source_target_pairs={{0,8},{4,12},{8,0},{12,4},{16,24},{20,28},{24,16},{28,20},{1,9},{5... | collective-permute-start | bytes 786440 | tf_op jit(solution)/shard_map/even_step_2_right/ppermute | solution.py:622
  53.4 0.5 collective-permute-start.14
  54.0 0.1 collective-permute-done.9.a2
  54.1 1.8 %tail_left.1 = (f32[256,512]{1,0:T(8,128)S(1)}, f32[32,512]{1,0:T(8,128)S(1)}, f32[2,8,512]{2,1,0:T(8,128)S(1)}, f32[2,128,256]{2,1,0:T(8,128)S(1)}, f32[2,128,256]{2,1,0:T(8,128)S(1)}) custom-call(bf16[288,512]{1,0:T(8,128)(2,1)S(1)} %copy-done, bf16[288,512]{1,0:T(8,128)(2,1)S(1)} %collective-permute-done.4.a1, ...), custom_call_target="tpu_custom_call" | custom-call | flops 500000000 | bytes 4000000 | tf_op jit(solution)/shard_map/tail_left/pallas_call | solution.py:454
  56.0 3.8 %collective-permute-done.14.b1 = bf16[256,512]{1,0:T(8,128)(2,1)S(1)} collective-permute-done((bf16[256,512]{1,0:T(8,128)(2,1)S(1)}, bf16[256,512]{1,0:T(8,128)(2,1)S(1)}, u32[]{:S(2)}, u32[]{:S(2)}) %collective-permute-start.14) | collective-permute-done | bytes 262176 | tf_op jit(solution)/shard_map/across_turn_6_of/ppermute | solution.py:553
  59.8 1.8 %tail_right.1 = (f32[256,512]{1,0:T(8,128)S(1)}, bf16[128,512]{1,0:T(8,128)(2,1)S(1)}, bf16[128,512]{1,0:T(8,128)(2,1)S(1)}, f32[2,128,512]{2,1,0:T(8,128)S(1)}) custom-call(bf16[256,512]{1,0:T(8,128)(2,1)S(1)} %copy-done.1, bf16[256,512]{1,0:T(8,128)(2,1)S(1)} %collective-permute-done.14.b1, bf16[256,512]{1,0:T(8,128)(2,1)S(1)} %collective-permute-done.15.b2, ...), custom_call_target="tpu_custom_call" | custom-call | tf_op jit(solution)/shard_map/tail_right/pallas_call | solution.py:473
  61.5 0.1 collective-permute-start.17
  61.6 1.3 %collective-permute-done.17 = bf16[128,512]{1,0:T(8,128)(2,1)S(1)} collective-permute-done((bf16[128,512]{1,0:T(8,128)(2,1)S(1)}, bf16[128,512]{1,0:T(8,128)(2,1)S(1)}, u32[]{:S(2)}, u32[]{:S(2)}) %collective-permute-start.17) | collective-permute-done | bytes 131104 | tf_op jit(solution)/shard_map/ppermute | solution.py:482
  63.0 0.2 collective-permute-start.18
  63.2 1.5 %collective-permute-start.19 = (bf16[128,512]{1,0:T(8,128)(2,1)S(1)}, bf16[128,512]{1,0:T(8,128)(2,1)S(1)}, u32[]{:S(2)}, u32[]{:S(2)}) collective-permute-start(bf16[128,512]{1,0:T(8,128)(2,1)S(1)} %fusion.9), channel_id=1, source_target_pairs={{0,2},{1,3},{2,0},{3,1},{4,6},{5,7},{6,4},{7,5},{8,10},{9,11},{10,... | collective-permute-start | bytes 393224 | tf_op jit(solution)/shard_map/ppermute | solution.py:483
  64.7 1.3 %tail_image.1 = f32[512,512]{1,0:T(8,128)} custom-call(f32[256,512]{1,0:T(8,128)S(1)} %get-tuple-element.79.left, f32[256,512]{1,0:T(8,128)S(1)} %get-tuple-element.96.right), custom_call_target="tpu_custom_call" | custom-call | bytes 2000000 | tf_op jit(solution)/shard_map/tail_image/pallas_call | solution.py:486
  66.0 3.0 %collective-permute-done.19 = bf16[128,512]{1,0:T(8,128)(2,1)S(1)} collective-permute-done((bf16[128,512]{1,0:T(8,128)(2,1)S(1)}, bf16[128,512]{1,0:T(8,128)(2,1)S(1)}, u32[]{:S(2)}, u32[]{:S(2)}) %collective-permute-start.19) | collective-permute-done | bytes 131104 | tf_op jit(solution)/shard_map/ppermute | solution.py:483
  69.0 0.7 %fusion.8 = f32[128,512]{1,0:T(8,128)} fusion(bf16[128,512]{1,0:T(8,128)(2,1)S(1)} %collective-permute-done.19, bf16[128,512]{1,0:T(8,128)(2,1)S(1)} %collective-permute-done.18, f32[2,128,512]{2,1,0:T(8,128)S(1)} %get-tuple-element.94), kind=kLoop, calls=%fused_computation.23 | loop fusion | flops 262144 | bytes 786432 | tf_op jit(solution)/shard_map/add | solution.py:495
  (34 shorter events, 0.2 us)
Async XLA Ops:
  6.5 12.6 %collective-permute-start.2 = (bf16[288,512]{1,0:T(8,128)(2,1)}, bf16[288,512]{1,0:T(8,128)(2,1)}, u32[]{:S(2)}, u32[]{:S(2)}) collective-permute-start(bf16[288,512]{1,0:T(8,128)(2,1)} %get-tuple-element.58), channel_id=1, source_target_pairs={{0,4},{4,0},{8,12},{12,8},{16,20},{20,16},{24,28},{28,24},{1,5},{5... | collective-permute-start | bytes 884744 | tf_op jit(solution)/shard_map/across_turn_0_of/ppermute | solution.py:553
  9.5 14.3 %collective-permute-start = (bf16[512,512]{1,0:T(8,128)(2,1)}, bf16[512,512]{1,0:T(8,128)(2,1)}, u32[]{:S(2)}, u32[]{:S(2)}) collective-permute-start(bf16[512,512]{1,0:T(8,128)(2,1)} %get-tuple-element.56), channel_id=1, source_target_pairs={{0,8},{4,12},{8,0},{12,4},{16,24},{20,28},{24,16},{28,20},{1,9},{5... | collective-permute-start | bytes 1572872 | tf_op jit(solution)/shard_map/even_step_0_right/ppermute | solution.py:542
  19.0 17.6 %copy-start.10 = (bf16[288,512]{1,0:T(8,128)(2,1)S(1)}, bf16[288,512]{1,0:T(8,128)(2,1)}, u32[]{:S(2)}) copy-start(bf16[288,512]{1,0:T(8,128)(2,1)} %get-tuple-element.65) | copy-start | bytes 884740
  19.0 21.5 %copy-start.9 = (bf16[288,512]{1,0:T(8,128)(2,1)S(1)}, bf16[288,512]{1,0:T(8,128)(2,1)}, u32[]{:S(2)}) copy-start(bf16[288,512]{1,0:T(8,128)(2,1)} %get-tuple-element.60) | copy-start | bytes 884740
  19.0 22.0 %copy-start.5 = (bf16[512,512]{1,0:T(8,128)(2,1)S(1)}, bf16[512,512]{1,0:T(8,128)(2,1)}, u32[]{:S(2)}) copy-start(bf16[512,512]{1,0:T(8,128)(2,1)} %get-tuple-element.56) | copy-start | bytes 1572868
  19.0 23.2 %copy-start.3 = (bf16[288,512]{1,0:T(8,128)(2,1)S(1)}, bf16[288,512]{1,0:T(8,128)(2,1)}, u32[]{:S(2)}) copy-start(bf16[288,512]{1,0:T(8,128)(2,1)} %get-tuple-element.69) | copy-start | bytes 884740
  19.0 27.8 %copy-start.6 = (bf16[288,512]{1,0:T(8,128)(2,1)S(1)}, bf16[288,512]{1,0:T(8,128)(2,1)}, u32[]{:S(2)}) copy-start(bf16[288,512]{1,0:T(8,128)(2,1)} %get-tuple-element.61) | copy-start | bytes 884740
  19.0 10.2 %collective-permute-start.5 = (bf16[288,512]{1,0:T(8,128)(2,1)}, bf16[288,512]{1,0:T(8,128)(2,1)S(1)}, u32[]{:S(2)}, u32[]{:S(2)}) collective-permute-start(bf16[288,512]{1,0:T(8,128)(2,1)} %get-tuple-element.64), channel_id=1, source_target_pairs={{0,4},{4,0},{8,12},{12,8},{16,20},{20,16},{24,28},{28,24},{1,5},{5... | collective-permute-start | bytes 884744 | tf_op jit(solution)/shard_map/across_turn_1_of/ppermute | solution.py:553
  19.6 28.6 %copy-start.4 = (bf16[256,512]{1,0:T(8,128)(2,1)S(1)}, bf16[256,512]{1,0:T(8,128)(2,1)}, u32[]{:S(2)}) copy-start(bf16[256,512]{1,0:T(8,128)(2,1)} %get-tuple-element.70) | copy-start | bytes 786436
  19.6 28.6 %copy-start.8 = (bf16[256,512]{1,0:T(8,128)(2,1)S(1)}, bf16[256,512]{1,0:T(8,128)(2,1)}, u32[]{:S(2)}) copy-start(bf16[256,512]{1,0:T(8,128)(2,1)} %get-tuple-element.81) | copy-start | bytes 786436
  20.8 10.0 %collective-permute-start.7 = (bf16[288,512]{1,0:T(8,128)(2,1)S(1)}, bf16[288,512]{1,0:T(8,128)(2,1)S(1)}, u32[]{:S(2)}, u32[]{:S(2)}) collective-permute-start(bf16[288,512]{1,0:T(8,128)(2,1)S(1)} %fusion), channel_id=1, source_target_pairs={{0,8},{4,12},{8,0},{12,4},{16,24},{20,28},{24,16},{28,20},{1,9},{5... | collective-permute-start | bytes 884744 | tf_op jit(solution)/shard_map/even_step_0_left/ppermute | solution.py:622
  21.4 13.5 %collective-permute-start.3 = (bf16[256,512]{1,0:T(8,128)(2,1)}, bf16[256,512]{1,0:T(8,128)(2,1)S(1)}, u32[]{:S(2)}, u32[]{:S(2)}) collective-permute-start(bf16[256,512]{1,0:T(8,128)(2,1)} %get-tuple-element.59), channel_id=1, source_target_pairs={{0,4},{4,0},{8,12},{12,8},{16,20},{20,16},{24,28},{28,24},{1,5},{5... | collective-permute-start | bytes 786440 | tf_op jit(solution)/shard_map/across_turn_2_of/ppermute | solution.py:553
  25.0 23.5 %copy-start.2 = (f32[1,25]{1,0:T(1,128)S(1)}, f32[1,25]{1,0:T(1,128)}, u32[]{:S(2)}) copy-start(f32[1,25]{1,0:T(1,128)} %det) | copy-start | bytes 304
  25.0 25.0 %copy-start.7 = (bf16[256,512]{1,0:T(8,128)(2,1)S(1)}, bf16[256,512]{1,0:T(8,128)(2,1)}, u32[]{:S(2)}) copy-start(bf16[256,512]{1,0:T(8,128)(2,1)} %get-tuple-element.82) | copy-start | bytes 786436
  25.0 15.5 %collective-permute-start.1 = (bf16[256,512]{1,0:T(8,128)(2,1)S(1)}, bf16[256,512]{1,0:T(8,128)(2,1)S(1)}, u32[]{:S(2)}, u32[]{:S(2)}) collective-permute-start(bf16[256,512]{1,0:T(8,128)(2,1)S(1)} %select_convert_fusion.3), channel_id=1, source_target_pairs={{0,4},{4,0},{8,12},{12,8},{16,20},{20,16},{24,28},{28,24},{1,5},{5... | collective-permute-start | bytes 786440 | tf_op jit(solution)/shard_map/across_turn_3_of/ppermute | solution.py:553
  30.3 23.8 %copy-start = (bf16[288,512]{1,0:T(8,128)(2,1)S(1)}, bf16[288,512]{1,0:T(8,128)(2,1)}, u32[]{:S(2)}) copy-start(bf16[288,512]{1,0:T(8,128)(2,1)} %get-tuple-element.53.a0) | copy-start | bytes 884740
  30.3 11.8 %collective-permute-start.10 = (bf16[288,512]{1,0:T(8,128)(2,1)S(1)}, bf16[288,512]{1,0:T(8,128)(2,1)S(1)}, u32[]{:S(2)}, u32[]{:S(2)}) collective-permute-start(bf16[288,512]{1,0:T(8,128)(2,1)S(1)} %fusion.1), channel_id=1, source_target_pairs={{0,8},{4,12},{8,0},{12,4},{16,24},{20,28},{24,16},{28,20},{1,9},{5... | collective-permute-start | bytes 884744 | tf_op jit(solution)/shard_map/even_step_1_left/ppermute | solution.py:622
  32.0 10.9 %collective-permute-start.8 = (bf16[288,512]{1,0:T(8,128)(2,1)S(1)}, bf16[288,512]{1,0:T(8,128)(2,1)S(1)}, u32[]{:S(2)}, u32[]{:S(2)}) collective-permute-start(bf16[288,512]{1,0:T(8,128)(2,1)S(1)} %add_convert_fusion.2), channel_id=1, source_target_pairs={{0,1},{1,0},{2,3},{3,2},{4,5},{5,4},{6,7},{7,6},{8,16},{9,17},{10,... | collective-permute-start | bytes 884744 | tf_op jit(solution)/shard_map/odd_step_1_left/ppermute | solution.py:636
  36.0 6.7 %collective-permute-start.12 = (bf16[256,512]{1,0:T(8,128)(2,1)S(1)}, bf16[256,512]{1,0:T(8,128)(2,1)S(1)}, u32[]{:S(2)}, u32[]{:S(2)}) collective-permute-start(bf16[256,512]{1,0:T(8,128)(2,1)S(1)} %select_convert_fusion.2), channel_id=1, source_target_pairs={{0,8},{4,12},{8,0},{12,4},{16,24},{20,28},{24,16},{28,20},{1,9},{5... | collective-permute-start | bytes 786440 | tf_op jit(solution)/shard_map/even_step_1_right/ppermute | solution.py:622
  36.5 10.3 %collective-permute-start.6 = (bf16[288,512]{1,0:T(8,128)(2,1)S(1)}, bf16[288,512]{1,0:T(8,128)(2,1)S(1)}, u32[]{:S(2)}, u32[]{:S(2)}) collective-permute-start(bf16[288,512]{1,0:T(8,128)(2,1)S(1)} %copy-done.10), channel_id=1, source_target_pairs={{0,4},{4,0},{8,12},{12,8},{16,20},{20,16},{24,28},{28,24},{1,5},{5... | collective-permute-start | bytes 884744 | tf_op jit(solution)/shard_map/across_turn_4_of/ppermute | solution.py:553
  40.5 10.9 %collective-permute-start.4 = (bf16[288,512]{1,0:T(8,128)(2,1)S(1)}, bf16[288,512]{1,0:T(8,128)(2,1)S(1)}, u32[]{:S(2)}, u32[]{:S(2)}) collective-permute-start(bf16[288,512]{1,0:T(8,128)(2,1)S(1)} %copy-done.9), channel_id=1, source_target_pairs={{0,4},{4,0},{8,12},{12,8},{16,20},{20,16},{24,28},{28,24},{1,5},{5... | collective-permute-start | bytes 884744 | tf_op jit(solution)/shard_map/across_turn_5_of/ppermute | solution.py:553
  42.1 17.7 %copy-start.1 = (bf16[256,512]{1,0:T(8,128)(2,1)S(1)}, bf16[256,512]{1,0:T(8,128)(2,1)}, u32[]{:S(2)}) copy-start(bf16[256,512]{1,0:T(8,128)(2,1)} %get-tuple-element.80.b0) | copy-start | bytes 786436
  42.1 7.9 %collective-permute-start.13 = (bf16[256,512]{1,0:T(8,128)(2,1)S(1)}, bf16[256,512]{1,0:T(8,128)(2,1)S(1)}, u32[]{:S(2)}, u32[]{:S(2)}) collective-permute-start(bf16[256,512]{1,0:T(8,128)(2,1)S(1)} %fusion.2), channel_id=1, source_target_pairs={{0,1},{1,0},{2,3},{3,2},{4,5},{5,4},{6,7},{7,6},{8,16},{9,17},{10,... | collective-permute-start | bytes 786440 | tf_op jit(solution)/shard_map/odd_step_1_right/ppermute | solution.py:636
  42.7 11.2 %collective-permute-start.11 = (bf16[288,512]{1,0:T(8,128)(2,1)S(1)}, bf16[288,512]{1,0:T(8,128)(2,1)S(1)}, u32[]{:S(2)}, u32[]{:S(2)}) collective-permute-start(bf16[288,512]{1,0:T(8,128)(2,1)S(1)} %add_convert_fusion), channel_id=1, source_target_pairs={{0,1},{1,0},{2,3},{3,2},{4,5},{5,4},{6,7},{7,6},{8,16},{9,17},{10,... | collective-permute-start | bytes 884744 | tf_op jit(solution)/shard_map/odd_step_2_left/ppermute | solution.py:636
  46.9 7.1 %collective-permute-start.9 = (bf16[288,512]{1,0:T(8,128)(2,1)S(1)}, bf16[288,512]{1,0:T(8,128)(2,1)S(1)}, u32[]{:S(2)}, u32[]{:S(2)}) collective-permute-start(bf16[288,512]{1,0:T(8,128)(2,1)S(1)} %add_convert_fusion.1), channel_id=1, source_target_pairs={{0,8},{4,12},{8,0},{12,4},{16,24},{20,28},{24,16},{28,20},{1,9},{5... | collective-permute-start | bytes 884744 | tf_op jit(solution)/shard_map/even_step_2_left/ppermute | solution.py:622
  48.4 7.5 %collective-permute-start.16 = (bf16[256,512]{1,0:T(8,128)(2,1)S(1)}, bf16[256,512]{1,0:T(8,128)(2,1)S(1)}, u32[]{:S(2)}, u32[]{:S(2)}) collective-permute-start(bf16[256,512]{1,0:T(8,128)(2,1)S(1)} %get-tuple-element.86), channel_id=1, source_target_pairs={{0,1},{1,0},{2,3},{3,2},{4,5},{5,4},{6,7},{7,6},{8,16},{9,17},{10,... | collective-permute-start | bytes 786440 | tf_op jit(solution)/shard_map/odd_step_2_right/ppermute | solution.py:636
  51.4 8.4 %collective-permute-start.15 = (bf16[256,512]{1,0:T(8,128)(2,1)S(1)}, bf16[256,512]{1,0:T(8,128)(2,1)S(1)}, u32[]{:S(2)}, u32[]{:S(2)}) collective-permute-start(bf16[256,512]{1,0:T(8,128)(2,1)S(1)} %fusion.4), channel_id=1, source_target_pairs={{0,8},{4,12},{8,0},{12,4},{16,24},{20,28},{24,16},{28,20},{1,9},{5... | collective-permute-start | bytes 786440 | tf_op jit(solution)/shard_map/even_step_2_right/ppermute | solution.py:622
  53.4 6.4 %collective-permute-start.14 = (bf16[256,512]{1,0:T(8,128)(2,1)S(1)}, bf16[256,512]{1,0:T(8,128)(2,1)S(1)}, u32[]{:S(2)}, u32[]{:S(2)}) collective-permute-start(bf16[256,512]{1,0:T(8,128)(2,1)S(1)} %get-tuple-element.85), channel_id=1, source_target_pairs={{0,4},{4,0},{8,12},{12,8},{16,20},{20,16},{24,28},{28,24},{1,5},{5... | collective-permute-start | bytes 786440 | tf_op jit(solution)/shard_map/across_turn_6_of/ppermute | solution.py:553
  61.5 1.4 %collective-permute-start.17 = (bf16[128,512]{1,0:T(8,128)(2,1)S(1)}, bf16[128,512]{1,0:T(8,128)(2,1)S(1)}, u32[]{:S(2)}, u32[]{:S(2)}) collective-permute-start(bf16[128,512]{1,0:T(8,128)(2,1)S(1)} %get-tuple-element.95), channel_id=1, source_target_pairs={{0,1},{1,0},{2,3},{3,2},{4,5},{5,4},{6,7},{7,6},{8,9},{9,8},{10,11... | collective-permute-start | bytes 393224 | tf_op jit(solution)/shard_map/ppermute | solution.py:482
  63.0 3.0 %collective-permute-start.18 = (bf16[128,512]{1,0:T(8,128)(2,1)S(1)}, bf16[128,512]{1,0:T(8,128)(2,1)S(1)}, u32[]{:S(2)}, u32[]{:S(2)}) collective-permute-start(bf16[128,512]{1,0:T(8,128)(2,1)S(1)} %get-tuple-element.97), channel_id=1, source_target_pairs={{0,1},{1,0},{2,3},{3,2},{4,5},{5,4},{6,7},{7,6},{8,9},{9,8},{10,11... | collective-permute-start | bytes 393224 | tf_op jit(solution)/shard_map/ppermute | solution.py:485
  63.2 5.8 %collective-permute-start.19 = (bf16[128,512]{1,0:T(8,128)(2,1)S(1)}, bf16[128,512]{1,0:T(8,128)(2,1)S(1)}, u32[]{:S(2)}, u32[]{:S(2)}) collective-permute-start(bf16[128,512]{1,0:T(8,128)(2,1)S(1)} %fusion.9), channel_id=1, source_target_pairs={{0,2},{1,3},{2,0},{3,1},{4,6},{5,7},{6,4},{7,5},{8,10},{9,11},{10,... | collective-permute-start | bytes 393224 | tf_op jit(solution)/shard_map/ppermute | solution.py:483
